TPU v7x, 32 devices: a whole 2x2x4 slice. The times are simulated.
32 devices in a mesh: seq: 8 (over z, y), batch: 4 (over x, core).
Axes of the slice: x: 2, y: 2, z: 4, core: 2. Of those that a mesh axis runs over, the one named last changes fastest.
Arguments:
- inputs: bfloat16 [32, 1024, 512], P('batch', 'seq'), may hold values from -6 to 6
- cotangent: bfloat16 [32, 1024, 512], P('batch', 'seq'), may hold values from -6 to 6
- lengths: int32 [32], P('batch'), may hold values from 256 to 1024, as said below
- norm1_gain: float32 [512], replicated, may hold values from 0.25 to 1.75
- norm1_bias: float32 [512], replicated, may hold values from -4 to 4
- qkv_weight: bfloat16 [512, 1536], replicated, may hold values from -0.25 to 0.25
- blend_weights: float32 [3, 8], replicated, may hold values from 0.5 to 4
- out_weight: bfloat16 [512, 512], replicated, may hold values from -1 to 1
- norm2_gain: float32 [512], replicated, may hold values from 0.25 to 1.75
- norm2_bias: float32 [512], replicated, may hold values from -4 to 4
- in_weight: bfloat16 [512, 2048], replicated, may hold values from -0.25 to 0.25
- in_bias: float32 [2048], replicated, may hold values from -4 to 4
- down_weight: bfloat16 [2048, 512], replicated, may hold values from -0.125 to 0.125
- down_bias: float32 [512], replicated, may hold values from -4 to 4
Outputs:
- output: bfloat16 [32, 1024, 512], P('batch', 'seq')
- input_grad: bfloat16 [32, 1024, 512], P('batch', 'seq')
- norm1_gain_grad: float32 [512], replicated
- norm1_bias_grad: float32 [512], replicated
- qkv_weight_grad: float32 [512, 1536], replicated
- blend_grad: float32 [3, 8], replicated
- out_weight_grad: float32 [512, 512], replicated
- norm2_gain_grad: float32 [512], replicated
- norm2_bias_grad: float32 [512], replicated
- in_weight_grad: float32 [512, 2048], replicated
- in_bias_grad: float32 [2048], replicated
- down_weight_grad: float32 [2048, 512], replicated
- down_bias_grad: float32 [512], replicated
Inputs may be any that keep to these rules, and one draw needn't show every extreme that they name: `lengths`: in each aligned group of 8 sequences one, drawn from the seed, has length 1024.
All inputs are finite; a program needn't handle non-finite values.
Results may differ from a plain program's by a relative error of at most 0.009.
Values may be sent and summed in bfloat16 or wider, within the bound.
No kernel may reach another device: no remote copies, remote signals or barrier semaphores. Data moves between devices by JAX's collectives and lax.ppermute only.
A program may use at most 320 MiB of HBM per device.

v0:
```python
import functools

import jax
import jax.numpy as jnp
from jax import lax
from jax.experimental import pallas as pl
from jax.experimental.pallas import tpu as pltpu
from jax.sharding import PartitionSpec as P

WINDOW = 30
HEAD = 64
PAIR = 2 * HEAD
TILE = 64
EPS = 1e-05
NEG = -1e30
VMEM = 58 * 2**20
BF16 = jnp.bfloat16
F32 = jnp.float32


def layer_norm(field, gain, shift):
    center = field - jnp.mean(field, axis=-1, keepdims=True)
    spread = jnp.mean(center * center, axis=-1, keepdims=True)
    return center * lax.rsqrt(spread + EPS) * gain + shift


def rows_product(left, right):
    return lax.dot_general(
        left, right, (((0,), (0,)), ((), ())), preferred_element_type=F32
    )


def times_transposed(left, right):
    return lax.dot_general(
        left, right, (((1,), (1,)), ((), ())), preferred_element_type=F32
    )


def times(left, right):
    return lax.dot_general(
        left, right, (((1,), (0,)), ((), ())), preferred_element_type=F32
    )


def elu_feature(field):
    return jnp.where(field > 0, field + 1.0, jnp.exp(jnp.minimum(field, 0.0)))


def tanh_feature(field):
    return 1.0 + jnp.tanh(field)


def pair_lanes(p, part=0, width=PAIR):
    return slice(p * width + part * PAIR, p * width + (part + 1) * PAIR)


def store_split(ref, index, rows, block):
    lane = lax.broadcasted_iota(jnp.int32, (block.shape[0], PAIR), 1)
    for p in range(block.shape[1] // PAIR):
        pair = block[:, pair_lanes(p)]
        for h in range(2):
            mine = (lane < HEAD) if h == 0 else (lane >= HEAD)
            ref[index + (rows, pair_lanes(p, h, 2 * PAIR))] = jnp.where(mine, pair, 0.0).astype(
                BF16
            )


def load_split(ref, index, rows, p):
    return jnp.concatenate([ref[index + (rows, pair_lanes(p, h, 2 * PAIR))] for h in range(2)], 0)


def tall(block):
    return jnp.concatenate([block[:, :PAIR], block[:, PAIR:]], 0)


def fill_features(meta_ref, q_ref, k_ref, v_ref, halo_k, halo_v, keys, values, fq, fk, split):
    rows, width = q_ref.shape
    chunk = 2 * TILE
    front = pl.ds(0, TILE)
    zero = jnp.zeros((TILE, width), F32)
    store_split(keys, (), front, halo_k[...].astype(F32) * 0.125)
    store_split(values, (), front, halo_v[...].astype(F32))
    for c in range(2):
        store_split(fk, (c,), front, zero)

    def fill(step, carry):
        at = pl.multiple_of(step * chunk, chunk)
        here, there = pl.ds(at, chunk), pl.ds(at + TILE, chunk)
        q = q_ref[here, :].astype(F32)
        k = k_ref[here, :].astype(F32)
        store_split(keys, (), there, k * 0.125)
        store_split(values, (), there, v_ref[here, :].astype(F32))
        position = meta_ref[1] + at + lax.broadcasted_iota(jnp.int32, (chunk, width), 0)
        valid = position < meta_ref[0]
        for c, feature in enumerate((elu_feature, tanh_feature)):
            if split:
                store_split(fq, (c,), here, feature(q))
            else:
                fq[c, here, :] = feature(q).astype(BF16)
            store_split(fk, (c,), there, jnp.where(valid, feature(k), 0.0))
        return carry

    lax.fori_loop(0, rows // chunk, fill, 0)


def tile_masks(meta_ref, tile):
    shape = (TILE, 2 * PAIR)
    row = lax.broadcasted_iota(jnp.int32, shape, 0)
    lane = lax.broadcasted_iota(jnp.int32, shape, 1) % PAIR
    back = row + TILE - lane
    key = meta_ref[1] + (tile - 1) * TILE + lane
    known = (key >= 0) & (key < meta_ref[0])
    near = (back >= 0) & (back <= WINDOW) & (known | (back == 0))
    return near, back >= 0


def softmax_pair(scores):
    halves = []
    for h in range(2):
        part = scores[:, h * PAIR : (h + 1) * PAIR]
        part = jnp.exp(part - jnp.max(part, axis=1, keepdims=True))
        halves.append(part * (1.0 / jnp.sum(part, axis=1, keepdims=True)))
    return jnp.concatenate(halves, 1)


def tile_constants():
    row = lax.broadcasted_iota(jnp.int32, (2 * PAIR, PAIR), 0)
    lane = lax.broadcasted_iota(jnp.int32, (2 * PAIR, PAIR), 1)
    ones = jnp.where(row // PAIR == lane // HEAD, 1.0, 0.0).astype(BF16)
    row = lax.broadcasted_iota(jnp.int32, (PAIR, 2 * PAIR), 0)
    lane = lax.broadcasted_iota(jnp.int32, (PAIR, 2 * PAIR), 1)
    return ones, row // HEAD == (lane % PAIR) // HEAD


def whole(split):
    half = split.shape[0] // 2
    return split[:half] + split[half:]


def state_share(block, fks, vs):
    ones = jnp.ones((TILE, PAIR), BF16)
    share = rows_product(whole(fks), jnp.concatenate([whole(vs), ones], 1))
    return jnp.where(block, share, 0.0)


def attend_kernel(
    together, meta_ref, blend_ref, q_ref, k_ref, v_ref, halo_k, halo_v, state_ref,
    att_ref, total_ref, keys, values, fq, fk, state,
):
    rows, width = q_ref.shape
    pairs = range(width // PAIR)
    near_by = range(together)
    units = [(s, p) for s in near_by for p in pairs]
    fill_features(meta_ref, q_ref, k_ref, v_ref, halo_k, halo_v, keys, values, fq, fk, False)
    state[...] = state_ref[...]
    ones, block = tile_constants()

    def step(number, carry):
        first = number * together
        at = pl.multiple_of(first * TILE, TILE)
        here = [pl.ds(at + s * TILE, TILE) for s in near_by]
        window = [pl.ds(at + s * TILE, 2 * TILE) for s in near_by]
        masks = [tile_masks(meta_ref, first + s) for s in near_by]
        q = {(s, p): q_ref[here[s], pair_lanes(p)] for s, p in units}
        feats = {(s, p): [fq[c, here[s], pair_lanes(p)] for c in range(2)] for s, p in units}
        ks = {(s, p): load_split(keys, (), window[s], p) for s, p in units}
        fks = {(s, p): [load_split(fk, (c,), window[s], p) for c in range(2)] for s, p in units}
        wide = {
            (s, p): jnp.concatenate([load_split(values, (), window[s], p), ones], 1)
            for s, p in units
        }
        held = {(0, p): [state[c, p] for c in range(2)] for p in pairs}
        for s, p in units:
            vs = load_split(values, (), here[s], p)
            held[s + 1, p] = [
                held[s, p][c] + state_share(block, load_split(fk, (c,), here[s], p), vs)
                for c in range(2)
            ]
        near = {u: times_transposed(q[u], ks[u]) for u in units}
        far = {u: [times_transposed(feats[u][c], fks[u][c]) for c in range(2)] for u in units}
        old = {u: [times(feats[u][c], held[u][c].astype(BF16)) for c in range(2)] for u in units}
        near = {u: softmax_pair(jnp.where(masks[u[0]][0], near[u], NEG)) for u in units}
        far = {u: [jnp.where(masks[u[0]][1], f, 0.0) for f in far[u]] for u in units}
        stack = {u: jnp.concatenate([near[u]] + far[u], 0).astype(BF16) for u in units}
        sums = {u: times(stack[u], wide[u]) for u in units}
        for s, p in units:
            u, lanes = (s, p), pair_lanes(p)
            mixed = blend_ref[0:1, lanes] * sums[u][:TILE, :PAIR]
            for c in range(2):
                mine = sums[u][(c + 1) * TILE : (c + 2) * TILE] + old[u][c]
                mixed = mixed + blend_ref[c + 1 : c + 2, lanes] * (
                    mine[:, :PAIR] / mine[:, PAIR:]
                )
            att_ref[here[s], lanes] = mixed.astype(BF16)
        for p in pairs:
            for c in range(2):
                state[c, p] = held[together, p][c]
        return carry

    lax.fori_loop(0, rows // (together * TILE), step, 0)
    last = pl.ds(rows, TILE)
    for p in pairs:
        for c in range(2):
            total_ref[c, p] = state[c, p] + state_share(
                block, load_split(fk, (c,), last, p), load_split(values, (), last, p)
            )


def slopes_of(field):
    small = jnp.exp(jnp.minimum(field, 0.0))
    bent = jnp.tanh(field)
    return [jnp.where(field > 0, 1.0, small), 1.0 - bent * bent]


def split_heads(block):
    lane = lax.broadcasted_iota(jnp.int32, block.shape, 1)
    zero = jnp.zeros_like(block)
    return jnp.concatenate(
        [jnp.where(lane < HEAD, block, zero), jnp.where(lane < HEAD, zero, block)], 0
    )


def attend_back_kernel(
    together, meta_ref, blend_ref, q_ref, k_ref, v_ref, halo_k, halo_v, state_ref, later_ref,
    go_ref, gq_ref, gk_ref, gv_ref, hk_ref, hv_ref, mix_ref, total_ref,
    keys, values, fq, fk, state, gk, gv, gfk, gon,
):
    rows, width = q_ref.shape
    pairs = range(width // PAIR)
    tiles = rows // TILE
    near_by = range(together)
    units = [(s, p) for s in near_by for p in pairs]
    fill_features(meta_ref, q_ref, k_ref, v_ref, halo_k, halo_v, keys, values, fq, fk, True)
    state[...] = state_ref[...]
    mix_ref[...] = jnp.zeros_like(mix_ref)
    gk[:TILE, :] = jnp.zeros((TILE, width), F32)
    gv[:TILE, :] = jnp.zeros((TILE, width), F32)
    gfk[:, :TILE, :] = jnp.zeros((2, TILE, width), F32)
    ones, block = tile_constants()
    row = lax.broadcasted_iota(jnp.int32, (2 * PAIR, PAIR), 0) % PAIR
    lane = lax.broadcasted_iota(jnp.int32, (2 * PAIR, PAIR), 1)
    heads = jnp.where(row // HEAD == lane // HEAD, 1.0, 0.0).astype(BF16)
    plain_ones = jnp.ones((TILE, PAIR), BF16)
    high = (lax.broadcasted_iota(jnp.int32, (TILE, PAIR), 1) % HEAD) < HEAD // 2

    def step(number, carry):
        first = number * together
        at = pl.multiple_of(first * TILE, TILE)
        here = [pl.ds(at + s * TILE, TILE) for s in range(together + 1)]
        window = [pl.ds(at + s * TILE, 2 * TILE) for s in near_by]
        masks = [tile_masks(meta_ref, first + s) for s in near_by]
        q = {(s, p): q_ref[here[s], pair_lanes(p)] for s, p in units}
        go = {(s, p): go_ref[here[s], pair_lanes(p)] for s, p in units}
        blend = [[blend_ref[c : c + 1, pair_lanes(p)] for c in range(3)] for p in pairs]
        fqs = {(s, p): [load_split(fq, (c,), here[s], p) for c in range(2)] for s, p in units}
        feats = {u: [whole(f) for f in fqs[u]] for u in units}
        ks = {(s, p): load_split(keys, (), window[s], p) for s, p in units}
        fks = {(s, p): [load_split(fk, (c,), window[s], p) for c in range(2)] for s, p in units}
        wide = {
            (s, p): jnp.concatenate([load_split(values, (), window[s], p), ones], 1)
            for s, p in units
        }
        held = {(0, p): [state[c, p] for c in range(2)] for p in pairs}
        for s, p in units:
            vs = load_split(values, (), here[s], p)
            held[s + 1, p] = [
                held[s, p][c] + state_share(block, load_split(fk, (c,), here[s], p), vs)
                for c in range(2)
            ]
        past = {u: [h.astype(BF16) for h in held[u]] for u in units}
        old_k = [gk[here[0], pair_lanes(p)] for p in pairs]
        old_v = [gv[here[0], pair_lanes(p)] for p in pairs]
        old_f = [[gfk[c, here[0], pair_lanes(p)] for c in range(2)] for p in pairs]

        near = {u: times_transposed(q[u], ks[u]) for u in units}
        far = {u: [times_transposed(feats[u][c], fks[u][c]) for c in range(2)] for u in units}
        old = {u: [times(feats[u][c], past[u][c]) for c in range(2)] for u in units}
        near = {u: softmax_pair(jnp.where(masks[u[0]][0], near[u], NEG)) for u in units}
        far = {u: [jnp.where(masks[u[0]][1], f, 0.0).astype(BF16) for f in far[u]] for u in units}
        stack = {u: jnp.concatenate([near[u].astype(BF16)] + far[u], 0) for u in units}
        sums = {u: times(stack[u], wide[u]) for u in units}
        scales, prods = {}, {}
        for u in units:
            outs = [sums[u][:TILE, :PAIR]]
            scales[u] = [jnp.broadcast_to(blend[u[1]][0], (TILE, PAIR))]
            for c in range(2):
                mine = sums[u][(c + 1) * TILE : (c + 2) * TILE] + old[u][c]
                inverse = 1.0 / mine[:, PAIR:]
                outs.append(mine[:, :PAIR] * inverse)
                scales[u].append(blend[u[1]][c + 1] * inverse)
            prods[u] = jnp.concatenate([go[u] * out for out in outs], 0)
        deltas = {}
        for u in units:
            low = prods[u].astype(BF16)
            rest = (prods[u] - low.astype(F32)).astype(BF16)
            deltas[u] = times(jnp.concatenate([low, rest], 1), heads)
        grads = {}
        for u in units:
            grads[u] = []
            for c in range(3):
                delta = scales[u][c] * deltas[u][c * TILE : (c + 1) * TILE] * (-2.0 / HEAD)
                delta_low = delta.astype(BF16).astype(F32)
                delta = jnp.where(high, delta_low, delta - delta_low)
                grads[u].append(jnp.concatenate([scales[u][c] * go[u], delta], 1).astype(BF16))
        back = {u: times_transposed(jnp.concatenate(grads[u], 0), wide[u]) for u in units}
        late = {u: [times_transposed(grads[u][c + 1], past[u][c]) for c in range(2)] for u in units}
        ds = {u: (near[u] * back[u][:TILE]).astype(BF16) for u in units}
        gas = {
            u: [
                jnp.where(masks[u[0]][1], back[u][(c + 1) * TILE : (c + 2) * TILE], 0.0).astype(BF16)
                for c in range(2)
            ]
            for u in units
        }
        gq_near = {u: times(ds[u], ks[u]) for u in units}
        gq_far = {u: [times(gas[u][c], fks[u][c]) + late[u][c] for c in range(2)] for u in units}
        new_k = {u: rows_product(tall(ds[u]), split_heads(q[u] * 0.125)) for u in units}
        new_f = {u: [rows_product(tall(gas[u][c]), fqs[u][c]) for c in range(2)] for u in units}
        new_v = {
            u: rows_product(
                jnp.concatenate([tall(stack[u][c * TILE : (c + 1) * TILE]) for c in range(3)], 0),
                jnp.concatenate([split_heads(g[:, :PAIR]) for g in grads[u]], 0),
            )
            for u in units
        }

        def overlap(old, new, p):
            parts = [old + new(0, p)[:TILE]]
            parts += [new(s, p)[TILE:] + new(s + 1, p)[:TILE] for s in range(together - 1)]
            return parts + [new(together - 1, p)[TILE:]]

        for s, p in units:
            u, lanes = (s, p), pair_lanes(p)
            slopes = slopes_of(q[u].astype(F32))
            gq = gq_near[u] + slopes[0] * gq_far[u][0] + slopes[1] * gq_far[u][1]
            gq_ref[here[s], lanes] = gq.astype(BF16)
            for c in range(2):
                gon[c, here[s], p * 2 * PAIR : (p + 1) * 2 * PAIR] = grads[u][c + 1]
        for p in pairs:
            lanes = pair_lanes(p)
            for c in range(3):
                mix_ref[c : c + 1, lanes] += sum(
                    jnp.sum(prods[s, p][c * TILE : (c + 1) * TILE], axis=0, keepdims=True)
                    for s in near_by
                )
            for rows_at, part in zip(here, overlap(old_k[p], lambda s, p: new_k[s, p], p)):
                gk[rows_at, lanes] = part
            for rows_at, part in zip(here, overlap(old_v[p], lambda s, p: new_v[s, p], p)):
                gv[rows_at, lanes] = part
            for c in range(2):
                parts = overlap(old_f[p][c], lambda s, p: new_f[s, p][c], p)
                for rows_at, part in zip(here, parts):
                    gfk[c, rows_at, lanes] = part
                state[c, p] = held[together, p][c]
        return carry

    lax.fori_loop(0, tiles // together, step, 0)
    hk_ref[...] = gk[:TILE, :].astype(BF16)
    hv_ref[...] = gv[:TILE, :].astype(BF16)
    state[...] = later_ref[...]

    def come(at, c, p):
        here = pl.ds(at, TILE)
        grads = gon[c, here, p * 2 * PAIR : (p + 1) * 2 * PAIR]
        share = rows_product(whole(load_split(fq, (c,), here, p)), grads)
        return jnp.where(block, share, 0.0)

    def back_step(number, carry):
        first = tiles - 1 - number * together
        at = [pl.multiple_of((first - s) * TILE, TILE) for s in near_by]
        here = [pl.ds(a, TILE) for a in at]
        there = [pl.ds(a + TILE, TILE) for a in at]
        held = {(-1, p): [state[c, p] for c in range(2)] for p in pairs}
        for s, p in units:
            tile = first - s + 2
            nearer = pl.multiple_of(jnp.minimum(tile, tiles - 1) * TILE, TILE)
            held[s, p] = [
                held[s - 1, p][c] + jnp.where(tile < tiles, come(nearer, c, p), 0.0)
                for c in range(2)
            ]
        later = {u: [h.astype(BF16) for h in held[u]] for u in units}
        vs = {(s, p): whole(load_split(values, (), there[s], p)) for s, p in units}
        fks = {
            (s, p): jnp.concatenate([whole(load_split(fk, (c,), there[s], p)) for c in range(2)], 1)
            for s, p in units
        }
        wide = {u: jnp.concatenate([vs[u], plain_ones], 1) for u in units}
        far_k = {u: [times_transposed(wide[u], later[u][c]) for c in range(2)] for u in units}
        far_v = {
            u: times(fks[u], jnp.concatenate([g[:, :PAIR] for g in later[u]], 0)) for u in units
        }
        for s, p in units:
            u, lanes = (s, p), pair_lanes(p)
            position = meta_ref[1] + at[s] + lax.broadcasted_iota(jnp.int32, (TILE, PAIR), 0)
            slopes = slopes_of(k_ref[here[s], lanes].astype(F32))
            grad_f = [gfk[c, there[s], lanes] + far_k[u][c] for c in range(2)]
            bent = slopes[0] * grad_f[0] + slopes[1] * grad_f[1]
            grad_k = gk[there[s], lanes] + jnp.where(position < meta_ref[0], bent, 0.0)
            gk_ref[here[s], lanes] = grad_k.astype(BF16)
            gv_ref[here[s], lanes] = (gv[there[s], lanes] + far_v[u]).astype(BF16)
        for p in pairs:
            for c in range(2):
                state[c, p] = held[together - 1, p][c]
        return carry

    lax.fori_loop(0, tiles // together, back_step, 0)
    for p in pairs:
        for c in range(2):
            total_ref[c, p] = state[c, p] + come(0, c, p) + come(TILE, c, p)


def attention_specs(rows, width, lanes, number):
    calls = width // lanes

    def columns(height, part):
        return pl.BlockSpec((height, lanes), lambda i: (0, part * calls + number(i)))

    state = pl.BlockSpec(
        (2, lanes // PAIR, PAIR, 2 * PAIR), lambda i: (0, number(i), 0, 0)
    )
    ins = [pl.BlockSpec(memory_space=pltpu.SMEM), columns(3, 0)]
    ins += [columns(rows, part) for part in range(3)]
    ins += [columns(TILE, part) for part in range(2)]
    return columns, ins, state


def attention_scratch(rows, lanes, split):
    return [
        pltpu.VMEM((rows + TILE, 2 * lanes), BF16),
        pltpu.VMEM((rows + TILE, 2 * lanes), BF16),
        pltpu.VMEM((2, rows, (2 if split else 1) * lanes), BF16),
        pltpu.VMEM((2, rows + TILE, 2 * lanes), BF16),
        pltpu.VMEM((2, lanes // PAIR, PAIR, 2 * PAIR), F32),
    ]


def outcome(shape, dtype):
    return jax.ShapeDtypeStruct(shape, dtype), pl.BlockSpec(shape, lambda _: (0,) * len(shape))


UNITS = 8


def attend(meta, blend, qkv, halo, state):
    rows, width = qkv.shape[0], qkv.shape[1] // 3
    lanes = PAIR
    columns, ins, held = attention_specs(rows, width, lanes, lambda i: i)
    return pl.pallas_call(
        functools.partial(attend_kernel, UNITS * PAIR // lanes),
        grid=(width // lanes,),
        out_shape=(
            jax.ShapeDtypeStruct((rows, width), BF16),
            jax.ShapeDtypeStruct(state.shape, F32),
        ),
        in_specs=ins + [held],
        out_specs=(columns(rows, 0), held),
        scratch_shapes=attention_scratch(rows, lanes, False),
        compiler_params=pltpu.CompilerParams(vmem_limit_bytes=VMEM),
        cost_estimate=pl.CostEstimate(
            flops=rows * width * 44000, bytes_accessed=rows * width * 8, transcendentals=0
        ),
    )(meta, blend, qkv, qkv, qkv, halo, halo, state)


def attend_back(meta, blend, qkv, halo, state, later, go, calls, number):
    rows, width = qkv.shape[0], qkv.shape[1] // 3
    lanes = width // calls
    columns, ins, held = attention_specs(rows, width, lanes, lambda i: number)
    shapes, blocks = zip(
        *[outcome((rows, lanes), BF16)] * 3,
        *[outcome((TILE, lanes), BF16)] * 2,
        outcome((3, lanes), F32),
        outcome((2, lanes // PAIR, PAIR, 2 * PAIR), F32),
    )
    return pl.pallas_call(
        functools.partial(attend_back_kernel, UNITS * PAIR // lanes),
        grid=(1,),
        out_shape=shapes,
        in_specs=ins + [held, held, columns(rows, 0)],
        out_specs=blocks,
        scratch_shapes=attention_scratch(rows, lanes, True)
        + [
            pltpu.VMEM((rows + TILE, lanes), F32),
            pltpu.VMEM((rows + TILE, lanes), F32),
            pltpu.VMEM((2, rows + TILE, lanes), F32),
            pltpu.VMEM((2, rows, 2 * lanes), BF16),
        ],
        compiler_params=pltpu.CompilerParams(vmem_limit_bytes=VMEM),
        cost_estimate=pl.CostEstimate(
            flops=rows * lanes * 96000, bytes_accessed=rows * lanes * 16, transcendentals=0
        ),
    )(meta, blend, qkv, qkv, qkv, halo, halo, state, later, go)


CHUNK = 512
GELU_A, GELU_B = 0.7978845608028654, 0.044715


def normalized(field):
    center = field - jnp.mean(field, axis=-1, keepdims=True)
    scale = lax.rsqrt(jnp.mean(center * center, axis=-1, keepdims=True) + EPS)
    return center * scale, scale


def norm_back(grad, unit, scale):
    shared = jnp.mean(grad * unit, axis=-1, keepdims=True)
    return scale * (grad - jnp.mean(grad, axis=-1, keepdims=True) - unit * shared)


def gelu_pair(field):
    square = field * field
    bent = jnp.tanh(GELU_A * field * (1.0 + GELU_B * square))
    half = 0.5 + 0.5 * bent
    slope = half + 0.5 * field * (1.0 - bent * bent) * (GELU_A + 3.0 * GELU_A * GELU_B * square)
    return field * half, slope


def column_sum(block):
    return jnp.sum(block, axis=0, keepdims=True)


def deal(core_ref, rows, lanes, value, keep_ref, send_ref):
    half = value.shape[0] // 2

    @pl.when(core_ref[0] == 0)
    def _():
        keep_ref[rows, lanes] = value[:half]
        send_ref[rows, lanes] = value[half:]

    @pl.when(core_ref[0] != 0)
    def _():
        keep_ref[rows, lanes] = value[half:]
        send_ref[rows, lanes] = value[:half]


def feed_kernel(
    pieces, core_ref, x_ref, att_ref, grad_ref, out_w, gain_ref, bias_ref, in_w, in_b, down_w,
    down_b, result_ref, first_ref, go_ref, keep_ref, send_ref, small_ref, wide_ref,
    second, hidden, pre_low, att_low, att_all, grad_all,
):
    chunk, width = x_ref.shape
    inner = in_w.shape[1]
    number = pl.program_id(0)
    here = pl.ds(pl.multiple_of(number * chunk, chunk), chunk)

    @pl.when(number == 0)
    def _():
        small_ref[...] = jnp.zeros_like(small_ref)
        wide_ref[...] = jnp.zeros_like(wide_ref)

    att = att_ref[...]
    att_all[here, :] = att
    first = x_ref[...].astype(F32) + times(att, out_w[...])
    unit, scale = normalized(first)
    low = (unit * gain_ref[...] + bias_ref[...]).astype(BF16)
    second[here, :] = low
    grad = grad_ref[...]
    grad_all[here, :] = grad
    grad_f = grad.astype(F32)
    result = first + down_b[...]
    back = jnp.zeros((chunk, width), F32)
    for at in range(0, inner, width):
        lanes = slice(at, at + width)
        act, slope = gelu_pair(times(low, in_w[:, lanes]) + in_b[:, lanes])
        act = act.astype(BF16)
        hidden[here, lanes] = act
        result = result + times(act, down_w[lanes, :])
        pre = (times_transposed(grad, down_w[lanes, :]) * slope).astype(BF16)
        pre_low[here, lanes] = pre
        wide_ref[:, lanes] += column_sum(pre.astype(F32))
        back = back + times_transposed(pre, in_w[:, lanes])
    result_ref[...] = result.astype(BF16)
    small_ref[0:1, :] += column_sum(back * unit)
    small_ref[1:2, :] += column_sum(back)
    small_ref[2:3, :] += column_sum(grad_f)
    grad_first = grad_f + norm_back(back * gain_ref[...], unit, scale)
    first_ref[...] = grad_first
    grad_att = grad_first.astype(BF16)
    att_low[here, :] = grad_att
    go_ref[...] = times_transposed(grad_att, out_w[...])

    @pl.when(number == pl.num_programs(0) - 1)
    def _():
        every = slice(0, width // 2)
        for at in range(0, inner, width):
            lanes = slice(at, at + width)
            share = rows_product(second[...], pre_low[:, lanes]).astype(BF16)
            deal(core_ref, every, lanes, share, keep_ref, send_ref)
        share = rows_product(att_all[...], att_low[...]).astype(BF16)
        deal(core_ref, every, slice(inner, inner + width), share, keep_ref, send_ref)
        flat = width // pieces
        blocks = inner // width
        for block in range(blocks):
            lanes = slice(inner + (block + 1) * width, inner + (block + 2) * width)
            part = hidden[:, block * width : (block + 1) * width]
            share = rows_product(part, grad_all[...]).astype(BF16)
            each = width // flat
            for below in range(each):
                piece, side = divmod(block * each + below, blocks)
                lanes = slice(inner + (side + 1) * width, inner + (side + 2) * width)
                rows = slice(piece % (pieces // 2) * flat, (piece % (pieces // 2) + 1) * flat)
                mine = core_ref[0] == 2 * piece // pieces
                some = share[below * flat : (below + 1) * flat]

                @pl.when(mine)
                def _(rows=rows, lanes=lanes, some=some):
                    keep_ref[rows, lanes] = some

                @pl.when(jnp.logical_not(mine))
                def _(rows=rows, lanes=lanes, some=some):
                    send_ref[rows, lanes] = some


def by_rows(height, width):
    return pl.BlockSpec((height, width), lambda i: (i, 0))


def constant(shape):
    return pl.BlockSpec(shape, lambda i: (0, 0))


def feed_forward(pieces, core, x, att, grad, out_w, gain, bias, in_w, in_b, down_w, down_b):
    rows, width = x.shape
    inner = in_w.shape[1]
    packed = (width // 2, 2 * inner + width)
    block = by_rows(CHUNK, width)
    return pl.pallas_call(
        functools.partial(feed_kernel, pieces),
        grid=(rows // CHUNK,),
        out_shape=(
            jax.ShapeDtypeStruct((rows, width), BF16),
            jax.ShapeDtypeStruct((rows, width), F32),
            jax.ShapeDtypeStruct((rows, width), F32),
            jax.ShapeDtypeStruct(packed, BF16),
            jax.ShapeDtypeStruct(packed, BF16),
            jax.ShapeDtypeStruct((3, width), F32),
            jax.ShapeDtypeStruct((1, inner), F32),
        ),
        in_specs=[pl.BlockSpec(memory_space=pltpu.SMEM)]
        + [block] * 3
        + [constant(a.shape) for a in (out_w, gain[None], bias[None], in_w, in_b[None], down_w)]
        + [constant((1, width))],
        out_specs=(block, block, block, constant(packed), constant(packed))
        + (constant((3, width)), constant((1, inner))),
        scratch_shapes=[
            pltpu.VMEM((rows, width), BF16),
            pltpu.VMEM((rows, inner), BF16),
            pltpu.VMEM((rows, inner), BF16),
            pltpu.VMEM((rows, width), BF16),
            pltpu.VMEM((rows, width), BF16),
            pltpu.VMEM((rows, width), BF16),
        ],
        compiler_params=pltpu.CompilerParams(vmem_limit_bytes=VMEM),
        cost_estimate=pl.CostEstimate(
            flops=rows * width * inner * 24, bytes_accessed=rows * width * 20, transcendentals=0
        ),
    )(core, x, att, grad, out_w, gain[None], bias[None], in_w, in_b[None], down_w, down_b[None])


def project_back_kernel(
    calls, core_ref, x_ref, first_ref, w_ref, gain_ref, bias_ref, mix_ref, small2_ref, wide_ref,
    *refs,
):
    grads = refs[: 3 * calls]
    result_ref, keep_ref, send_ref, normed, gathered, sums, rows_of = refs[3 * calls :]
    chunk, width = x_ref.shape
    number = pl.program_id(0)
    here = pl.ds(pl.multiple_of(number * chunk, chunk), chunk)

    @pl.when(number == 0)
    def _():
        sums[...] = jnp.zeros_like(sums)

    unit, scale = normalized(x_ref[...].astype(F32))
    normed[here, :] = (unit * gain_ref[...] + bias_ref[...]).astype(BF16)
    grad = jnp.concatenate([ref[...] for ref in grads], 1)
    gathered[here, :] = grad
    back = times_transposed(grad, w_ref[...])
    sums[0:1, :] += column_sum(back * unit)
    sums[1:2, :] += column_sum(back)
    grad_x = first_ref[...] + norm_back(back * gain_ref[...], unit, scale)
    result_ref[...] = grad_x.astype(BF16)

    @pl.when(number == pl.num_programs(0) - 1)
    def _():
        every = slice(0, width // 2)
        for at in range(0, 3 * width, width):
            lanes = slice(at, at + width)
            share = rows_product(normed[...], gathered[:, lanes]).astype(BF16)
            deal(core_ref, every, lanes, share, keep_ref, send_ref)
        rows_of[...] = jnp.zeros_like(rows_of)
        at = 0
        for ref in (sums, small2_ref, mix_ref, wide_ref):
            for row in range(ref.shape[0]):
                for lane in range(0, ref.shape[1], PAIR):
                    rows_of[at : at + 1, :] = ref[row : row + 1, lane : lane + PAIR]
                    at += 1
        exact = rows_of[...]
        high = exact.astype(BF16)
        low = (exact - high.astype(F32)).astype(BF16)
        for part, value in enumerate((high, low)):
            lanes = slice(3 * width + part * PAIR, 3 * width + (part + 1) * PAIR)
            deal(core_ref, every, lanes, value, keep_ref, send_ref)


def project_back(core, x, grad_first, weight, gain, bias, mix, small2, wide, grads):
    rows, width = x.shape
    calls = len(grads) // 3
    packed = (width // 2, 3 * width + 2 * PAIR)
    block, chunk = by_rows(CHUNK, width), by_rows(CHUNK, width // calls)
    return pl.pallas_call(
        functools.partial(project_back_kernel, calls),
        grid=(rows // CHUNK,),
        out_shape=(
            jax.ShapeDtypeStruct((rows, width), BF16),
            jax.ShapeDtypeStruct(packed, BF16),
            jax.ShapeDtypeStruct(packed, BF16),
        ),
        in_specs=[pl.BlockSpec(memory_space=pltpu.SMEM), block, block]
        + [constant(a.shape) for a in (weight, gain[None], bias[None], mix, small2, wide)]
        + [chunk] * (3 * calls),
        out_specs=(block, constant(packed), constant(packed)),
        scratch_shapes=[
            pltpu.VMEM((rows, width), BF16),
            pltpu.VMEM((rows, 3 * width), BF16),
            pltpu.VMEM((2, width), F32),
            pltpu.VMEM((width, PAIR), F32),
        ],
        compiler_params=pltpu.CompilerParams(vmem_limit_bytes=VMEM),
        cost_estimate=pl.CostEstimate(
            flops=rows * width * width * 24, bytes_accessed=rows * width * 20, transcendentals=0
        ),
    )(core, x, grad_first, weight, gain[None], bias[None], mix, small2, wide, *grads)


def to_sequences(block, axis, groups):
    return lax.all_to_all(block, axis, 0, 0, axis_index_groups=groups)


def after(value, *others):
    return lax.optimization_barrier((value,) + others)[0]


def settle_kernel(source_ref, out_ref):
    out_ref[...] = source_ref[...]


def settle(value):
    vmem = pl.BlockSpec(memory_space=pltpu.VMEM)
    return pl.pallas_call(
        settle_kernel,
        out_shape=jax.ShapeDtypeStruct(value.shape, value.dtype),
        in_specs=[vmem],
        out_specs=vmem,
        compiler_params=pltpu.CompilerParams(vmem_limit_bytes=8 * 2**20),
        cost_estimate=pl.CostEstimate(flops=0, bytes_accessed=4 * value.size, transcendentals=0),
    )(value)


def from_parts(total, axis, parts, stride, forward):
    size = lax.axis_size(axis)
    low = total.astype(BF16)
    result = jnp.zeros_like(total)
    for hop in range(1, parts):
        distance = hop * stride
        route = [
            (i, i + distance) if forward else (i + distance, i) for i in range(size - distance)
        ]
        result = result + lax.ppermute(low, axis, route).astype(F32)
    return result


class Ring:
    def __init__(self, batch, seq):
        self.batch, self.seq = batch, seq
        self.low = 2 ** ((seq.bit_length() - 1) // 2)
        self.sizes = {"core": 2, "near": batch // 2 * self.low, "far": seq // self.low}
        self.pieces = batch * seq

    def place(self, s, b):
        return {"core": b % 2, "near": b // 2 * self.low + s % self.low, "far": s // self.low}

    def device(self, place):
        s = place["far"] * self.low + place["near"] % self.low
        return s * self.batch + place["near"] // self.low * 2 + place["core"]

    def mine(self):
        return self.place(lax.axis_index("seq"), lax.axis_index("batch"))

    def swap(self, value, level, k):
        route = []
        for s in range(self.seq):
            for b in range(self.batch):
                place = self.place(s, b)
                place[level] ^= k
                route.append((s * self.batch + b, self.device(place)))
        return lax.ppermute(value, ("seq", "batch"), route)

    def scatter(self, value, level, fine=0, beside=()):
        size, me = self.sizes[level], self.mine()[level]
        value = value.reshape((size, value.shape[0] // size) + value.shape[1:])
        parts = [
            self.swap(lax.dynamic_index_in_dim(value, me ^ k, 0, False), level, k)
            for k in range(1, size)
        ]
        return self.add(lax.dynamic_index_in_dim(value, me, 0, False), parts, fine, beside)

    def scatter_cores(self, keep, send, fine=0, beside=()):
        return self.add(self.to_pieces(keep), [self.swap(self.to_pieces(send), "core", 1)], fine, beside)

    def add(self, value, parts, fine, beside):
        total = after(value, *beside).astype(F32)
        for part in parts:
            total = total + part.astype(F32)
        if not fine:
            return total.astype(BF16)
        end = total.shape[-1] - 2 * fine
        exact = total[..., end : end + fine] + total[..., end + fine :]
        high = lax.reduce_precision(exact, 8, 7)
        return jnp.concatenate([total[..., :end], high, exact - high], -1).astype(BF16)

    def gather(self, value, level, beside=()):
        parts = [self.swap(value, level, k) for k in range(1, self.sizes[level])]
        return jnp.concatenate([after(value, *beside)] + parts, 0)

    def to_pieces(self, value):
        return value.reshape(self.pieces // 2, -1, value.shape[1])

    def order(self):
        me = self.mine()
        piece = jnp.arange(self.pieces, dtype=jnp.int32)
        far, near = self.sizes["far"], self.sizes["near"]
        core = (piece // (far * near)) ^ me["core"]
        near = ((piece // far) % near) ^ me["near"]
        return (core * self.sizes["near"] + near) * far + ((piece % far) ^ me["far"])


def unpack_kernel(write, order_ref, own_ref, other_ref, *out_refs):
    half = own_ref.shape[0]
    for piece in range(2 * half):
        at = order_ref[piece]

        @pl.when(at < half)
        def _(piece=piece, at=at):
            write(piece, own_ref[at].astype(F32), out_refs)

        @pl.when(at >= half)
        def _(piece=piece, at=at):
            write(piece, other_ref[at - half].astype(F32), out_refs)


def write_feed(piece, block, out_refs):
    in_ref, out_ref, down_ref = out_refs
    size, inner, width = block.shape[0], in_ref.shape[1], in_ref.shape[0]
    rows = slice(piece * size, (piece + 1) * size)
    in_ref[rows, :] = block[:, :inner]
    out_ref[rows, :] = block[:, inner : inner + width]
    tall_rows = inner // (width // size)
    for below in range(0, tall_rows, size):
        at = inner + width + below // size * width
        down_ref[piece * tall_rows + below : piece * tall_rows + below + size, :] = block[
            :, at : at + width
        ]


def write_project(piece, block, out_refs):
    w_ref, small_ref = out_refs
    size, end = block.shape[0], w_ref.shape[1]
    rows = slice(piece * size, (piece + 1) * size)
    w_ref[rows, :] = block[:, :end]
    small_ref[rows, :] = block[:, end : end + PAIR] + block[:, end + PAIR :]


def unpack(write, order, halves, shapes):
    vmem = pl.BlockSpec(memory_space=pltpu.VMEM)
    return pl.pallas_call(
        functools.partial(unpack_kernel, write),
        out_shape=[jax.ShapeDtypeStruct(shape, F32) for shape in shapes],
        in_specs=[pl.BlockSpec(memory_space=pltpu.SMEM), vmem, vmem],
        out_specs=[vmem] * len(shapes),
        compiler_params=pltpu.CompilerParams(vmem_limit_bytes=VMEM),
        cost_estimate=pl.CostEstimate(
            flops=0, bytes_accessed=8 * halves[0].size, transcendentals=0
        ),
    )(order, *halves)


def local(
    inputs,
    cotangent,
    lengths,
    norm1_gain,
    norm1_bias,
    qkv_weight,
    blend_weights,
    out_weight,
    norm2_gain,
    norm2_bias,
    in_weight,
    in_bias,
    down_weight,
    down_bias,
):
    seqs, span, width = inputs.shape
    heads = blend_weights.shape[1]
    devices = lax.axis_size("seq")
    parts = devices // seqs
    rows = seqs * span
    index = lax.axis_index("seq")
    groups = None
    if parts > 1:
        groups = [[r * seqs + s for s in range(seqs)] for r in range(parts)]
    mine, part = index % seqs, index // seqs
    meta = jnp.stack([lax.dynamic_index_in_dim(lengths, mine, 0, False), part * rows])
    blend = jnp.repeat(blend_weights, width // heads, axis=1)

    ring = Ring(lax.axis_size("batch"), devices)
    by_ring = width % (16 * ring.pieces) == 0
    inner = in_weight.shape[1]

    x = to_sequences(inputs, "seq", groups).reshape(rows, width)
    grad_out = to_sequences(cotangent, "seq", groups).reshape(rows, width)

    normed = layer_norm(x.astype(F32), norm1_gain, norm1_bias).astype(BF16)
    qkv = times(normed, qkv_weight).astype(BF16)
    halo = jnp.zeros((TILE, 2 * width), BF16)
    state = jnp.zeros((2, width // PAIR, PAIR, 2 * PAIR), F32)
    later = state
    if parts > 1:
        onward = [(i, i + seqs) for i in range(devices - seqs)]
        halo = lax.ppermute(qkv[rows - TILE :, width:], "seq", onward)
        total = attend(meta, blend, qkv, halo, state)[1]
        state = from_parts(total, "seq", parts, seqs, True)
    attended = attend(meta, blend, qkv, halo, state)[0]

    core = (lax.axis_index("batch") % 2)[None] if by_ring else jnp.zeros(1, jnp.int32)
    result, grad_first, grad_o, feed_keep, feed_send, small2, grad_in_b = feed_forward(
        ring.pieces if by_ring else 16,
        core, x, attended, grad_out, out_weight, norm2_gain, norm2_bias,
        in_weight, in_bias, down_weight, down_bias,
    )
    output = to_sequences(result.reshape(seqs, span, width), "seq", groups)
    def unpack_feed(order, halves):
        shapes = [(width, inner), (width, width), (inner, width)]
        return unpack(write_feed, order, halves, shapes)

    calls = 4

    def back(meta, number, later):
        return attend_back(meta, blend, qkv, halo, state, later, grad_o, calls, number)

    if parts > 1:
        total = jnp.concatenate([back(meta, number, later)[6] for number in range(calls)], 1)
        later = from_parts(total, "seq", parts, seqs, False)
    backs, turn = [], meta
    if by_ring:
        held = None
        for number in range(calls):
            if number == 1:
                held = ring.scatter_cores(feed_keep, feed_send)
                turn = after(turn, held)
            if number == 3:
                held = ring.scatter(held, "near")
                turn = after(turn, held)
            backs.append(back(turn, number, later))
            turn = after(turn, backs[-1][5])
        held = ring.scatter(held, "far")
        output = settle(after(output, backs[1][5]))
        grad_first = after(grad_first, held, output)
    else:
        backs = [back(meta, number, later) for number in range(calls)]
    grads = [[call[part] for call in backs] for part in range(3)]
    if parts > 1:
        homeward = [(i + seqs, i) for i in range(devices - seqs)]
        for part in (1, 2):
            for number in range(calls):
                received = lax.ppermute(backs[number][part + 2], "seq", homeward)
                grad = grads[part][number]
                tail = grad[rows - TILE :].astype(F32) + received.astype(F32)
                grads[part][number] = grad.at[rows - TILE :].set(tail.astype(BF16))
    mix = jnp.concatenate([call[5] for call in backs], 1)
    grad_x, project_keep, project_send = project_back(
        core, x, grad_first, qkv_weight, norm1_gain, norm1_bias, mix, small2, grad_in_b,
        grads[0] + grads[1] + grads[2],
    )
    if by_ring:
        order = ring.order()
        late = ring.scatter_cores(project_keep, project_send, PAIR)
        moved = to_sequences(after(grad_x, late).reshape(seqs, span, width), "seq", groups)
        held = ring.gather(held, "far")
        late = after(ring.scatter(late, "near", PAIR), moved)
        held = ring.gather(held, "near", (late,))
        other = ring.swap(held, "core", 1)
        late = ring.scatter(late, "far", PAIR, (held,))
        grad_in_w, grad_out_w, grad_down_w = unpack_feed(order, (held, after(other, late)))
        late = ring.gather(late, "far", (grad_out_w,))
        input_grad = settle(after(moved, late))
        late = ring.gather(late, "near", (input_grad,))
        project_halves = late, ring.swap(late, "core", 1)
    else:
        input_grad = to_sequences(grad_x.reshape(seqs, span, width), "seq", groups)
        order = jnp.arange(16, dtype=jnp.int32)
        halves = (feed_keep, feed_send, project_keep, project_send)
        halves = lax.psum([half.astype(F32) for half in halves], ("seq", "batch"))
        halves = [half.reshape(8, width // 16, -1) for half in halves]
        feed_halves, project_halves = halves[:2], halves[2:]
        grad_in_w, grad_out_w, grad_down_w = unpack_feed(order, feed_halves)
    grad_qkv_w, small = unpack(
        write_project, order, project_halves, [(width, 3 * width), (width, PAIR)]
    )
    vectors = small.reshape(-1)
    vector = [vectors[at : at + width] for at in range(0, 8 * width, width)]
    grad_blend = vectors[5 * width : 8 * width].reshape(3, heads, width // heads).sum(-1)
    return (
        output,
        input_grad,
        vector[0],
        vector[1],
        grad_qkv_w,
        grad_blend,
        grad_out_w,
        vector[2],
        vector[3],
        grad_in_w,
        vectors[8 * width : 8 * width + inner],
        grad_down_w,
        vector[4],
    )


def solution(mesh):
    rows = P("batch", "seq", None)
    return jax.shard_map(
        local,
        mesh=mesh,
        in_specs=(rows, rows, P("batch")) + (P(),) * 11,
        out_specs=(rows, rows) + (P(),) * 11,
        check_vma=False,
    )
```

profile of v0, /device:TPU:0, one launch (start us, length us, event | category | flops | bytes accessed | tf_op | source)
XLA Modules:
  0.0 283.4 jit_solution(2278192614883691162)
XLA Ops:
  0.7 7.4 %all-to-all-start = ((bf16[8,128,512]{2,1,0:T(8,128)(2,1)}), bf16[8,128,512]{2,1,0:T(8,128)(2,1)S(1)}, u32[]{:S(2)}, u32[]{:S(2)}) async-start(bf16[8,128,512]{2,1,0:T(8,128)(2,1)} %param.14), calls=%async_computation | async-start | bytes 2097152 | tf_op jit(solution)/shard_map/all_to_all | solution.py:737
  10.7 23.2 %all-to-all-done = bf16[8,128,512]{2,1,0:T(8,128)(2,1)S(1)} async-done(((bf16[8,128,512]{2,1,0:T(8,128)(2,1)}), bf16[8,128,512]{2,1,0:T(8,128)(2,1)S(1)}, u32[]{:S(2)}, u32[]{:S(2)}) %all-to-all-start) | async-done | bytes 1048608 | tf_op jit(solution)/shard_map/all_to_all | solution.py:737
  33.9 3.6 %all-to-all-start.1 = ((bf16[8,128,512]{2,1,0:T(8,128)(2,1)}), bf16[8,128,512]{2,1,0:T(8,128)(2,1)S(1)}, u32[]{:S(2)}, u32[]{:S(2)}) async-start(bf16[8,128,512]{2,1,0:T(8,128)(2,1)} %param.15), calls=%async_computation.1 | async-start | bytes 2097152 | tf_op jit(solution)/shard_map/all_to_all | solution.py:737
  38.9 3.6 %convolution_convert_fusion.q_ref.k_ref.v_ref = bf16[1024,1536]{1,0:T(8,128)(2,1)} fusion(bf16[512,1536]{1,0:T(8,128)(2,1)S(1)} %copy-done.13, bf16[1024,512]{1,0:T(8,128)(2,1)S(1)} %bitcast.54, f32[512]{0:T(512)S(1)} %copy-done.14, f32[512]{0:T(512)S(1)} %copy-done.15, f32[1024]{0:T(1024)S(1)} %rsqrt_bitcast_fusion, f32[1024]{0:T(1024)S(1)} %get-tuple-element.132), kind=kOutput, calls=%fused_computation.1 | convolution fusion | flops 1615331328 | bytes 5779456 | tf_op jit(solution)/shard_map/dot_general | solution.py:40
  44.2 17.9 %shard_map.237 = (bf16[1024,512]{1,0:T(8,128)(2,1)}, f32[2,4,128,256]{3,2,1,0:T(8,128)}) custom-call(s32[2]{0:T(128)} %pad_add_fusion.meta_ref, f32[3,512]{1,0:T(4,128)} %reshape.168.blend_ref, bf16[1024,1536]{1,0:T(8,128)(2,1)} %convolution_convert_fusion.q_ref.k_ref.v_ref, bf16[1024,1536]{1,0:T(8,128)(2,1)} %convolution_convert_fusion.q_ref.k_ref.v_ref, ...), custom_call_target="tpu_custom_call" | custom-call | flops 23068672000 | bytes 4194304 | tf_op jit(solution)/shard_map/pallas_call | solution.py:448
  64.4 29.3 %shard_map.238 = (bf16[1024,512]{1,0:T(8,128)(2,1)}, f32[1024,512]{1,0:T(8,128)}, f32[1024,512]{1,0:T(8,128)}, bf16[256,4608]{1,0:T(8,128)(2,1)}, bf16[256,4608]...) custom-call(s32[1]{0:T(128)} %bitcast.core_ref, bf16[1024,512]{1,0:T(8,128)(2,1)} %bitcast.55, ...), custom_call_target="tpu_custom_call" | custom-call | flops 25769803776 | bytes 10485760 | tf_op jit(solution)/shard_map/pallas_call | solution.py:627
  93.8 11.9 %shard_map.239 = (bf16[1024,128]{1,0:T(8,128)(2,1)}, bf16[1024,128]{1,0:T(8,128)(2,1)}, bf16[1024,128]{1,0:T(8,128)(2,1)}, bf16[64,128]{1,0:T(8,128)(2,1)}, bf16...) custom-call(s32[2]{0:T(128)} %pad_add_fusion.meta_ref, f32[3,512]{1,0:T(4,128)} %reshape.168.blend_ref, ...), custom_call_target="tpu_custom_call" | custom-call | flops 12582912000 | bytes 2097152 | tf_op jit(solution)/shard_map/pallas_call | solution.py:475
  105.8 4.7 %all-to-all-start.2 = ((bf16[8,128,512]{2,1,0:T(8,128)(2,1)}), bf16[8,128,512]{2,1,0:T(8,128)(2,1)S(1)}, u32[]{:S(2)}, u32[]{:S(2)}) async-start(bf16[8,128,512]{2,1,0:T(8,128)(2,1)} %bitcast.59), calls=%async_computation.2 | async-start | bytes 2097152 | tf_op jit(solution)/shard_map/all_to_all | solution.py:737
  110.5 2.4 add_convert_fusion
  113.9 2.0 collective-permute-start.1
  117.4 11.8 %shard_map.240 = (bf16[1024,128]{1,0:T(8,128)(2,1)}, bf16[1024,128]{1,0:T(8,128)(2,1)}, bf16[1024,128]{1,0:T(8,128)(2,1)}, bf16[64,128]{1,0:T(8,128)(2,1)}, bf16...) custom-call(s32[2]{0:T(128)} %pad_add_fusion.meta_ref, f32[3,512]{1,0:T(4,128)} %reshape.168.blend_ref, ...), custom_call_target="tpu_custom_call" | custom-call | flops 12582912000 | bytes 2097152 | tf_op jit(solution)/shard_map/pallas_call | solution.py:475
  129.2 11.8 %shard_map.242 = (bf16[1024,128]{1,0:T(8,128)(2,1)}, bf16[1024,128]{1,0:T(8,128)(2,1)}, bf16[1024,128]{1,0:T(8,128)(2,1)}, bf16[64,128]{1,0:T(8,128)(2,1)}, bf16...) custom-call(s32[2]{0:T(128)} %pad_add_fusion.meta_ref, f32[3,512]{1,0:T(4,128)} %reshape.168.blend_ref, ...), custom_call_target="tpu_custom_call" | custom-call | flops 12582912000 | bytes 2097152 | tf_op jit(solution)/shard_map/pallas_call | solution.py:475
  142.0 7.9 %collective-permute-done.1 = bf16[4,16,4608]{2,1,0:T(8,128)(2,1)S(1)} collective-permute-done((bf16[4,16,4608]{2,1,0:T(8,128)(2,1)}, bf16[4,16,4608]{2,1,0:T(8,128)(2,1)S(1)}, u32[]{:S(2)}, u32[]{:S(2)}) %collective-permute-start.1) | collective-permute-done | bytes 589856 | tf_op jit(solution)/shard_map/ppermute | solution.py:797
  153.0 2.8 collective-permute-start.5
  156.0 11.9 %shard_map.243 = (bf16[1024,128]{1,0:T(8,128)(2,1)}, bf16[1024,128]{1,0:T(8,128)(2,1)}, bf16[1024,128]{1,0:T(8,128)(2,1)}, bf16[64,128]{1,0:T(8,128)(2,1)}, bf16...) custom-call(s32[2]{0:T(128)} %pad_add_fusion.meta_ref, f32[3,512]{1,0:T(4,128)} %reshape.168.blend_ref, ...), custom_call_target="tpu_custom_call" | custom-call | flops 12582912000 | bytes 2097152 | tf_op jit(solution)/shard_map/pallas_call | solution.py:475
  169.3 9.2 %shard_map.244 = (bf16[1024,512]{1,0:T(8,128)(2,1)}, bf16[256,1792]{1,0:T(8,128)(2,1)}, bf16[256,1792]{1,0:T(8,128)(2,1)}) custom-call(s32[1]{0:T(128)} %bitcast.core_ref, bf16[1024,512]{1,0:T(8,128)(2,1)} %bitcast.56, f32[1024,512]{1,0:T(8,128)} %get-tuple-element.70.first_ref, bf16[512,1536]{1,0:T(8,128)(2,1)} %w_ref.1, f32[1,512]{1,0:T(1,128)} %bitcast.72, ...), custom_call_target="tpu_custom_call" | custom-call | flops 6442450944 | bytes 10485760 | tf_op jit(solution)/shard_map/pallas_call | solution.py:711
  179.3 3.7 %collective-permute-start.12 = (bf16[1,16,4608]{2,1,0:T(8,128)(2,1)S(1)}, bf16[1,16,4608]{2,1,0:T(8,128)(2,1)S(1)}, u32[]{:S(2)}, u32[]{:S(2)}) collective-permute-start(bf16[1,16,4608]{2,1,0:T(8,128)(2,1)S(1)} %add_convert_fusion.4), channel_id=1, source_target_pairs={{0,16},{1,17},{2,18},{3,19},{4,20},{5,21},{6,22},{7,23},{8,24},{9,... | collective-permute-start | bytes 442376 | tf_op jit(solution)/shard_map/ppermute | solution.py:797
  183.1 5.0 %all-to-all-start.3 = ((bf16[8,128,512]{2,1,0:T(8,128)(2,1)}), bf16[8,128,512]{2,1,0:T(8,128)(2,1)S(1)}, u32[]{:S(2)}, u32[]{:S(2)}) async-start(bf16[8,128,512]{2,1,0:T(8,128)(2,1)} %bitcast.60), calls=%async_computation.3 | async-start | bytes 2097152 | tf_op jit(solution)/shard_map/all_to_all | solution.py:737
  188.6 3.0 %collective-permute-start.10 = (bf16[4,16,1792]{2,1,0:T(8,128)(2,1)S(1)}, bf16[4,16,1792]{2,1,0:T(8,128)(2,1)S(1)}, u32[]{:S(2)}, u32[]{:S(2)}) collective-permute-start(bf16[4,16,1792]{2,1,0:T(8,128)(2,1)S(1)} %get-tuple-element.112), channel_id=1, source_target_pairs={{0,6},{1,7},{2,4},{3,5},{4,2},{5,3},{6,0},{7,1},{8,14},{9,15},{10,... | collective-permute-start | bytes 688136 | tf_op jit(solution)/shard_map/ppermute | solution.py:797
  196.7 1.9 collective-permute-done.10
  198.6 3.9 %collective-permute-start.16 = (bf16[4,16,4608]{2,1,0:T(8,128)(2,1)S(1)}, bf16[4,16,4608]{2,1,0:T(8,128)(2,1)S(1)}, u32[]{:S(2)}, u32[]{:S(2)}) collective-permute-start(bf16[4,16,4608]{2,1,0:T(8,128)(2,1)S(1)} %pad_maximum_fusion.1), channel_id=1, source_target_pairs={{0,6},{1,7},{2,4},{3,5},{4,2},{5,3},{6,0},{7,1},{8,14},{9,15},{10,... | collective-permute-start | bytes 1769480 | tf_op jit(solution)/shard_map/ppermute | solution.py:797
  202.6 10.3 %collective-permute-done.8 = bf16[4,16,1792]{2,1,0:T(8,128)(2,1)S(1)} collective-permute-done((bf16[4,16,1792]{2,1,0:T(8,128)(2,1)S(1)}, bf16[4,16,1792]{2,1,0:T(8,128)(2,1)S(1)}, u32[]{:S(2)}, u32[]{:S(2)}) %collective-permute-start.8) | collective-permute-done | bytes 229408 | tf_op jit(solution)/shard_map/ppermute | solution.py:797
  213.8 6.6 %all-to-all-done.3.source_ref = bf16[8,128,512]{2,1,0:T(8,128)(2,1)S(1)} async-done(((bf16[8,128,512]{2,1,0:T(8,128)(2,1)}), bf16[8,128,512]{2,1,0:T(8,128)(2,1)S(1)}, u32[]{:S(2)}, u32[]{:S(2)}) %all-to-all-start.3) | async-done | bytes 1048608 | tf_op jit(solution)/shard_map/all_to_all | solution.py:737
  220.4 16.1 %collective-permute-done.14 = bf16[4,16,4608]{2,1,0:T(8,128)(2,1)S(1)} collective-permute-done((bf16[4,16,4608]{2,1,0:T(8,128)(2,1)S(1)}, bf16[4,16,4608]{2,1,0:T(8,128)(2,1)S(1)}, u32[]{:S(2)}, u32[]{:S(2)}) %collective-permute-start.14) | collective-permute-done | bytes 589856 | tf_op jit(solution)/shard_map/ppermute | solution.py:797
  238.5 2.4 collective-permute-start.18
  241.8 3.4 %collective-permute-done.18 = bf16[1,16,1792]{2,1,0:T(8,128)(2,1)S(1)} collective-permute-done((bf16[1,16,1792]{2,1,0:T(8,128)(2,1)S(1)}, bf16[1,16,1792]{2,1,0:T(8,128)(2,1)S(1)}, u32[]{:S(2)}, u32[]{:S(2)}) %collective-permute-start.18) | collective-permute-done | bytes 57376 | tf_op jit(solution)/shard_map/ppermute | solution.py:797
  249.4 2.0 collective-permute-start.23
  252.9 7.2 %shard_map.245 = (f32[512,2048]{1,0:T(8,128)}, f32[512,512]{1,0:T(8,128)}, f32[2048,512]{1,0:T(8,128)}) custom-call(s32[32]{0:T(128)} %fusion.10.order_ref, bf16[16,16,4608]{2,1,0:T(8,128)(2,1)} %copy-done.1, bf16[16,16,4608]{2,1,0:T(8,128)(2,1)} %copy-done.3), custom_call_target="tpu_custom_call" | custom-call | bytes 9437184 | tf_op jit(solution)/shard_map/pallas_call | solution.py:876
  264.7 3.9 %collective-permute-done.24 = bf16[4,16,1792]{2,1,0:T(8,128)(2,1)S(1)} collective-permute-done((bf16[4,16,1792]{2,1,0:T(8,128)(2,1)S(1)}, bf16[4,16,1792]{2,1,0:T(8,128)(2,1)S(1)}, u32[]{:S(2)}, u32[]{:S(2)}) %collective-permute-start.24) | collective-permute-done | bytes 229408 | tf_op jit(solution)/shard_map/ppermute | solution.py:797
  268.7 3.0 %collective-permute-done.26 = bf16[4,16,1792]{2,1,0:T(8,128)(2,1)S(1)} collective-permute-done((bf16[4,16,1792]{2,1,0:T(8,128)(2,1)S(1)}, bf16[4,16,1792]{2,1,0:T(8,128)(2,1)S(1)}, u32[]{:S(2)}, u32[]{:S(2)}) %collective-permute-start.26) | collective-permute-done | bytes 229408 | tf_op jit(solution)/shard_map/ppermute | solution.py:797
  271.9 2.5 collective-permute-done.27.other_ref
  275.3 3.8 %shard_map.247 = (f32[512,1536]{1,0:T(8,128)}, f32[512,128]{1,0:T(8,128)}) custom-call(s32[32]{0:T(128)} %fusion.10.order_ref, bf16[16,16,1792]{2,1,0:T(8,128)(2,1)} %copy-done.4, bf16[16,16,1792]{2,1,0:T(8,128)(2,1)} %copy-done.8), custom_call_target="tpu_custom_call" | custom-call | bytes 3670016 | tf_op jit(solution)/shard_map/pallas_call | solution.py:876
  (127 shorter events, 41.7 us)
Async XLA Ops:
  0.7 33.2 %all-to-all-start = ((bf16[8,128,512]{2,1,0:T(8,128)(2,1)}), bf16[8,128,512]{2,1,0:T(8,128)(2,1)S(1)}, u32[]{:S(2)}, u32[]{:S(2)}) async-start(bf16[8,128,512]{2,1,0:T(8,128)(2,1)} %param.14), calls=%async_computation | async-start | bytes 2097152 | tf_op jit(solution)/shard_map/all_to_all | solution.py:737
  33.9 29.5 %all-to-all-start.1 = ((bf16[8,128,512]{2,1,0:T(8,128)(2,1)}), bf16[8,128,512]{2,1,0:T(8,128)(2,1)S(1)}, u32[]{:S(2)}, u32[]{:S(2)}) async-start(bf16[8,128,512]{2,1,0:T(8,128)(2,1)} %param.15), calls=%async_computation.1 | async-start | bytes 2097152 | tf_op jit(solution)/shard_map/all_to_all | solution.py:737
  93.7 16.8 %collective-permute-start = (bf16[16,16,4608]{2,1,0:T(8,128)(2,1)}, bf16[16,16,4608]{2,1,0:T(8,128)(2,1)}, u32[]{:S(2)}, u32[]{:S(2)}) collective-permute-start(bf16[16,16,4608]{2,1,0:T(8,128)(2,1)} %bitcast.65), channel_id=1, source_target_pairs={{0,1},{1,0},{2,3},{3,2},{4,5},{5,4},{6,7},{7,6},{8,9},{9,8},{10,11... | collective-permute-start | bytes 7077896 | tf_op jit(solution)/shard_map/ppermute | solution.py:797
  105.8 35.2 %all-to-all-start.2 = ((bf16[8,128,512]{2,1,0:T(8,128)(2,1)}), bf16[8,128,512]{2,1,0:T(8,128)(2,1)S(1)}, u32[]{:S(2)}, u32[]{:S(2)}) async-start(bf16[8,128,512]{2,1,0:T(8,128)(2,1)} %bitcast.59), calls=%async_computation.2 | async-start | bytes 2097152 | tf_op jit(solution)/shard_map/all_to_all | solution.py:737
  113.9 36.0 %collective-permute-start.1 = (bf16[4,16,4608]{2,1,0:T(8,128)(2,1)}, bf16[4,16,4608]{2,1,0:T(8,128)(2,1)S(1)}, u32[]{:S(2)}, u32[]{:S(2)}) collective-permute-start(bf16[4,16,4608]{2,1,0:T(8,128)(2,1)} %get-tuple-element.108), channel_id=1, source_target_pairs={{0,4},{1,5},{2,6},{3,7},{4,0},{5,1},{6,2},{7,3},{8,12},{9,13},{10,... | collective-permute-start | bytes 1769480 | tf_op jit(solution)/shard_map/ppermute | solution.py:797
  115.9 34.0 %collective-permute-start.2 = (bf16[4,16,4608]{2,1,0:T(8,128)(2,1)S(1)}, bf16[4,16,4608]{2,1,0:T(8,128)(2,1)}, u32[]{:S(2)}, u32[]{:S(2)}) collective-permute-start(bf16[4,16,4608]{2,1,0:T(8,128)(2,1)S(1)} %get-tuple-element.107), channel_id=1, source_target_pairs={{0,2},{1,3},{2,0},{3,1},{4,6},{5,7},{6,4},{7,5},{8,10},{9,11},{10,... | collective-permute-start | bytes 1769480 | tf_op jit(solution)/shard_map/ppermute | solution.py:797
  117.4 32.5 %collective-permute-start.3 = (bf16[4,16,4608]{2,1,0:T(8,128)(2,1)S(1)}, bf16[4,16,4608]{2,1,0:T(8,128)(2,1)}, u32[]{:S(2)}, u32[]{:S(2)}) collective-permute-start(bf16[4,16,4608]{2,1,0:T(8,128)(2,1)S(1)} %get-tuple-element.106), channel_id=1, source_target_pairs={{0,6},{1,7},{2,4},{3,5},{4,2},{5,3},{6,0},{7,1},{8,14},{9,15},{10,... | collective-permute-start | bytes 1769480 | tf_op jit(solution)/shard_map/ppermute | solution.py:797
  151.5 17.7 %collective-permute-start.4 = (bf16[1,16,4608]{2,1,0:T(8,128)(2,1)S(1)}, bf16[1,16,4608]{2,1,0:T(8,128)(2,1)S(1)}, u32[]{:S(2)}, u32[]{:S(2)}) collective-permute-start(bf16[1,16,4608]{2,1,0:T(8,128)(2,1)S(1)} %get-tuple-element.118), channel_id=1, source_target_pairs={{0,8},{1,9},{2,10},{3,11},{4,12},{5,13},{6,14},{7,15},{8,0},{9,1},... | collective-permute-start | bytes 442376 | tf_op jit(solution)/shard_map/ppermute | solution.py:797
  153.0 16.2 %collective-permute-start.5 = (bf16[1,16,4608]{2,1,0:T(8,128)(2,1)S(1)}, bf16[1,16,4608]{2,1,0:T(8,128)(2,1)S(1)}, u32[]{:S(2)}, u32[]{:S(2)}) collective-permute-start(bf16[1,16,4608]{2,1,0:T(8,128)(2,1)S(1)} %get-tuple-element.117), channel_id=1, source_target_pairs={{0,16},{1,17},{2,18},{3,19},{4,20},{5,21},{6,22},{7,23},{8,24},{9,... | collective-permute-start | bytes 442376 | tf_op jit(solution)/shard_map/ppermute | solution.py:797
  155.8 13.4 %collective-permute-start.6 = (bf16[1,16,4608]{2,1,0:T(8,128)(2,1)S(1)}, bf16[1,16,4608]{2,1,0:T(8,128)(2,1)S(1)}, u32[]{:S(2)}, u32[]{:S(2)}) collective-permute-start(bf16[1,16,4608]{2,1,0:T(8,128)(2,1)S(1)} %get-tuple-element.116), channel_id=1, source_target_pairs={{0,24},{1,25},{2,26},{3,27},{4,28},{5,29},{6,30},{7,31},{8,16},{9,... | collective-permute-start | bytes 442376 | tf_op jit(solution)/shard_map/ppermute | solution.py:797
  178.6 9.5 %collective-permute-start.7 = (bf16[16,16,1792]{2,1,0:T(8,128)(2,1)}, bf16[16,16,1792]{2,1,0:T(8,128)(2,1)S(1)}, u32[]{:S(2)}, u32[]{:S(2)}) collective-permute-start(bf16[16,16,1792]{2,1,0:T(8,128)(2,1)} %bitcast.66), channel_id=1, source_target_pairs={{0,1},{1,0},{2,3},{3,2},{4,5},{5,4},{6,7},{7,6},{8,9},{9,8},{10,11... | collective-permute-start | bytes 2752520 | tf_op jit(solution)/shard_map/ppermute | solution.py:797
  178.7 13.0 %collective-permute-start.11 = (bf16[1,16,4608]{2,1,0:T(8,128)(2,1)S(1)}, bf16[1,16,4608]{2,1,0:T(8,128)(2,1)S(1)}, u32[]{:S(2)}, u32[]{:S(2)}) collective-permute-start(bf16[1,16,4608]{2,1,0:T(8,128)(2,1)S(1)} %add_convert_fusion.4), channel_id=1, source_target_pairs={{0,8},{1,9},{2,10},{3,11},{4,12},{5,13},{6,14},{7,15},{8,0},{9,1},... | collective-permute-start | bytes 442376 | tf_op jit(solution)/shard_map/ppermute | solution.py:797
  179.3 14.7 %collective-permute-start.12 = (bf16[1,16,4608]{2,1,0:T(8,128)(2,1)S(1)}, bf16[1,16,4608]{2,1,0:T(8,128)(2,1)S(1)}, u32[]{:S(2)}, u32[]{:S(2)}) collective-permute-start(bf16[1,16,4608]{2,1,0:T(8,128)(2,1)S(1)} %add_convert_fusion.4), channel_id=1, source_target_pairs={{0,16},{1,17},{2,18},{3,19},{4,20},{5,21},{6,22},{7,23},{8,24},{9,... | collective-permute-start | bytes 442376 | tf_op jit(solution)/shard_map/ppermute | solution.py:797
  183.0 11.0 %collective-permute-start.13 = (bf16[1,16,4608]{2,1,0:T(8,128)(2,1)S(1)}, bf16[1,16,4608]{2,1,0:T(8,128)(2,1)S(1)}, u32[]{:S(2)}, u32[]{:S(2)}) collective-permute-start(bf16[1,16,4608]{2,1,0:T(8,128)(2,1)S(1)} %add_convert_fusion.4), channel_id=1, source_target_pairs={{0,24},{1,25},{2,26},{3,27},{4,28},{5,29},{6,30},{7,31},{8,16},{9,... | collective-permute-start | bytes 442376 | tf_op jit(solution)/shard_map/ppermute | solution.py:797
  183.1 37.3 %all-to-all-start.3 = ((bf16[8,128,512]{2,1,0:T(8,128)(2,1)}), bf16[8,128,512]{2,1,0:T(8,128)(2,1)S(1)}, u32[]{:S(2)}, u32[]{:S(2)}) async-start(bf16[8,128,512]{2,1,0:T(8,128)(2,1)} %bitcast.60), calls=%async_computation.3 | async-start | bytes 2097152 | tf_op jit(solution)/shard_map/all_to_all | solution.py:737
  188.6 10.0 %collective-permute-start.10 = (bf16[4,16,1792]{2,1,0:T(8,128)(2,1)S(1)}, bf16[4,16,1792]{2,1,0:T(8,128)(2,1)S(1)}, u32[]{:S(2)}, u32[]{:S(2)}) collective-permute-start(bf16[4,16,1792]{2,1,0:T(8,128)(2,1)S(1)} %get-tuple-element.112), channel_id=1, source_target_pairs={{0,6},{1,7},{2,4},{3,5},{4,2},{5,3},{6,0},{7,1},{8,14},{9,15},{10,... | collective-permute-start | bytes 688136 | tf_op jit(solution)/shard_map/ppermute | solution.py:797
  191.6 21.3 %collective-permute-start.8 = (bf16[4,16,1792]{2,1,0:T(8,128)(2,1)S(1)}, bf16[4,16,1792]{2,1,0:T(8,128)(2,1)S(1)}, u32[]{:S(2)}, u32[]{:S(2)}) collective-permute-start(bf16[4,16,1792]{2,1,0:T(8,128)(2,1)S(1)} %get-tuple-element.114), channel_id=1, source_target_pairs={{0,4},{1,5},{2,6},{3,7},{4,0},{5,1},{6,2},{7,3},{8,12},{9,13},{10,... | collective-permute-start | bytes 688136 | tf_op jit(solution)/shard_map/ppermute | solution.py:797
  191.6 21.3 %collective-permute-start.9 = (bf16[4,16,1792]{2,1,0:T(8,128)(2,1)S(1)}, bf16[4,16,1792]{2,1,0:T(8,128)(2,1)S(1)}, u32[]{:S(2)}, u32[]{:S(2)}) collective-permute-start(bf16[4,16,1792]{2,1,0:T(8,128)(2,1)S(1)} %get-tuple-element.113), channel_id=1, source_target_pairs={{0,2},{1,3},{2,0},{3,1},{4,6},{5,7},{6,4},{7,5},{8,10},{9,11},{10,... | collective-permute-start | bytes 688136 | tf_op jit(solution)/shard_map/ppermute | solution.py:797
  194.1 42.4 %collective-permute-start.14 = (bf16[4,16,4608]{2,1,0:T(8,128)(2,1)S(1)}, bf16[4,16,4608]{2,1,0:T(8,128)(2,1)S(1)}, u32[]{:S(2)}, u32[]{:S(2)}) collective-permute-start(bf16[4,16,4608]{2,1,0:T(8,128)(2,1)S(1)} %pad_maximum_fusion.1), channel_id=1, source_target_pairs={{0,4},{1,5},{2,6},{3,7},{4,0},{5,1},{6,2},{7,3},{8,12},{9,13},{10,... | collective-permute-start | bytes 1769480 | tf_op jit(solution)/shard_map/ppermute | solution.py:797
  195.2 41.4 %collective-permute-start.15 = (bf16[4,16,4608]{2,1,0:T(8,128)(2,1)S(1)}, bf16[4,16,4608]{2,1,0:T(8,128)(2,1)S(1)}, u32[]{:S(2)}, u32[]{:S(2)}) collective-permute-start(bf16[4,16,4608]{2,1,0:T(8,128)(2,1)S(1)} %pad_maximum_fusion.1), channel_id=1, source_target_pairs={{0,2},{1,3},{2,0},{3,1},{4,6},{5,7},{6,4},{7,5},{8,10},{9,11},{10,... | collective-permute-start | bytes 1769480 | tf_op jit(solution)/shard_map/ppermute | solution.py:797
  198.6 38.0 %collective-permute-start.16 = (bf16[4,16,4608]{2,1,0:T(8,128)(2,1)S(1)}, bf16[4,16,4608]{2,1,0:T(8,128)(2,1)S(1)}, u32[]{:S(2)}, u32[]{:S(2)}) collective-permute-start(bf16[4,16,4608]{2,1,0:T(8,128)(2,1)S(1)} %pad_maximum_fusion.1), channel_id=1, source_target_pairs={{0,6},{1,7},{2,4},{3,5},{4,2},{5,3},{6,0},{7,1},{8,14},{9,15},{10,... | collective-permute-start | bytes 1769480 | tf_op jit(solution)/shard_map/ppermute | solution.py:797
  236.7 14.8 %collective-permute-start.20 = (bf16[16,16,4608]{2,1,0:T(8,128)(2,1)S(1)}, bf16[16,16,4608]{2,1,0:T(8,128)(2,1)S(1)}, u32[]{:S(2)}, u32[]{:S(2)}) collective-permute-start(bf16[16,16,4608]{2,1,0:T(8,128)(2,1)S(1)} %constant_dynamic-update-slice_fusion.own_ref), channel_id=1, source_target_pairs={{0,1},{1,0},{2,3},{3,2},{4,5},{5,4},{6,7},{7,6},{8,9},{9,8},{10,11... | collective-permute-start | bytes 7077896 | tf_op jit(solution)/shard_map/ppermute | solution.py:797
  236.8 5.0 %collective-permute-start.17 = (bf16[1,16,1792]{2,1,0:T(8,128)(2,1)S(1)}, bf16[1,16,1792]{2,1,0:T(8,128)(2,1)S(1)}, u32[]{:S(2)}, u32[]{:S(2)}) collective-permute-start(bf16[1,16,1792]{2,1,0:T(8,128)(2,1)S(1)} %get-tuple-element.129), channel_id=1, source_target_pairs={{0,8},{1,9},{2,10},{3,11},{4,12},{5,13},{6,14},{7,15},{8,0},{9,1},... | collective-permute-start | bytes 172040 | tf_op jit(solution)/shard_map/ppermute | solution.py:797
  238.5 6.7 %collective-permute-start.18 = (bf16[1,16,1792]{2,1,0:T(8,128)(2,1)S(1)}, bf16[1,16,1792]{2,1,0:T(8,128)(2,1)S(1)}, u32[]{:S(2)}, u32[]{:S(2)}) collective-permute-start(bf16[1,16,1792]{2,1,0:T(8,128)(2,1)S(1)} %get-tuple-element.128), channel_id=1, source_target_pairs={{0,16},{1,17},{2,18},{3,19},{4,20},{5,21},{6,22},{7,23},{8,24},{9,... | collective-permute-start | bytes 172040 | tf_op jit(solution)/shard_map/ppermute | solution.py:797
  240.9 6.0 %collective-permute-start.19 = (bf16[1,16,1792]{2,1,0:T(8,128)(2,1)S(1)}, bf16[1,16,1792]{2,1,0:T(8,128)(2,1)S(1)}, u32[]{:S(2)}, u32[]{:S(2)}) collective-permute-start(bf16[1,16,1792]{2,1,0:T(8,128)(2,1)S(1)} %get-tuple-element.127), channel_id=1, source_target_pairs={{0,24},{1,25},{2,26},{3,27},{4,28},{5,29},{6,30},{7,31},{8,16},{9,... | collective-permute-start | bytes 172040 | tf_op jit(solution)/shard_map/ppermute | solution.py:797
  247.0 13.0 %collective-permute-start.21 = (bf16[1,16,1792]{2,1,0:T(8,128)(2,1)S(1)}, bf16[1,16,1792]{2,1,0:T(8,128)(2,1)S(1)}, u32[]{:S(2)}, u32[]{:S(2)}) collective-permute-start(bf16[1,16,1792]{2,1,0:T(8,128)(2,1)S(1)} %pad_maximum_fusion.3), channel_id=1, source_target_pairs={{0,8},{1,9},{2,10},{3,11},{4,12},{5,13},{6,14},{7,15},{8,0},{9,1},... | collective-permute-start | bytes 172040 | tf_op jit(solution)/shard_map/ppermute | solution.py:797
  247.9 12.2 %collective-permute-start.22 = (bf16[1,16,1792]{2,1,0:T(8,128)(2,1)S(1)}, bf16[1,16,1792]{2,1,0:T(8,128)(2,1)S(1)}, u32[]{:S(2)}, u32[]{:S(2)}) collective-permute-start(bf16[1,16,1792]{2,1,0:T(8,128)(2,1)S(1)} %pad_maximum_fusion.3), channel_id=1, source_target_pairs={{0,16},{1,17},{2,18},{3,19},{4,20},{5,21},{6,22},{7,23},{8,24},{9,... | collective-permute-start | bytes 172040 | tf_op jit(solution)/shard_map/ppermute | solution.py:797
  249.4 10.6 %collective-permute-start.23 = (bf16[1,16,1792]{2,1,0:T(8,128)(2,1)S(1)}, bf16[1,16,1792]{2,1,0:T(8,128)(2,1)S(1)}, u32[]{:S(2)}, u32[]{:S(2)}) collective-permute-start(bf16[1,16,1792]{2,1,0:T(8,128)(2,1)S(1)} %pad_maximum_fusion.3), channel_id=1, source_target_pairs={{0,24},{1,25},{2,26},{3,27},{4,28},{5,29},{6,30},{7,31},{8,16},{9,... | collective-permute-start | bytes 172040 | tf_op jit(solution)/shard_map/ppermute | solution.py:797
  260.1 8.5 %collective-permute-start.24 = (bf16[4,16,1792]{2,1,0:T(8,128)(2,1)S(1)}, bf16[4,16,1792]{2,1,0:T(8,128)(2,1)S(1)}, u32[]{:S(2)}, u32[]{:S(2)}) collective-permute-start(bf16[4,16,1792]{2,1,0:T(8,128)(2,1)S(1)} %constant_dynamic-update-slice_fusion.4), channel_id=1, source_target_pairs={{0,4},{1,5},{2,6},{3,7},{4,0},{5,1},{6,2},{7,3},{8,12},{9,13},{10,... | collective-permute-start | bytes 688136 | tf_op jit(solution)/shard_map/ppermute | solution.py:797
  260.6 8.1 %collective-permute-start.25 = (bf16[4,16,1792]{2,1,0:T(8,128)(2,1)S(1)}, bf16[4,16,1792]{2,1,0:T(8,128)(2,1)S(1)}, u32[]{:S(2)}, u32[]{:S(2)}) collective-permute-start(bf16[4,16,1792]{2,1,0:T(8,128)(2,1)S(1)} %constant_dynamic-update-slice_fusion.4), channel_id=1, source_target_pairs={{0,2},{1,3},{2,0},{3,1},{4,6},{5,7},{6,4},{7,5},{8,10},{9,11},{10,... | collective-permute-start | bytes 688136 | tf_op jit(solution)/shard_map/ppermute | solution.py:797
  262.1 9.7 %collective-permute-start.26 = (bf16[4,16,1792]{2,1,0:T(8,128)(2,1)S(1)}, bf16[4,16,1792]{2,1,0:T(8,128)(2,1)S(1)}, u32[]{:S(2)}, u32[]{:S(2)}) collective-permute-start(bf16[4,16,1792]{2,1,0:T(8,128)(2,1)S(1)} %constant_dynamic-update-slice_fusion.4), channel_id=1, source_target_pairs={{0,6},{1,7},{2,4},{3,5},{4,2},{5,3},{6,0},{7,1},{8,14},{9,15},{10,... | collective-permute-start | bytes 688136 | tf_op jit(solution)/shard_map/ppermute | solution.py:797
  271.8 2.5 collective-permute-start.27
  (17 other events, 176.0 us)
where the time goes:
time: 288 us; the launch traced here: 283 us
  Pallas kernels  117 us (41%)
  waiting for transfers between devices  83.8 us (29%)
  starting transfers between devices  56 us (19%)
  local copies, waits for them, and re-layouts  12 us (4%)
  other arithmetic  9.74 us (3%)
  matrix products  3.61 us (1%)
    ppermute x28, waiting for transfers between devices, swap(): return lax.ppermute(value, ('seq', 'batch'), route)  52.7 us
    pallas_call x4, Pallas kernels, attend_back(): pl.pallas_call(functools.partial(attend_back_kernel, UNITS * PAIR // lane...  47.4 us
    ppermute x28, starting transfers between devices, swap(): return lax.ppermute(value, ('seq', 'batch'), route)  35.4 us
    all_to_all x4, waiting for transfers between devices, to_sequences(): return lax.all_to_all(block, axis, 0, 0, axis_index_groups=groups)  31.1 us
    pallas_call x1, Pallas kernels, feed_forward(): pl.pallas_call(functools.partial(feed_kernel, pieces), grid=(rows // CHUN...  29.3 us
    all_to_all x4, starting transfers between devices, to_sequences(): return lax.all_to_all(block, axis, 0, 0, axis_index_groups=groups)  20.7 us
    pallas_call x1, Pallas kernels, attend(): pl.pallas_call(functools.partial(attend_kernel, UNITS * PAIR // lanes), g...  17.9 us
    pallas_call x2, Pallas kernels, unpack(): pl.pallas_call(functools.partial(unpack_kernel, write), out_shape=[jax.Sh...  11 us
  transfers between devices with their start and end apart: 32, of which 13 were waited for; matrix products, arithmetic and copies ran while one was open for 5% of the time, Pallas kernels for 26%

commit v1 on v0

--- a/solution.py
+++ b/solution.py
@@ -14,6 +14,7 @@
 EPS = 1e-05
 NEG = -1e30
 VMEM = 58 * 2**20
+BRIEF = pl.CostEstimate(flops=1000, bytes_accessed=1000, transcendentals=0)
 BF16 = jnp.bfloat16
 F32 = jnp.float32
 
@@ -77,11 +78,12 @@
     rows, width = q_ref.shape
     chunk = 2 * TILE
     front = pl.ds(0, TILE)
-    zero = jnp.zeros((TILE, width), F32)
-    store_split(keys, (), front, halo_k[...].astype(F32) * 0.125)
-    store_split(values, (), front, halo_v[...].astype(F32))
-    for c in range(2):
-        store_split(fk, (c,), front, zero)
+    keys[front, :] = jnp.zeros((TILE, 2 * width), BF16)
+    values[front, :] = jnp.zeros((TILE, 2 * width), BF16)
+    fk[:, front, :] = jnp.zeros((2, TILE, 2 * width), BF16)
+    if halo_k is not None:
+        store_split(keys, (), front, halo_k[...].astype(F32) * 0.125)
+        store_split(values, (), front, halo_v[...].astype(F32))
 
     def fill(step, carry):
         at = pl.multiple_of(step * chunk, chunk)
@@ -144,15 +146,16 @@
 
 
 def attend_kernel(
-    together, meta_ref, blend_ref, q_ref, k_ref, v_ref, halo_k, halo_v, state_ref,
-    att_ref, total_ref, keys, values, fq, fk, state,
+    together, whole_sequence, meta_ref, blend_ref, q_ref, k_ref, v_ref, *refs
 ):
+    halo_k, halo_v, state_ref = (None,) * 3 if whole_sequence else refs[:3]
+    att_ref, total_ref, keys, values, fq, fk, state = refs[-7:]
     rows, width = q_ref.shape
     pairs = range(width // PAIR)
     near_by = range(together)
     units = [(s, p) for s in near_by for p in pairs]
     fill_features(meta_ref, q_ref, k_ref, v_ref, halo_k, halo_v, keys, values, fq, fk, False)
-    state[...] = state_ref[...]
+    state[...] = jnp.zeros_like(state) if whole_sequence else state_ref[...]
     ones, block = tile_constants()
 
     def step(number, carry):
@@ -221,17 +224,18 @@
 
 
 def attend_back_kernel(
-    together, meta_ref, blend_ref, q_ref, k_ref, v_ref, halo_k, halo_v, state_ref, later_ref,
-    go_ref, gq_ref, gk_ref, gv_ref, hk_ref, hv_ref, mix_ref, total_ref,
-    keys, values, fq, fk, state, gk, gv, gfk, gon,
+    together, whole_sequence, meta_ref, blend_ref, q_ref, k_ref, v_ref, go_ref, *refs
 ):
+    halo_k, halo_v, state_ref, later_ref = (None,) * 4 if whole_sequence else refs[:4]
+    gq_ref, gk_ref, gv_ref, hk_ref, hv_ref, mix_ref, total_ref = refs[-16:-9]
+    keys, values, fq, fk, state, gk, gv, gfk, gon = refs[-9:]
     rows, width = q_ref.shape
     pairs = range(width // PAIR)
     tiles = rows // TILE
     near_by = range(together)
     units = [(s, p) for s in near_by for p in pairs]
     fill_features(meta_ref, q_ref, k_ref, v_ref, halo_k, halo_v, keys, values, fq, fk, True)
-    state[...] = state_ref[...]
+    state[...] = jnp.zeros_like(state) if whole_sequence else state_ref[...]
     mix_ref[...] = jnp.zeros_like(mix_ref)
     gk[:TILE, :] = jnp.zeros((TILE, width), F32)
     gv[:TILE, :] = jnp.zeros((TILE, width), F32)
@@ -357,7 +361,7 @@
     lax.fori_loop(0, tiles // together, step, 0)
     hk_ref[...] = gk[:TILE, :].astype(BF16)
     hv_ref[...] = gv[:TILE, :].astype(BF16)
-    state[...] = later_ref[...]
+    state[...] = jnp.zeros_like(state) if whole_sequence else later_ref[...]
 
     def come(at, c, p):
         here = pl.ds(at, TILE)
@@ -420,8 +424,7 @@
     )
     ins = [pl.BlockSpec(memory_space=pltpu.SMEM), columns(3, 0)]
     ins += [columns(rows, part) for part in range(3)]
-    ins += [columns(TILE, part) for part in range(2)]
-    return columns, ins, state
+    return columns, ins, [columns(TILE, part) for part in range(2)] + [state]
 
 
 def attention_scratch(rows, lanes, split):
@@ -444,28 +447,30 @@
 def attend(meta, blend, qkv, halo, state):
     rows, width = qkv.shape[0], qkv.shape[1] // 3
     lanes = PAIR
-    columns, ins, held = attention_specs(rows, width, lanes, lambda i: i)
+    columns, ins, before = attention_specs(rows, width, lanes, lambda i: i)
+    held = before[-1]
+    share = (2, width // PAIR, PAIR, 2 * PAIR)
+    earlier = () if state is None else (halo, halo, state)
     return pl.pallas_call(
-        functools.partial(attend_kernel, UNITS * PAIR // lanes),
+        functools.partial(attend_kernel, UNITS * PAIR // lanes, state is None),
         grid=(width // lanes,),
         out_shape=(
             jax.ShapeDtypeStruct((rows, width), BF16),
-            jax.ShapeDtypeStruct(state.shape, F32),
+            jax.ShapeDtypeStruct(share, F32),
         ),
-        in_specs=ins + [held],
+        in_specs=ins + before[: len(earlier)],
         out_specs=(columns(rows, 0), held),
         scratch_shapes=attention_scratch(rows, lanes, False),
         compiler_params=pltpu.CompilerParams(vmem_limit_bytes=VMEM),
-        cost_estimate=pl.CostEstimate(
-            flops=rows * width * 44000, bytes_accessed=rows * width * 8, transcendentals=0
-        ),
-    )(meta, blend, qkv, qkv, qkv, halo, halo, state)
+        cost_estimate=BRIEF,
+    )(meta, blend, qkv, qkv, qkv, *earlier)
 
 
 def attend_back(meta, blend, qkv, halo, state, later, go, calls, number):
     rows, width = qkv.shape[0], qkv.shape[1] // 3
     lanes = width // calls
-    columns, ins, held = attention_specs(rows, width, lanes, lambda i: number)
+    columns, ins, before = attention_specs(rows, width, lanes, lambda i: number)
+    others = () if state is None else (halo, halo, state, later)
     shapes, blocks = zip(
         *[outcome((rows, lanes), BF16)] * 3,
         *[outcome((TILE, lanes), BF16)] * 2,
@@ -473,10 +478,10 @@
         outcome((2, lanes // PAIR, PAIR, 2 * PAIR), F32),
     )
     return pl.pallas_call(
-        functools.partial(attend_back_kernel, UNITS * PAIR // lanes),
+        functools.partial(attend_back_kernel, UNITS * PAIR // lanes, state is None),
         grid=(1,),
         out_shape=shapes,
-        in_specs=ins + [held, held, columns(rows, 0)],
+        in_specs=ins + [columns(rows, 0)] + (before + before[-1:])[: len(others)],
         out_specs=blocks,
         scratch_shapes=attention_scratch(rows, lanes, True)
         + [
@@ -486,10 +491,8 @@
             pltpu.VMEM((2, rows, 2 * lanes), BF16),
         ],
         compiler_params=pltpu.CompilerParams(vmem_limit_bytes=VMEM),
-        cost_estimate=pl.CostEstimate(
-            flops=rows * lanes * 96000, bytes_accessed=rows * lanes * 16, transcendentals=0
-        ),
-    )(meta, blend, qkv, qkv, qkv, halo, halo, state, later, go)
+        cost_estimate=BRIEF,
+    )(meta, blend, qkv, qkv, qkv, go, *others)
 
 
 CHUNK = 512
@@ -534,22 +537,38 @@
 
 
 def feed_kernel(
-    pieces, core_ref, x_ref, att_ref, grad_ref, out_w, gain_ref, bias_ref, in_w, in_b, down_w,
-    down_b, result_ref, first_ref, go_ref, keep_ref, send_ref, small_ref, wide_ref,
-    second, hidden, pre_low, att_low, att_all, grad_all,
+    pieces, core_ref, x_ref, att_ref, grad_ref, out_from, gain_ref, bias_ref, in_from, in_b,
+    down_from, down_b, result_ref, first_ref, go_ref, keep_to, send_to, small_ref, wide_ref,
+    second, hidden, pre_low, att_low, att_all, grad_all, out_w, in_w, down_w, keep_ref, send_ref,
+    in_sems, out_sems,
 ):
     chunk, width = x_ref.shape
     inner = in_w.shape[1]
     number = pl.program_id(0)
     here = pl.ds(pl.multiple_of(number * chunk, chunk), chunk)
+    tiles = [slice(at, at + width) for at in range(0, inner, width)]
+    copies = [pltpu.make_async_copy(out_from, out_w, in_sems.at[0])]
+    for i, lanes in enumerate(tiles):
+        copies += [
+            pltpu.make_async_copy(in_from.at[:, lanes], in_w.at[:, lanes], in_sems.at[2 * i + 1]),
+            pltpu.make_async_copy(down_from.at[lanes, :], down_w.at[lanes, :], in_sems.at[2 * i + 2]),
+        ]
+
+    def arrived(i):
+        @pl.when(number == 0)
+        def _():
+            copies[i].wait()
 
     @pl.when(number == 0)
     def _():
+        for copy in copies:
+            copy.start()
         small_ref[...] = jnp.zeros_like(small_ref)
         wide_ref[...] = jnp.zeros_like(wide_ref)
 
     att = att_ref[...]
     att_all[here, :] = att
+    arrived(0)
     first = x_ref[...].astype(F32) + times(att, out_w[...])
     unit, scale = normalized(first)
     low = (unit * gain_ref[...] + bias_ref[...]).astype(BF16)
@@ -559,8 +578,9 @@
     grad_f = grad.astype(F32)
     result = first + down_b[...]
     back = jnp.zeros((chunk, width), F32)
-    for at in range(0, inner, width):
-        lanes = slice(at, at + width)
+    for i, lanes in enumerate(tiles):
+        arrived(2 * i + 1)
+        arrived(2 * i + 2)
         act, slope = gelu_pair(times(low, in_w[:, lanes]) + in_b[:, lanes])
         act = act.astype(BF16)
         hidden[here, lanes] = act
@@ -582,33 +602,43 @@
     @pl.when(number == pl.num_programs(0) - 1)
     def _():
         every = slice(0, width // 2)
-        for at in range(0, inner, width):
-            lanes = slice(at, at + width)
-            share = rows_product(second[...], pre_low[:, lanes]).astype(BF16)
-            deal(core_ref, every, lanes, share, keep_ref, send_ref)
-        share = rows_product(att_all[...], att_low[...]).astype(BF16)
-        deal(core_ref, every, slice(inner, inner + width), share, keep_ref, send_ref)
-        flat = width // pieces
-        blocks = inner // width
-        for block in range(blocks):
-            lanes = slice(inner + (block + 1) * width, inner + (block + 2) * width)
-            part = hidden[:, block * width : (block + 1) * width]
-            share = rows_product(part, grad_all[...]).astype(BF16)
-            each = width // flat
+        leaving = []
+
+        def leave(lanes):
+            for here, there in ((keep_ref, keep_to), (send_ref, send_to)):
+                sem = out_sems.at[len(leaving)]
+                copy = pltpu.make_async_copy(here.at[:, lanes], there.at[:, lanes], sem)
+                copy.start()
+                leaving.append(copy)
+
+        flat, each, after_out = width // pieces, pieces, inner + width
+        for block, lanes in enumerate(tiles):
+            share = rows_product(hidden[:, lanes], grad_all[...]).astype(BF16)
             for below in range(each):
-                piece, side = divmod(block * each + below, blocks)
-                lanes = slice(inner + (side + 1) * width, inner + (side + 2) * width)
+                piece, side = divmod(block * each + below, len(tiles))
+                to = slice(after_out + side * width, after_out + (side + 1) * width)
                 rows = slice(piece % (pieces // 2) * flat, (piece % (pieces // 2) + 1) * flat)
                 mine = core_ref[0] == 2 * piece // pieces
                 some = share[below * flat : (below + 1) * flat]
 
                 @pl.when(mine)
-                def _(rows=rows, lanes=lanes, some=some):
-                    keep_ref[rows, lanes] = some
+                def _(rows=rows, to=to, some=some):
+                    keep_ref[rows, to] = some
 
                 @pl.when(jnp.logical_not(mine))
-                def _(rows=rows, lanes=lanes, some=some):
-                    send_ref[rows, lanes] = some
+                def _(rows=rows, to=to, some=some):
+                    send_ref[rows, to] = some
+
+        leave(slice(after_out, after_out + inner))
+        for lanes in tiles:
+            share = rows_product(second[...], pre_low[:, lanes]).astype(BF16)
+            deal(core_ref, every, lanes, share, keep_ref, send_ref)
+            leave(lanes)
+        share = rows_product(att_all[...], att_low[...]).astype(BF16)
+        deal(core_ref, every, slice(inner, after_out), share, keep_ref, send_ref)
+        leave(slice(inner, after_out))
+        for copy in leaving:
+            copy.wait()
 
 
 def by_rows(height, width):
@@ -623,7 +653,7 @@
     rows, width = x.shape
     inner = in_w.shape[1]
     packed = (width // 2, 2 * inner + width)
-    block = by_rows(CHUNK, width)
+    block, far = by_rows(CHUNK, width), pl.BlockSpec(memory_space=pl.ANY)
     return pl.pallas_call(
         functools.partial(feed_kernel, pieces),
         grid=(rows // CHUNK,),
@@ -638,9 +668,9 @@
         ),
         in_specs=[pl.BlockSpec(memory_space=pltpu.SMEM)]
         + [block] * 3
-        + [constant(a.shape) for a in (out_w, gain[None], bias[None], in_w, in_b[None], down_w)]
+        + [far, constant((1, width)), constant((1, width)), far, constant((1, inner)), far]
         + [constant((1, width))],
-        out_specs=(block, block, block, constant(packed), constant(packed))
+        out_specs=(block, block, block, far, far)
         + (constant((3, width)), constant((1, inner))),
         scratch_shapes=[
             pltpu.VMEM((rows, width), BF16),
@@ -649,20 +679,24 @@
             pltpu.VMEM((rows, width), BF16),
             pltpu.VMEM((rows, width), BF16),
             pltpu.VMEM((rows, width), BF16),
+            pltpu.VMEM(out_w.shape, BF16),
+            pltpu.VMEM(in_w.shape, BF16),
+            pltpu.VMEM(down_w.shape, BF16),
+            pltpu.VMEM(packed, BF16),
+            pltpu.VMEM(packed, BF16),
+            pltpu.SemaphoreType.DMA((1 + 2 * inner // width,)),
+            pltpu.SemaphoreType.DMA((4 + 2 * inner // width,)),
         ],
         compiler_params=pltpu.CompilerParams(vmem_limit_bytes=VMEM),
-        cost_estimate=pl.CostEstimate(
-            flops=rows * width * inner * 24, bytes_accessed=rows * width * 20, transcendentals=0
-        ),
+        cost_estimate=BRIEF,
     )(core, x, att, grad, out_w, gain[None], bias[None], in_w, in_b[None], down_w, down_b[None])
 
 
 def project_back_kernel(
-    calls, core_ref, x_ref, first_ref, w_ref, gain_ref, bias_ref, mix_ref, small2_ref, wide_ref,
-    *refs,
+    calls, core_ref, x_ref, first_ref, w_ref, gain_ref, bias_ref, small2_ref, wide_ref, *refs
 ):
-    grads = refs[: 3 * calls]
-    result_ref, keep_ref, send_ref, normed, gathered, sums, rows_of = refs[3 * calls :]
+    grads, mixes = refs[: 3 * calls], refs[3 * calls : 4 * calls]
+    result_ref, keep_ref, send_ref, normed, gathered, sums, rows_of = refs[4 * calls :]
     chunk, width = x_ref.shape
     number = pl.program_id(0)
     here = pl.ds(pl.multiple_of(number * chunk, chunk), chunk)
@@ -684,41 +718,48 @@
     @pl.when(number == pl.num_programs(0) - 1)
     def _():
         every = slice(0, width // 2)
-        for at in range(0, 3 * width, width):
-            lanes = slice(at, at + width)
-            share = rows_product(normed[...], gathered[:, lanes]).astype(BF16)
-            deal(core_ref, every, lanes, share, keep_ref, send_ref)
         rows_of[...] = jnp.zeros_like(rows_of)
         at = 0
-        for ref in (sums, small2_ref, mix_ref, wide_ref):
+        for ref in (sums, small2_ref, wide_ref):
             for row in range(ref.shape[0]):
                 for lane in range(0, ref.shape[1], PAIR):
                     rows_of[at : at + 1, :] = ref[row : row + 1, lane : lane + PAIR]
                     at += 1
+        lane = lax.broadcasted_iota(jnp.int32, (3, PAIR), 1)
+        blend = jnp.zeros((3, PAIR), F32)
+        head = 0
+        for mix in mixes:
+            for first in range(0, mix.shape[1], HEAD):
+                mine = jnp.sum(mix[:, first : first + HEAD], axis=1, keepdims=True)
+                blend = blend + jnp.where(lane == head, mine, 0.0)
+                head += 1
+        rows_of[at : at + 3, :] = blend
         exact = rows_of[...]
         high = exact.astype(BF16)
         low = (exact - high.astype(F32)).astype(BF16)
         for part, value in enumerate((high, low)):
             lanes = slice(3 * width + part * PAIR, 3 * width + (part + 1) * PAIR)
             deal(core_ref, every, lanes, value, keep_ref, send_ref)
-
-
-def project_back(core, x, grad_first, weight, gain, bias, mix, small2, wide, grads):
+        for at in range(0, 3 * width, width):
+            lanes = slice(at, at + width)
+            share = rows_product(normed[...], gathered[:, lanes]).astype(BF16)
+            deal(core_ref, every, lanes, share, keep_ref, send_ref)
+
+
+def project_back(core, x, grad_first, weight, gain, bias, small2, wide, grads, mixes):
     rows, width = x.shape
-    calls = len(grads) // 3
+    calls = len(mixes)
     packed = (width // 2, 3 * width + 2 * PAIR)
     block, chunk = by_rows(CHUNK, width), by_rows(CHUNK, width // calls)
     return pl.pallas_call(
         functools.partial(project_back_kernel, calls),
         grid=(rows // CHUNK,),
-        out_shape=(
-            jax.ShapeDtypeStruct((rows, width), BF16),
-            jax.ShapeDtypeStruct(packed, BF16),
-            jax.ShapeDtypeStruct(packed, BF16),
-        ),
+        out_shape=(jax.ShapeDtypeStruct((rows, width), BF16),)
+        + (jax.ShapeDtypeStruct(packed, BF16),) * 2,
         in_specs=[pl.BlockSpec(memory_space=pltpu.SMEM), block, block]
-        + [constant(a.shape) for a in (weight, gain[None], bias[None], mix, small2, wide)]
-        + [chunk] * (3 * calls),
+        + [constant(a.shape) for a in (weight, gain[None], bias[None], small2, wide)]
+        + [chunk] * (3 * calls)
+        + [constant(mix.shape) for mix in mixes],
         out_specs=(block, constant(packed), constant(packed)),
         scratch_shapes=[
             pltpu.VMEM((rows, width), BF16),
@@ -727,10 +768,8 @@
             pltpu.VMEM((width, PAIR), F32),
         ],
         compiler_params=pltpu.CompilerParams(vmem_limit_bytes=VMEM),
-        cost_estimate=pl.CostEstimate(
-            flops=rows * width * width * 24, bytes_accessed=rows * width * 20, transcendentals=0
-        ),
-    )(core, x, grad_first, weight, gain[None], bias[None], mix, small2, wide, *grads)
+        cost_estimate=BRIEF,
+    )(core, x, grad_first, weight, gain[None], bias[None], small2, wide, *grads, *mixes)
 
 
 def to_sequences(block, axis, groups):
@@ -753,7 +792,7 @@
         in_specs=[vmem],
         out_specs=vmem,
         compiler_params=pltpu.CompilerParams(vmem_limit_bytes=8 * 2**20),
-        cost_estimate=pl.CostEstimate(flops=0, bytes_accessed=4 * value.size, transcendentals=0),
+        cost_estimate=BRIEF,
     )(value)
 
 
@@ -835,7 +874,7 @@
         return (core * self.sizes["near"] + near) * far + ((piece % far) ^ me["far"])
 
 
-def unpack_kernel(write, order_ref, own_ref, other_ref, *out_refs):
+def unpack_kernel(write, finish, order_ref, own_ref, other_ref, *out_refs):
     half = own_ref.shape[0]
     for piece in range(2 * half):
         at = order_ref[piece]
@@ -847,6 +886,8 @@
         @pl.when(at >= half)
         def _(piece=piece, at=at):
             write(piece, other_ref[at - half].astype(F32), out_refs)
+
+    finish(out_refs)
 
 
 def write_feed(piece, block, out_refs):
@@ -864,24 +905,34 @@
 
 
 def write_project(piece, block, out_refs):
-    w_ref, small_ref = out_refs
+    w_ref, small = out_refs[0], out_refs[-1]
     size, end = block.shape[0], w_ref.shape[1]
     rows = slice(piece * size, (piece + 1) * size)
     w_ref[rows, :] = block[:, :end]
-    small_ref[rows, :] = block[:, end : end + PAIR] + block[:, end + PAIR :]
-
-
-def unpack(write, order, halves, shapes):
+    if piece * size < small.shape[0]:
+        small[rows, :] = block[:, end : end + PAIR] + block[:, end + PAIR :]
+
+
+def finish_project(out_refs):
+    small, at = out_refs[-1], 0
+    for vector in out_refs[1:-2]:
+        for lane in range(0, vector.shape[0], PAIR):
+            vector[lane : lane + PAIR] = small[at, :]
+            at += 1
+    blend = out_refs[-2]
+    blend[...] = small[at : at + 3, : blend.shape[1]]
+
+
+def unpack(write, order, halves, shapes, finish=lambda refs: None, scratch=()):
     vmem = pl.BlockSpec(memory_space=pltpu.VMEM)
     return pl.pallas_call(
-        functools.partial(unpack_kernel, write),
+        functools.partial(unpack_kernel, write, finish),
         out_shape=[jax.ShapeDtypeStruct(shape, F32) for shape in shapes],
         in_specs=[pl.BlockSpec(memory_space=pltpu.SMEM), vmem, vmem],
         out_specs=[vmem] * len(shapes),
+        scratch_shapes=scratch,
         compiler_params=pltpu.CompilerParams(vmem_limit_bytes=VMEM),
-        cost_estimate=pl.CostEstimate(
-            flops=0, bytes_accessed=8 * halves[0].size, transcendentals=0
-        ),
+        cost_estimate=BRIEF,
     )(order, *halves)
 
 
@@ -923,10 +974,9 @@
 
     normed = layer_norm(x.astype(F32), norm1_gain, norm1_bias).astype(BF16)
     qkv = times(normed, qkv_weight).astype(BF16)
-    halo = jnp.zeros((TILE, 2 * width), BF16)
-    state = jnp.zeros((2, width // PAIR, PAIR, 2 * PAIR), F32)
-    later = state
+    halo = state = later = None
     if parts > 1:
+        state = later = jnp.zeros((2, width // PAIR, PAIR, 2 * PAIR), F32)
         onward = [(i, i + seqs) for i in range(devices - seqs)]
         halo = lax.ppermute(qkv[rows - TILE :, width:], "seq", onward)
         total = attend(meta, blend, qkv, halo, state)[1]
@@ -957,15 +1007,15 @@
         held = None
         for number in range(calls):
             if number == 1:
-                held = ring.scatter_cores(feed_keep, feed_send)
+                held = ring.scatter_cores(feed_keep, feed_send, 0, (backs[0][5],))
                 turn = after(turn, held)
             if number == 3:
-                held = ring.scatter(held, "near")
+                held = ring.scatter(held, "near", 0, (backs[2][5],))
                 turn = after(turn, held)
             backs.append(back(turn, number, later))
             turn = after(turn, backs[-1][5])
-        held = ring.scatter(held, "far")
-        output = settle(after(output, backs[1][5]))
+        held = ring.scatter(held, "far", 0, (backs[3][5],))
+        output = settle(after(output, backs[2][5]))
         grad_first = after(grad_first, held, output)
     else:
         backs = [back(meta, number, later) for number in range(calls)]
@@ -978,53 +1028,56 @@
                 grad = grads[part][number]
                 tail = grad[rows - TILE :].astype(F32) + received.astype(F32)
                 grads[part][number] = grad.at[rows - TILE :].set(tail.astype(BF16))
-    mix = jnp.concatenate([call[5] for call in backs], 1)
+    grads = grads[0] + grads[1] + grads[2]
     grad_x, project_keep, project_send = project_back(
-        core, x, grad_first, qkv_weight, norm1_gain, norm1_bias, mix, small2, grad_in_b,
-        grads[0] + grads[1] + grads[2],
+        core, x, grad_first, qkv_weight, norm1_gain, norm1_bias, small2, grad_in_b, grads,
+        [call[5] for call in backs],
     )
+    moved = to_sequences(grad_x.reshape(seqs, span, width), "seq", groups)
+
     if by_ring:
         order = ring.order()
-        late = ring.scatter_cores(project_keep, project_send, PAIR)
-        moved = to_sequences(after(grad_x, late).reshape(seqs, span, width), "seq", groups)
-        held = ring.gather(held, "far")
+        held = ring.gather(held, "far", (project_keep,))
+        late = ring.scatter_cores(project_keep, project_send, PAIR, (held,))
+        near = [ring.swap(held, "near", k) for k in range(1, ring.sizes["near"])]
         late = after(ring.scatter(late, "near", PAIR), moved)
-        held = ring.gather(held, "near", (late,))
+        late = ring.scatter(late, "far", PAIR)
+        held = jnp.concatenate([after(held, late)] + near, 0)
         other = ring.swap(held, "core", 1)
-        late = ring.scatter(late, "far", PAIR, (held,))
+        late = ring.gather(late, "far", (held,))
         grad_in_w, grad_out_w, grad_down_w = unpack_feed(order, (held, after(other, late)))
-        late = ring.gather(late, "far", (grad_out_w,))
         input_grad = settle(after(moved, late))
-        late = ring.gather(late, "near", (input_grad,))
+        late = ring.gather(late, "near", (input_grad, grad_out_w))
         project_halves = late, ring.swap(late, "core", 1)
     else:
-        input_grad = to_sequences(grad_x.reshape(seqs, span, width), "seq", groups)
+        input_grad = moved
         order = jnp.arange(16, dtype=jnp.int32)
         halves = (feed_keep, feed_send, project_keep, project_send)
         halves = lax.psum([half.astype(F32) for half in halves], ("seq", "batch"))
         halves = [half.reshape(8, width // 16, -1) for half in halves]
         feed_halves, project_halves = halves[:2], halves[2:]
         grad_in_w, grad_out_w, grad_down_w = unpack_feed(order, feed_halves)
-    grad_qkv_w, small = unpack(
-        write_project, order, project_halves, [(width, 3 * width), (width, PAIR)]
+    vectors = [(width,)] * 5 + [(inner,)]
+    lines = sum(size for (size,) in vectors) // PAIR + 3
+    lines += -lines % (width // order.shape[0])
+    grad_qkv_w, gain1, bias1, gain2, bias2, grad_down_b, grad_in_b, grad_blend = unpack(
+        write_project, order, project_halves, [(width, 3 * width)] + vectors + [(3, heads)],
+        finish_project, [pltpu.VMEM((lines, PAIR), F32)],
     )
-    vectors = small.reshape(-1)
-    vector = [vectors[at : at + width] for at in range(0, 8 * width, width)]
-    grad_blend = vectors[5 * width : 8 * width].reshape(3, heads, width // heads).sum(-1)
     return (
         output,
         input_grad,
-        vector[0],
-        vector[1],
+        gain1,
+        bias1,
         grad_qkv_w,
         grad_blend,
         grad_out_w,
-        vector[2],
-        vector[3],
+        gain2,
+        bias2,
         grad_in_w,
-        vectors[8 * width : 8 * width + inner],
+        grad_in_b,
         grad_down_w,
-        vector[4],
+        grad_down_b,
     )
 
 

time: 288 us -> 281 us (0.976)
  blocking collectives: 0 us -> 33.1 us
  waiting for transfers between devices: 83.8 us -> 57.1 us
  starting transfers between devices: 56 us -> 46.2 us
  other arithmetic: 9.74 us -> 6.29 us
    all_to_all x0 -> x1, blocking collectives: none -> 33.1 us  [to_sequences(): return lax.all_to_all(block, axis, 0, 0, axis_index_groups=groups)]
    all_to_all x4 -> x3, waiting for transfers between devices: 31.1 us -> 2.95 us  [to_sequences(): return lax.all_to_all(block, axis, 0, 0, axis_index_groups=groups)]
    all_to_all x4 -> x3, starting transfers between devices: 20.7 us -> 14.2 us  [to_sequences(): return lax.all_to_all(block, axis, 0, 0, axis_index_groups=groups)]
    unnamed x43 -> x38, local copies, waits for them, and re-layouts: 4.16 us -> 8.24 us
    slice x3 -> x0, local copies, waits for them, and re-layouts: 3.36 us -> none  [the longest x1 1.36 us: local(): vector = [vectors[at:at + width] for at in range(0, 8 * width, width)]]
    ppermute x28, starting transfers between devices: 35.4 us -> 32 us  [swap(): return lax.ppermute(value, ('seq', 'batch'), route)]
  transfers between devices with their start and end apart: 32 -> 31, of which waited for: 13 -> 11; matrix products, arithmetic and copies ran while one was open for 5% -> 6% of each run, Pallas kernels for 26% -> 30%
where the time goes in v1:
time: 281 us; the launch traced here: 276 us
  Pallas kernels  116 us (41%)
  waiting for transfers between devices  57.1 us (20%)
  starting transfers between devices  46.2 us (16%)
  blocking collectives  33.1 us (12%)
  local copies, waits for them, and re-layouts  12.7 us (5%)
  other arithmetic  6.29 us (2%)
  matrix products  3.61 us (1%)
    ppermute x28, waiting for transfers between devices, swap(): return lax.ppermute(value, ('seq', 'batch'), route)  54.1 us
    pallas_call x4, Pallas kernels, attend_back(): pl.pallas_call(functools.partial(attend_back_kernel, UNITS * PAIR // lane...  46.5 us
    all_to_all x1, blocking collectives, to_sequences(): return lax.all_to_all(block, axis, 0, 0, axis_index_groups=groups)  33.1 us
    ppermute x28, starting transfers between devices, swap(): return lax.ppermute(value, ('seq', 'batch'), route)  32 us
    pallas_call x1, Pallas kernels, feed_forward(): pl.pallas_call(functools.partial(feed_kernel, pieces), grid=(rows // CHUN...  29.5 us
    pallas_call x1, Pallas kernels, attend(): pl.pallas_call(functools.partial(attend_kernel, UNITS * PAIR // lanes, st...  17.7 us
    all_to_all x3, starting transfers between devices, to_sequences(): return lax.all_to_all(block, axis, 0, 0, axis_index_groups=groups)  14.2 us
    pallas_call x2, Pallas kernels, unpack(): pl.pallas_call(functools.partial(unpack_kernel, write, finish), out_shape...  10.9 us
  transfers between devices with their start and end apart: 31, of which 11 were waited for; matrix products, arithmetic and copies ran while one was open for 6% of the time, Pallas kernels for 30%

profile of v1, /device:TPU:0, one launch (start us, length us, event | category | flops | bytes accessed | tf_op | source)
XLA Modules:
  0.0 276.3 jit_solution(3495313940210896890)
XLA Ops:
  0.7 33.1 %all_to_all.20 = bf16[8,128,512]{2,1,0:T(8,128)(2,1)S(1)} all-to-all(bf16[8,128,512]{2,1,0:T(8,128)(2,1)} %param.14), channel_id=1, replica_groups=mesh['seq'=8,'batch'=4] {'seq'}, dimensions={0} | all-to-all | bytes 2097152 | tf_op jit(solution)/shard_map/all_to_all | solution.py:776
  33.7 3.7 %all-to-all-start.1 = ((bf16[8,128,512]{2,1,0:T(8,128)(2,1)}), bf16[8,128,512]{2,1,0:T(8,128)(2,1)S(1)}, u32[]{:S(2)}, u32[]{:S(2)}) async-start(bf16[8,128,512]{2,1,0:T(8,128)(2,1)} %param.15), calls=%async_computation.1 | async-start | bytes 2097152 | tf_op jit(solution)/shard_map/all_to_all | solution.py:776
  41.0 3.6 %convolution_convert_fusion.q_ref.k_ref.v_ref = bf16[1024,1536]{1,0:T(8,128)(2,1)} fusion(bf16[512,1536]{1,0:T(8,128)(2,1)S(1)} %copy-done.5, bf16[1024,512]{1,0:T(8,128)(2,1)S(1)} %bitcast.41, f32[512]{0:T(512)S(1)} %copy-done.9, f32[512]{0:T(512)S(1)} %copy-done.10, f32[1024]{0:T(1024)S(1)} %rsqrt_bitcast_fusion, f32[1024]{0:T(1024)S(1)} %get-tuple-element.147), kind=kOutput, calls=%fused_computation.1 | convolution fusion | flops 1615331328 | bytes 5779456 | tf_op jit(solution)/shard_map/dot_general | solution.py:41
  44.6 17.7 %shard_map.237 = (bf16[1024,512]{1,0:T(8,128)(2,1)}, f32[2,4,128,256]{3,2,1,0:T(8,128)}) custom-call(s32[2]{0:T(128)} %pad_add_fusion.meta_ref, f32[3,512]{1,0:T(4,128)} %reshape.156.blend_ref, bf16[1024,1536]{1,0:T(8,128)(2,1)} %convolution_convert_fusion.q_ref.k_ref.v_ref, bf16[1024,1536]{1,0:T(8,128)(2,1)} %convolution_convert_fusion.q_ref.k_ref.v_ref, ...), custom_call_target="tpu_custom_call" | custom-call | flops 1000 | bytes 1000 | tf_op jit(solution)/shard_map/pallas_call | solution.py:454
  64.0 29.5 %shard_map.238 = (bf16[1024,512]{1,0:T(8,128)(2,1)}, f32[1024,512]{1,0:T(8,128)}, f32[1024,512]{1,0:T(8,128)}, bf16[256,4608]{1,0:T(8,128)(2,1)}, bf16[256,4608]...) custom-call(s32[1]{0:T(128)} %bitcast.core_ref, bf16[1024,512]{1,0:T(8,128)(2,1)} %bitcast.42, ...), custom_call_target="tpu_custom_call" | custom-call | flops 1000 | bytes 1000 | tf_op jit(solution)/shard_map/pallas_call | solution.py:657
  93.6 11.7 %shard_map.239 = (bf16[1024,128]{1,0:T(8,128)(2,1)}, bf16[1024,128]{1,0:T(8,128)(2,1)}, bf16[1024,128]{1,0:T(8,128)(2,1)}, bf16[64,128]{1,0:T(8,128)(2,1)}, bf16...) custom-call(s32[2]{0:T(128)} %pad_add_fusion.meta_ref, f32[3,512]{1,0:T(4,128)} %reshape.156.blend_ref, ...), custom_call_target="tpu_custom_call" | custom-call | flops 1000 | bytes 1000 | tf_op jit(solution)/shard_map/pallas_call | solution.py:480
  108.3 1.5 collective-permute-start.2
  110.6 5.2 %all-to-all-start.2 = ((bf16[8,128,512]{2,1,0:T(8,128)(2,1)}), bf16[8,128,512]{2,1,0:T(8,128)(2,1)S(1)}, u32[]{:S(2)}, u32[]{:S(2)}) async-start(bf16[8,128,512]{2,1,0:T(8,128)(2,1)} %bitcast.10), calls=%async_computation.2 | async-start | bytes 2097152 | tf_op jit(solution)/shard_map/all_to_all | solution.py:776
  115.8 11.5 %shard_map.240 = (bf16[1024,128]{1,0:T(8,128)(2,1)}, bf16[1024,128]{1,0:T(8,128)(2,1)}, bf16[1024,128]{1,0:T(8,128)(2,1)}, bf16[64,128]{1,0:T(8,128)(2,1)}, bf16...) custom-call(s32[2]{0:T(128)} %pad_add_fusion.meta_ref, f32[3,512]{1,0:T(4,128)} %reshape.156.blend_ref, ...), custom_call_target="tpu_custom_call" | custom-call | flops 1000 | bytes 1000 | tf_op jit(solution)/shard_map/pallas_call | solution.py:480
  127.3 11.6 %shard_map.241 = (bf16[1024,128]{1,0:T(8,128)(2,1)}, bf16[1024,128]{1,0:T(8,128)(2,1)}, bf16[1024,128]{1,0:T(8,128)(2,1)}, bf16[64,128]{1,0:T(8,128)(2,1)}, bf16...) custom-call(s32[2]{0:T(128)} %pad_add_fusion.meta_ref, f32[3,512]{1,0:T(4,128)} %reshape.156.blend_ref, ...), custom_call_target="tpu_custom_call" | custom-call | flops 1000 | bytes 1000 | tf_op jit(solution)/shard_map/pallas_call | solution.py:480
  138.9 5.6 %collective-permute-done.1 = bf16[4,16,4608]{2,1,0:T(8,128)(2,1)S(1)} collective-permute-done((bf16[4,16,4608]{2,1,0:T(8,128)(2,1)}, bf16[4,16,4608]{2,1,0:T(8,128)(2,1)S(1)}, u32[]{:S(2)}, u32[]{:S(2)}) %collective-permute-start.1) | collective-permute-done | bytes 589856 | tf_op jit(solution)/shard_map/ppermute | solution.py:836
  144.5 1.5 add_convert_fusion.2
  147.4 2.4 collective-permute-start.5
  151.6 11.7 %shard_map.243 = (bf16[1024,128]{1,0:T(8,128)(2,1)}, bf16[1024,128]{1,0:T(8,128)(2,1)}, bf16[1024,128]{1,0:T(8,128)(2,1)}, bf16[64,128]{1,0:T(8,128)(2,1)}, bf16...) custom-call(s32[2]{0:T(128)} %pad_add_fusion.meta_ref, f32[3,512]{1,0:T(4,128)} %reshape.156.blend_ref, ...), custom_call_target="tpu_custom_call" | custom-call | flops 1000 | bytes 1000 | tf_op jit(solution)/shard_map/pallas_call | solution.py:480
  164.4 3.3 %collective-permute-start.8 = (bf16[1,16,4608]{2,1,0:T(8,128)(2,1)}, bf16[1,16,4608]{2,1,0:T(8,128)(2,1)}, u32[]{:S(2)}, u32[]{:S(2)}) collective-permute-start(bf16[1,16,4608]{2,1,0:T(8,128)(2,1)} %add_convert_fusion.4), channel_id=1, source_target_pairs={{0,16},{1,17},{2,18},{3,19},{4,20},{5,21},{6,22},{7,23},{8,24},{9,... | collective-permute-start | bytes 442376 | tf_op jit(solution)/shard_map/ppermute | solution.py:836
  168.5 9.3 %shard_map.244 = (bf16[1024,512]{1,0:T(8,128)(2,1)}, bf16[256,1792]{1,0:T(8,128)(2,1)}, bf16[256,1792]{1,0:T(8,128)(2,1)}) custom-call(s32[1]{0:T(128)} %bitcast.core_ref, bf16[1024,512]{1,0:T(8,128)(2,1)} %bitcast.43, f32[1024,512]{1,0:T(8,128)} %get-tuple-element.88.first_ref, bf16[512,1536]{1,0:T(8,128)(2,1)} %w_ref.1, f32[1,512]{1,0:T(1,128)} %bitcast.57, ...), custom_call_target="tpu_custom_call" | custom-call | flops 1000 | bytes 1000 | tf_op jit(solution)/shard_map/pallas_call | solution.py:754
  178.9 5.2 %all-to-all-start.3 = ((bf16[8,128,512]{2,1,0:T(8,128)(2,1)}), bf16[8,128,512]{2,1,0:T(8,128)(2,1)S(1)}, u32[]{:S(2)}, u32[]{:S(2)}) async-start(bf16[8,128,512]{2,1,0:T(8,128)(2,1)} %bitcast.48), calls=%async_computation.3 | async-start | bytes 2097152 | tf_op jit(solution)/shard_map/all_to_all | solution.py:776
  187.5 2.1 collective-permute-start.11
  191.1 17.1 %collective-permute-done.11 = bf16[4,16,1792]{2,1,0:T(8,128)(2,1)S(1)} collective-permute-done((bf16[4,16,1792]{2,1,0:T(8,128)(2,1)S(1)}, bf16[4,16,1792]{2,1,0:T(8,128)(2,1)S(1)}, u32[]{:S(2)}, u32[]{:S(2)}) %collective-permute-start.11) | collective-permute-done | bytes 229408 | tf_op jit(solution)/shard_map/ppermute | solution.py:836
  208.4 2.2 all-to-all-done.3.source_ref
  210.7 2.8 %collective-permute-start.15 = (bf16[1,16,1792]{2,1,0:T(8,128)(2,1)S(1)}, bf16[1,16,1792]{2,1,0:T(8,128)(2,1)S(1)}, u32[]{:S(2)}, u32[]{:S(2)}) collective-permute-start(bf16[1,16,1792]{2,1,0:T(8,128)(2,1)S(1)} %get-tuple-element.143), channel_id=1, source_target_pairs={{0,16},{1,17},{2,18},{3,19},{4,20},{5,21},{6,22},{7,23},{8,24},{9,... | collective-permute-start | bytes 172040 | tf_op jit(solution)/shard_map/ppermute | solution.py:836
  213.5 1.6 collective-permute-start.16
  219.6 10.8 %collective-permute-done.17 = bf16[4,16,4608]{2,1,0:T(8,128)(2,1)S(1)} collective-permute-done((bf16[4,16,4608]{2,1,0:T(8,128)(2,1)S(1)}, bf16[4,16,4608]{2,1,0:T(8,128)(2,1)S(1)}, u32[]{:S(2)}, u32[]{:S(2)}) %collective-permute-start.17) | collective-permute-done | bytes 589856 | tf_op jit(solution)/shard_map/ppermute | solution.py:836
  230.4 2.3 collective-permute-done.18
  232.8 9.9 %collective-permute-done.19 = bf16[4,16,4608]{2,1,0:T(8,128)(2,1)S(1)} collective-permute-done((bf16[4,16,4608]{2,1,0:T(8,128)(2,1)S(1)}, bf16[4,16,4608]{2,1,0:T(8,128)(2,1)S(1)}, u32[]{:S(2)}, u32[]{:S(2)}) %collective-permute-start.19) | collective-permute-done | bytes 589856 | tf_op jit(solution)/shard_map/ppermute | solution.py:836
  243.4 3.4 %collective-permute-start.21 = (bf16[1,16,1792]{2,1,0:T(8,128)(2,1)S(1)}, bf16[1,16,1792]{2,1,0:T(8,128)(2,1)S(1)}, u32[]{:S(2)}, u32[]{:S(2)}) collective-permute-start(bf16[1,16,1792]{2,1,0:T(8,128)(2,1)S(1)} %pad_maximum_fusion.2), channel_id=1, source_target_pairs={{0,16},{1,17},{2,18},{3,19},{4,20},{5,21},{6,22},{7,23},{8,24},{9,... | collective-permute-start | bytes 172040 | tf_op jit(solution)/shard_map/ppermute | solution.py:836
  247.8 2.8 %collective-permute-done.21 = bf16[1,16,1792]{2,1,0:T(8,128)(2,1)S(1)} collective-permute-done((bf16[1,16,1792]{2,1,0:T(8,128)(2,1)S(1)}, bf16[1,16,1792]{2,1,0:T(8,128)(2,1)S(1)}, u32[]{:S(2)}, u32[]{:S(2)}) %collective-permute-start.21) | collective-permute-done | bytes 57376 | tf_op jit(solution)/shard_map/ppermute | solution.py:836
  250.6 2.2 collective-permute-done.22
  254.2 1.5 collective-permute-start.25
  258.8 7.2 %shard_map.246 = (f32[512,2048]{1,0:T(8,128)}, f32[512,512]{1,0:T(8,128)}, f32[2048,512]{1,0:T(8,128)}) custom-call(s32[32]{0:T(128)} %fusion.10.order_ref, bf16[16,16,4608]{2,1,0:T(8,128)(2,1)} %copy-done.2, bf16[16,16,4608]{2,1,0:T(8,128)(2,1)} %copy-done.4), custom_call_target="tpu_custom_call" | custom-call | flops 1000 | bytes 1000 | tf_op jit(solution)/shard_map/pallas_call | solution.py:928
  268.9 2.5 collective-permute-done.27.other_ref
  272.3 3.8 %shard_map.247 = (f32[512,1536]{1,0:T(8,128)}, f32[512]{0:T(512)}, f32[512]{0:T(512)}, f32[512]{0:T(512)}, f32[512]{0:T(512)}, /*index=5*/f32[512]{0:T(512)}, f32[2048]{0:T(1024)}, f32[3,8]{1,0:T(4,128)}) custom-call(s32[32]{0:T(128)} %fusion.10.order_ref, bf16[16,16,1792]{2,1,0:T(8,128)(2,1)} %copy-done.6, bf16[16,16,1792]{2,1,0:T(8,128)(2,1)} %copy-done.8), custom_call_target="tpu_custom_call" | custom-call | flops 1000 | bytes 1000 | tf_op jit(solution)/shard_map/pallas_call | solution.py:928
  (113 shorter events, 34.9 us)
Async XLA Ops:
  0.7 37.6 %copy-start.12 = (s32[8]{0:T(128)S(1)}, s32[8]{0:T(128)}, u32[]{:S(2)}) copy-start(s32[8]{0:T(128)} %param.16) | copy-start | bytes 100
  33.7 29.3 %all-to-all-start.1 = ((bf16[8,128,512]{2,1,0:T(8,128)(2,1)}), bf16[8,128,512]{2,1,0:T(8,128)(2,1)S(1)}, u32[]{:S(2)}, u32[]{:S(2)}) async-start(bf16[8,128,512]{2,1,0:T(8,128)(2,1)} %param.15), calls=%async_computation.1 | async-start | bytes 2097152 | tf_op jit(solution)/shard_map/all_to_all | solution.py:776
  93.5 11.8 %collective-permute-start = (bf16[16,16,4608]{2,1,0:T(8,128)(2,1)}, bf16[16,16,4608]{2,1,0:T(8,128)(2,1)S(1)}, u32[]{:S(2)}, u32[]{:S(2)}) collective-permute-start(bf16[16,16,4608]{2,1,0:T(8,128)(2,1)} %bitcast.58), channel_id=1, source_target_pairs={{0,1},{1,0},{2,3},{3,2},{4,5},{5,4},{6,7},{7,6},{8,9},{9,8},{10,11... | collective-permute-start | bytes 7077896 | tf_op jit(solution)/shard_map/ppermute | solution.py:836
  107.1 37.4 %collective-permute-start.1 = (bf16[4,16,4608]{2,1,0:T(8,128)(2,1)}, bf16[4,16,4608]{2,1,0:T(8,128)(2,1)S(1)}, u32[]{:S(2)}, u32[]{:S(2)}) collective-permute-start(bf16[4,16,4608]{2,1,0:T(8,128)(2,1)} %get-tuple-element.128), channel_id=1, source_target_pairs={{0,4},{1,5},{2,6},{3,7},{4,0},{5,1},{6,2},{7,3},{8,12},{9,13},{10,... | collective-permute-start | bytes 1769480 | tf_op jit(solution)/shard_map/ppermute | solution.py:836
  108.3 36.2 %collective-permute-start.2 = (bf16[4,16,4608]{2,1,0:T(8,128)(2,1)S(1)}, bf16[4,16,4608]{2,1,0:T(8,128)(2,1)}, u32[]{:S(2)}, u32[]{:S(2)}) collective-permute-start(bf16[4,16,4608]{2,1,0:T(8,128)(2,1)S(1)} %get-tuple-element.127), channel_id=1, source_target_pairs={{0,2},{1,3},{2,0},{3,1},{4,6},{5,7},{6,4},{7,5},{8,10},{9,11},{10,... | collective-permute-start | bytes 1769480 | tf_op jit(solution)/shard_map/ppermute | solution.py:836
  109.8 34.7 %collective-permute-start.3 = (bf16[4,16,4608]{2,1,0:T(8,128)(2,1)S(1)}, bf16[4,16,4608]{2,1,0:T(8,128)(2,1)}, u32[]{:S(2)}, u32[]{:S(2)}) collective-permute-start(bf16[4,16,4608]{2,1,0:T(8,128)(2,1)S(1)} %get-tuple-element.126), channel_id=1, source_target_pairs={{0,6},{1,7},{2,4},{3,5},{4,2},{5,3},{6,0},{7,1},{8,14},{9,15},{10,... | collective-permute-start | bytes 1769480 | tf_op jit(solution)/shard_map/ppermute | solution.py:836
  110.6 40.0 %all-to-all-start.2 = ((bf16[8,128,512]{2,1,0:T(8,128)(2,1)}), bf16[8,128,512]{2,1,0:T(8,128)(2,1)S(1)}, u32[]{:S(2)}, u32[]{:S(2)}) async-start(bf16[8,128,512]{2,1,0:T(8,128)(2,1)} %bitcast.10), calls=%async_computation.2 | async-start | bytes 2097152 | tf_op jit(solution)/shard_map/all_to_all | solution.py:776
  146.1 17.2 %collective-permute-start.4 = (bf16[1,16,4608]{2,1,0:T(8,128)(2,1)S(1)}, bf16[1,16,4608]{2,1,0:T(8,128)(2,1)S(1)}, u32[]{:S(2)}, u32[]{:S(2)}) collective-permute-start(bf16[1,16,4608]{2,1,0:T(8,128)(2,1)S(1)} %get-tuple-element.138), channel_id=1, source_target_pairs={{0,8},{1,9},{2,10},{3,11},{4,12},{5,13},{6,14},{7,15},{8,0},{9,1},... | collective-permute-start | bytes 442376 | tf_op jit(solution)/shard_map/ppermute | solution.py:836
  147.4 15.9 %collective-permute-start.5 = (bf16[1,16,4608]{2,1,0:T(8,128)(2,1)S(1)}, bf16[1,16,4608]{2,1,0:T(8,128)(2,1)S(1)}, u32[]{:S(2)}, u32[]{:S(2)}) collective-permute-start(bf16[1,16,4608]{2,1,0:T(8,128)(2,1)S(1)} %get-tuple-element.137), channel_id=1, source_target_pairs={{0,16},{1,17},{2,18},{3,19},{4,20},{5,21},{6,22},{7,23},{8,24},{9,... | collective-permute-start | bytes 442376 | tf_op jit(solution)/shard_map/ppermute | solution.py:836
  149.8 13.6 %collective-permute-start.6 = (bf16[1,16,4608]{2,1,0:T(8,128)(2,1)S(1)}, bf16[1,16,4608]{2,1,0:T(8,128)(2,1)S(1)}, u32[]{:S(2)}, u32[]{:S(2)}) collective-permute-start(bf16[1,16,4608]{2,1,0:T(8,128)(2,1)S(1)} %get-tuple-element.136), channel_id=1, source_target_pairs={{0,24},{1,25},{2,26},{3,27},{4,28},{5,29},{6,30},{7,31},{8,16},{9,... | collective-permute-start | bytes 442376 | tf_op jit(solution)/shard_map/ppermute | solution.py:836
  164.1 20.1 %collective-permute-start.7 = (bf16[1,16,4608]{2,1,0:T(8,128)(2,1)}, bf16[1,16,4608]{2,1,0:T(8,128)(2,1)}, u32[]{:S(2)}, u32[]{:S(2)}) collective-permute-start(bf16[1,16,4608]{2,1,0:T(8,128)(2,1)} %add_convert_fusion.4), channel_id=1, source_target_pairs={{0,8},{1,9},{2,10},{3,11},{4,12},{5,13},{6,14},{7,15},{8,0},{9,1},... | collective-permute-start | bytes 442376 | tf_op jit(solution)/shard_map/ppermute | solution.py:836
  164.4 20.7 %collective-permute-start.8 = (bf16[1,16,4608]{2,1,0:T(8,128)(2,1)}, bf16[1,16,4608]{2,1,0:T(8,128)(2,1)}, u32[]{:S(2)}, u32[]{:S(2)}) collective-permute-start(bf16[1,16,4608]{2,1,0:T(8,128)(2,1)} %add_convert_fusion.4), channel_id=1, source_target_pairs={{0,16},{1,17},{2,18},{3,19},{4,20},{5,21},{6,22},{7,23},{8,24},{9,... | collective-permute-start | bytes 442376 | tf_op jit(solution)/shard_map/ppermute | solution.py:836
  167.7 18.3 %collective-permute-start.9 = (bf16[1,16,4608]{2,1,0:T(8,128)(2,1)}, bf16[1,16,4608]{2,1,0:T(8,128)(2,1)}, u32[]{:S(2)}, u32[]{:S(2)}) collective-permute-start(bf16[1,16,4608]{2,1,0:T(8,128)(2,1)} %add_convert_fusion.4), channel_id=1, source_target_pairs={{0,24},{1,25},{2,26},{3,27},{4,28},{5,29},{6,30},{7,31},{8,16},{9,... | collective-permute-start | bytes 442376 | tf_op jit(solution)/shard_map/ppermute | solution.py:836
  178.8 8.1 %collective-permute-start.10 = (bf16[16,16,1792]{2,1,0:T(8,128)(2,1)}, bf16[16,16,1792]{2,1,0:T(8,128)(2,1)S(1)}, u32[]{:S(2)}, u32[]{:S(2)}) collective-permute-start(bf16[16,16,1792]{2,1,0:T(8,128)(2,1)} %bitcast.59), channel_id=1, source_target_pairs={{0,1},{1,0},{2,3},{3,2},{4,5},{5,4},{6,7},{7,6},{8,9},{9,8},{10,11... | collective-permute-start | bytes 2752520 | tf_op jit(solution)/shard_map/ppermute | solution.py:836
  178.9 31.6 %all-to-all-start.3 = ((bf16[8,128,512]{2,1,0:T(8,128)(2,1)}), bf16[8,128,512]{2,1,0:T(8,128)(2,1)S(1)}, u32[]{:S(2)}, u32[]{:S(2)}) async-start(bf16[8,128,512]{2,1,0:T(8,128)(2,1)} %bitcast.48), calls=%async_computation.3 | async-start | bytes 2097152 | tf_op jit(solution)/shard_map/all_to_all | solution.py:776
  187.5 20.7 %collective-permute-start.11 = (bf16[4,16,1792]{2,1,0:T(8,128)(2,1)S(1)}, bf16[4,16,1792]{2,1,0:T(8,128)(2,1)S(1)}, u32[]{:S(2)}, u32[]{:S(2)}) collective-permute-start(bf16[4,16,1792]{2,1,0:T(8,128)(2,1)S(1)} %get-tuple-element.134), channel_id=1, source_target_pairs={{0,4},{1,5},{2,6},{3,7},{4,0},{5,1},{6,2},{7,3},{8,12},{9,13},{10,... | collective-permute-start | bytes 688136 | tf_op jit(solution)/shard_map/ppermute | solution.py:836
  189.6 18.6 %collective-permute-start.12 = (bf16[4,16,1792]{2,1,0:T(8,128)(2,1)S(1)}, bf16[4,16,1792]{2,1,0:T(8,128)(2,1)S(1)}, u32[]{:S(2)}, u32[]{:S(2)}) collective-permute-start(bf16[4,16,1792]{2,1,0:T(8,128)(2,1)S(1)} %get-tuple-element.133), channel_id=1, source_target_pairs={{0,2},{1,3},{2,0},{3,1},{4,6},{5,7},{6,4},{7,5},{8,10},{9,11},{10,... | collective-permute-start | bytes 688136 | tf_op jit(solution)/shard_map/ppermute | solution.py:836
  191.1 17.2 %collective-permute-start.13 = (bf16[4,16,1792]{2,1,0:T(8,128)(2,1)S(1)}, bf16[4,16,1792]{2,1,0:T(8,128)(2,1)S(1)}, u32[]{:S(2)}, u32[]{:S(2)}) collective-permute-start(bf16[4,16,1792]{2,1,0:T(8,128)(2,1)S(1)} %get-tuple-element.132), channel_id=1, source_target_pairs={{0,6},{1,7},{2,4},{3,5},{4,2},{5,3},{6,0},{7,1},{8,14},{9,15},{10,... | collective-permute-start | bytes 688136 | tf_op jit(solution)/shard_map/ppermute | solution.py:836
  210.6 7.3 %collective-permute-start.14 = (bf16[1,16,1792]{2,1,0:T(8,128)(2,1)S(1)}, bf16[1,16,1792]{2,1,0:T(8,128)(2,1)S(1)}, u32[]{:S(2)}, u32[]{:S(2)}) collective-permute-start(bf16[1,16,1792]{2,1,0:T(8,128)(2,1)S(1)} %get-tuple-element.144), channel_id=1, source_target_pairs={{0,8},{1,9},{2,10},{3,11},{4,12},{5,13},{6,14},{7,15},{8,0},{9,1},... | collective-permute-start | bytes 172040 | tf_op jit(solution)/shard_map/ppermute | solution.py:836
  210.7 7.9 %collective-permute-start.15 = (bf16[1,16,1792]{2,1,0:T(8,128)(2,1)S(1)}, bf16[1,16,1792]{2,1,0:T(8,128)(2,1)S(1)}, u32[]{:S(2)}, u32[]{:S(2)}) collective-permute-start(bf16[1,16,1792]{2,1,0:T(8,128)(2,1)S(1)} %get-tuple-element.143), channel_id=1, source_target_pairs={{0,16},{1,17},{2,18},{3,19},{4,20},{5,21},{6,22},{7,23},{8,24},{9,... | collective-permute-start | bytes 172040 | tf_op jit(solution)/shard_map/ppermute | solution.py:836
  213.5 6.0 %collective-permute-start.16 = (bf16[1,16,1792]{2,1,0:T(8,128)(2,1)S(1)}, bf16[1,16,1792]{2,1,0:T(8,128)(2,1)S(1)}, u32[]{:S(2)}, u32[]{:S(2)}) collective-permute-start(bf16[1,16,1792]{2,1,0:T(8,128)(2,1)S(1)} %get-tuple-element.142), channel_id=1, source_target_pairs={{0,24},{1,25},{2,26},{3,27},{4,28},{5,29},{6,30},{7,31},{8,16},{9,... | collective-permute-start | bytes 172040 | tf_op jit(solution)/shard_map/ppermute | solution.py:836
  215.0 15.4 %collective-permute-start.17 = (bf16[4,16,4608]{2,1,0:T(8,128)(2,1)S(1)}, bf16[4,16,4608]{2,1,0:T(8,128)(2,1)S(1)}, u32[]{:S(2)}, u32[]{:S(2)}) collective-permute-start(bf16[4,16,4608]{2,1,0:T(8,128)(2,1)S(1)} %constant_dynamic-update-slice_fusion), channel_id=1, source_target_pairs={{0,4},{1,5},{2,6},{3,7},{4,0},{5,1},{6,2},{7,3},{8,12},{9,13},{10,... | collective-permute-start | bytes 1769480 | tf_op jit(solution)/shard_map/ppermute | solution.py:836
  216.5 16.3 %collective-permute-start.18 = (bf16[4,16,4608]{2,1,0:T(8,128)(2,1)S(1)}, bf16[4,16,4608]{2,1,0:T(8,128)(2,1)S(1)}, u32[]{:S(2)}, u32[]{:S(2)}) collective-permute-start(bf16[4,16,4608]{2,1,0:T(8,128)(2,1)S(1)} %constant_dynamic-update-slice_fusion), channel_id=1, source_target_pairs={{0,2},{1,3},{2,0},{3,1},{4,6},{5,7},{6,4},{7,5},{8,10},{9,11},{10,... | collective-permute-start | bytes 1769480 | tf_op jit(solution)/shard_map/ppermute | solution.py:836
  217.9 24.7 %collective-permute-start.19 = (bf16[4,16,4608]{2,1,0:T(8,128)(2,1)S(1)}, bf16[4,16,4608]{2,1,0:T(8,128)(2,1)S(1)}, u32[]{:S(2)}, u32[]{:S(2)}) collective-permute-start(bf16[4,16,4608]{2,1,0:T(8,128)(2,1)S(1)} %constant_dynamic-update-slice_fusion), channel_id=1, source_target_pairs={{0,6},{1,7},{2,4},{3,5},{4,2},{5,3},{6,0},{7,1},{8,14},{9,15},{10,... | collective-permute-start | bytes 1769480 | tf_op jit(solution)/shard_map/ppermute | solution.py:836
  242.7 14.7 %collective-permute-start.23 = (bf16[16,16,4608]{2,1,0:T(8,128)(2,1)S(1)}, bf16[16,16,4608]{2,1,0:T(8,128)(2,1)S(1)}, u32[]{:S(2)}, u32[]{:S(2)}) collective-permute-start(bf16[16,16,4608]{2,1,0:T(8,128)(2,1)S(1)} %constant_dynamic-update-slice_fusion.4.own_ref), channel_id=1, source_target_pairs={{0,1},{1,0},{2,3},{3,2},{4,5},{5,4},{6,7},{7,6},{8,9},{9,8},{10,11... | collective-permute-start | bytes 7077896 | tf_op jit(solution)/shard_map/ppermute | solution.py:836
  243.4 4.4 %collective-permute-start.20 = (bf16[1,16,1792]{2,1,0:T(8,128)(2,1)S(1)}, bf16[1,16,1792]{2,1,0:T(8,128)(2,1)S(1)}, u32[]{:S(2)}, u32[]{:S(2)}) collective-permute-start(bf16[1,16,1792]{2,1,0:T(8,128)(2,1)S(1)} %pad_maximum_fusion.2), channel_id=1, source_target_pairs={{0,8},{1,9},{2,10},{3,11},{4,12},{5,13},{6,14},{7,15},{8,0},{9,1},... | collective-permute-start | bytes 172040 | tf_op jit(solution)/shard_map/ppermute | solution.py:836
  243.4 7.2 %collective-permute-start.21 = (bf16[1,16,1792]{2,1,0:T(8,128)(2,1)S(1)}, bf16[1,16,1792]{2,1,0:T(8,128)(2,1)S(1)}, u32[]{:S(2)}, u32[]{:S(2)}) collective-permute-start(bf16[1,16,1792]{2,1,0:T(8,128)(2,1)S(1)} %pad_maximum_fusion.2), channel_id=1, source_target_pairs={{0,16},{1,17},{2,18},{3,19},{4,20},{5,21},{6,22},{7,23},{8,24},{9,... | collective-permute-start | bytes 172040 | tf_op jit(solution)/shard_map/ppermute | solution.py:836
  246.9 6.0 %collective-permute-start.22 = (bf16[1,16,1792]{2,1,0:T(8,128)(2,1)S(1)}, bf16[1,16,1792]{2,1,0:T(8,128)(2,1)S(1)}, u32[]{:S(2)}, u32[]{:S(2)}) collective-permute-start(bf16[1,16,1792]{2,1,0:T(8,128)(2,1)S(1)} %pad_maximum_fusion.2), channel_id=1, source_target_pairs={{0,24},{1,25},{2,26},{3,27},{4,28},{5,29},{6,30},{7,31},{8,16},{9,... | collective-permute-start | bytes 172040 | tf_op jit(solution)/shard_map/ppermute | solution.py:836
  252.8 13.1 %collective-permute-start.24 = (bf16[4,16,1792]{2,1,0:T(8,128)(2,1)S(1)}, bf16[4,16,1792]{2,1,0:T(8,128)(2,1)}, u32[]{:S(2)}, u32[]{:S(2)}) collective-permute-start(bf16[4,16,1792]{2,1,0:T(8,128)(2,1)S(1)} %constant_dynamic-update-slice_fusion.8), channel_id=1, source_target_pairs={{0,4},{1,5},{2,6},{3,7},{4,0},{5,1},{6,2},{7,3},{8,12},{9,13},{10,... | collective-permute-start | bytes 688136 | tf_op jit(solution)/shard_map/ppermute | solution.py:836
  254.2 12.7 %collective-permute-start.25 = (bf16[4,16,1792]{2,1,0:T(8,128)(2,1)S(1)}, bf16[4,16,1792]{2,1,0:T(8,128)(2,1)}, u32[]{:S(2)}, u32[]{:S(2)}) collective-permute-start(bf16[4,16,1792]{2,1,0:T(8,128)(2,1)S(1)} %constant_dynamic-update-slice_fusion.8), channel_id=1, source_target_pairs={{0,2},{1,3},{2,0},{3,1},{4,6},{5,7},{6,4},{7,5},{8,10},{9,11},{10,... | collective-permute-start | bytes 688136 | tf_op jit(solution)/shard_map/ppermute | solution.py:836
  255.7 12.2 %collective-permute-start.26 = (bf16[4,16,1792]{2,1,0:T(8,128)(2,1)S(1)}, bf16[4,16,1792]{2,1,0:T(8,128)(2,1)}, u32[]{:S(2)}, u32[]{:S(2)}) collective-permute-start(bf16[4,16,1792]{2,1,0:T(8,128)(2,1)S(1)} %constant_dynamic-update-slice_fusion.8), channel_id=1, source_target_pairs={{0,6},{1,7},{2,4},{3,5},{4,2},{5,3},{6,0},{7,1},{8,14},{9,15},{10,... | collective-permute-start | bytes 688136 | tf_op jit(solution)/shard_map/ppermute | solution.py:836
  268.9 2.5 collective-permute-start.27
  (12 other events, 102.0 us)

commit v2 on v1

--- a/solution.py
+++ b/solution.py
@@ -149,7 +149,8 @@
     together, whole_sequence, meta_ref, blend_ref, q_ref, k_ref, v_ref, *refs
 ):
     halo_k, halo_v, state_ref = (None,) * 3 if whole_sequence else refs[:3]
-    att_ref, total_ref, keys, values, fq, fk, state = refs[-7:]
+    att_ref, keys, values, fq, fk, state = refs[-6:] if whole_sequence else refs[3:4] + refs[-5:]
+    total_ref = None if whole_sequence else refs[4]
     rows, width = q_ref.shape
     pairs = range(width // PAIR)
     near_by = range(together)
@@ -201,6 +202,8 @@
         return carry
 
     lax.fori_loop(0, rows // (together * TILE), step, 0)
+    if whole_sequence:
+        return
     last = pl.ds(rows, TILE)
     for p in pairs:
         for c in range(2):
@@ -227,7 +230,10 @@
     together, whole_sequence, meta_ref, blend_ref, q_ref, k_ref, v_ref, go_ref, *refs
 ):
     halo_k, halo_v, state_ref, later_ref = (None,) * 4 if whole_sequence else refs[:4]
-    gq_ref, gk_ref, gv_ref, hk_ref, hv_ref, mix_ref, total_ref = refs[-16:-9]
+    if whole_sequence:
+        gq_ref, gk_ref, gv_ref, mix_ref = refs[:4]
+    else:
+        gq_ref, gk_ref, gv_ref, mix_ref, hk_ref, hv_ref, total_ref = refs[4:11]
     keys, values, fq, fk, state, gk, gv, gfk, gon = refs[-9:]
     rows, width = q_ref.shape
     pairs = range(width // PAIR)
@@ -359,8 +365,9 @@
         return carry
 
     lax.fori_loop(0, tiles // together, step, 0)
-    hk_ref[...] = gk[:TILE, :].astype(BF16)
-    hv_ref[...] = gv[:TILE, :].astype(BF16)
+    if not whole_sequence:
+        hk_ref[...] = gk[:TILE, :].astype(BF16)
+        hv_ref[...] = gv[:TILE, :].astype(BF16)
     state[...] = jnp.zeros_like(state) if whole_sequence else later_ref[...]
 
     def come(at, c, p):
@@ -408,6 +415,8 @@
         return carry
 
     lax.fori_loop(0, tiles // together, back_step, 0)
+    if whole_sequence:
+        return
     for p in pairs:
         for c in range(2):
             total_ref[c, p] = state[c, p] + come(0, c, p) + come(TILE, c, p)
@@ -441,7 +450,7 @@
     return jax.ShapeDtypeStruct(shape, dtype), pl.BlockSpec(shape, lambda _: (0,) * len(shape))
 
 
-UNITS = 8
+UNITS = 16
 
 
 def attend(meta, blend, qkv, halo, state):
@@ -457,9 +466,9 @@
         out_shape=(
             jax.ShapeDtypeStruct((rows, width), BF16),
             jax.ShapeDtypeStruct(share, F32),
-        ),
+        )[: 1 if state is None else 2],
         in_specs=ins + before[: len(earlier)],
-        out_specs=(columns(rows, 0), held),
+        out_specs=(columns(rows, 0), held)[: 1 if state is None else 2],
         scratch_shapes=attention_scratch(rows, lanes, False),
         compiler_params=pltpu.CompilerParams(vmem_limit_bytes=VMEM),
         cost_estimate=BRIEF,
@@ -471,12 +480,11 @@
     lanes = width // calls
     columns, ins, before = attention_specs(rows, width, lanes, lambda i: number)
     others = () if state is None else (halo, halo, state, later)
-    shapes, blocks = zip(
-        *[outcome((rows, lanes), BF16)] * 3,
-        *[outcome((TILE, lanes), BF16)] * 2,
-        outcome((3, lanes), F32),
-        outcome((2, lanes // PAIR, PAIR, 2 * PAIR), F32),
-    )
+    outs = [outcome((rows, lanes), BF16)] * 3 + [outcome((3, lanes), F32)]
+    if state is not None:
+        outs += [outcome((TILE, lanes), BF16)] * 2
+        outs += [outcome((2, lanes // PAIR, PAIR, 2 * PAIR), F32)]
+    shapes, blocks = zip(*outs)
     return pl.pallas_call(
         functools.partial(attend_back_kernel, UNITS * PAIR // lanes, state is None),
         grid=(1,),
@@ -780,6 +788,25 @@
     return lax.optimization_barrier((value,) + others)[0]
 
 
+def join_kernel(*refs):
+    out_ref = refs[-1]
+    size = refs[0].shape[0]
+    for k, part in enumerate(refs[:-1]):
+        out_ref[k * size : (k + 1) * size] = part[...]
+
+
+def join(parts):
+    vmem, part = pl.BlockSpec(memory_space=pltpu.VMEM), parts[0]
+    return pl.pallas_call(
+        join_kernel,
+        out_shape=jax.ShapeDtypeStruct((len(parts) * part.shape[0],) + part.shape[1:], part.dtype),
+        in_specs=[vmem] * len(parts),
+        out_specs=vmem,
+        compiler_params=pltpu.CompilerParams(vmem_limit_bytes=16 * 2**20),
+        cost_estimate=BRIEF,
+    )(*parts)
+
+
 def settle_kernel(source_ref, out_ref):
     out_ref[...] = source_ref[...]
 
@@ -860,7 +887,7 @@
 
     def gather(self, value, level, beside=()):
         parts = [self.swap(value, level, k) for k in range(1, self.sizes[level])]
-        return jnp.concatenate([after(value, *beside)] + parts, 0)
+        return join([after(value, *beside)] + parts)
 
     def to_pieces(self, value):
         return value.reshape(self.pieces // 2, -1, value.shape[1])
@@ -1007,15 +1034,12 @@
         held = None
         for number in range(calls):
             if number == 1:
-                held = ring.scatter_cores(feed_keep, feed_send, 0, (backs[0][5],))
-                turn = after(turn, held)
-            if number == 3:
-                held = ring.scatter(held, "near", 0, (backs[2][5],))
+                held = ring.scatter_cores(feed_keep, feed_send, 0, (backs[0][3],))
                 turn = after(turn, held)
             backs.append(back(turn, number, later))
-            turn = after(turn, backs[-1][5])
-        held = ring.scatter(held, "far", 0, (backs[3][5],))
-        output = settle(after(output, backs[2][5]))
+            turn = after(turn, backs[-1][3])
+        held = ring.scatter(held, "near", 0, (backs[3][3],))
+        output = settle(after(output, backs[2][3]))
         grad_first = after(grad_first, held, output)
     else:
         backs = [back(meta, number, later) for number in range(calls)]
@@ -1024,33 +1048,39 @@
         homeward = [(i + seqs, i) for i in range(devices - seqs)]
         for part in (1, 2):
             for number in range(calls):
-                received = lax.ppermute(backs[number][part + 2], "seq", homeward)
+                received = lax.ppermute(backs[number][part + 3], "seq", homeward)
                 grad = grads[part][number]
                 tail = grad[rows - TILE :].astype(F32) + received.astype(F32)
                 grads[part][number] = grad.at[rows - TILE :].set(tail.astype(BF16))
     grads = grads[0] + grads[1] + grads[2]
     grad_x, project_keep, project_send = project_back(
         core, x, grad_first, qkv_weight, norm1_gain, norm1_bias, small2, grad_in_b, grads,
-        [call[5] for call in backs],
+        [call[3] for call in backs],
     )
-    moved = to_sequences(grad_x.reshape(seqs, span, width), "seq", groups)
+
+    def move(grad_x):
+        return to_sequences(grad_x.reshape(seqs, span, width), "seq", groups)
 
     if by_ring:
         order = ring.order()
-        held = ring.gather(held, "far", (project_keep,))
+        held = ring.scatter(held, "far", 0, (project_keep,))
         late = ring.scatter_cores(project_keep, project_send, PAIR, (held,))
+        held = ring.gather(held, "far")
+        moved = move(after(grad_x, late))
         near = [ring.swap(held, "near", k) for k in range(1, ring.sizes["near"])]
-        late = after(ring.scatter(late, "near", PAIR), moved)
+        late = ring.scatter(late, "near", PAIR, (held,))
         late = ring.scatter(late, "far", PAIR)
-        held = jnp.concatenate([after(held, late)] + near, 0)
+        late = ring.gather(late, "far")
+        last = [ring.swap(late, "near", k) for k in range(1, ring.sizes["near"])]
+        input_grad = settle(after(moved, late))
+        held = join([after(held, late, input_grad)] + near)
         other = ring.swap(held, "core", 1)
-        late = ring.gather(late, "far", (held,))
+        late = join([after(late, held)] + last)
+        rest = ring.swap(late, "core", 1)
         grad_in_w, grad_out_w, grad_down_w = unpack_feed(order, (held, after(other, late)))
-        input_grad = settle(after(moved, late))
-        late = ring.gather(late, "near", (input_grad, grad_out_w))
-        project_halves = late, ring.swap(late, "core", 1)
+        project_halves = after(late, grad_out_w), rest
     else:
-        input_grad = moved
+        input_grad = move(grad_x)
         order = jnp.arange(16, dtype=jnp.int32)
         halves = (feed_keep, feed_send, project_keep, project_send)
         halves = lax.psum([half.astype(F32) for half in halves], ("seq", "batch"))

time: 281 us -> 252 us (0.90)
  waiting for transfers between devices: 57.1 us -> 29.5 us
  starting transfers between devices: 46.2 us -> 56.6 us
  local copies, waits for them, and re-layouts: 12.7 us -> 4.56 us
  Pallas kernels: 116 us -> 111 us
    ppermute x28, waiting for transfers between devices: 54.1 us -> 26.7 us  [swap(): return lax.ppermute(value, ('seq', 'batch'), route)]
    ppermute x28, starting transfers between devices: 32 us -> 45.4 us  [swap(): return lax.ppermute(value, ('seq', 'batch'), route)]
    unnamed x38 -> x22, local copies, waits for them, and re-layouts: 8.24 us -> 1.98 us
    pallas_call x4, Pallas kernels: 46.5 us -> 41.8 us  [attend_back(): pl.pallas_call(functools.partial(attend_back_kernel, UNITS * PAIR // lane...]
    all_to_all x3, starting transfers between devices: 14.2 us -> 11.2 us  [to_sequences(): return lax.all_to_all(block, axis, 0, 0, axis_index_groups=groups)]
  transfers between devices with their start and end apart: 31 -> 31, of which waited for: 11 -> 13; matrix products, arithmetic and copies ran while one was open for 6% -> 5% of each run, Pallas kernels for 30% -> 31%
where the time goes in v2:
time: 252 us; the launch traced here: 247 us
  Pallas kernels  111 us (44%)
  starting transfers between devices  56.6 us (22%)
  blocking collectives  33.1 us (13%)
  waiting for transfers between devices  29.5 us (12%)
  other arithmetic  7.82 us (3%)
  local copies, waits for them, and re-layouts  4.56 us (2%)
  matrix products  3.61 us (1%)
    ppermute x28, starting transfers between devices, swap(): return lax.ppermute(value, ('seq', 'batch'), route)  45.4 us
    pallas_call x4, Pallas kernels, attend_back(): pl.pallas_call(functools.partial(attend_back_kernel, UNITS * PAIR // lane...  41.8 us
    all_to_all x1, blocking collectives, to_sequences(): return lax.all_to_all(block, axis, 0, 0, axis_index_groups=groups)  33.1 us
    pallas_call x1, Pallas kernels, feed_forward(): pl.pallas_call(functools.partial(feed_kernel, pieces), grid=(rows // CHUN...  29.6 us
    ppermute x28, waiting for transfers between devices, swap(): return lax.ppermute(value, ('seq', 'batch'), route)  26.7 us
    pallas_call x1, Pallas kernels, attend(): pl.pallas_call(functools.partial(attend_kernel, UNITS * PAIR // lanes, st...  15.7 us
    all_to_all x3, starting transfers between devices, to_sequences(): return lax.all_to_all(block, axis, 0, 0, axis_index_groups=groups)  11.2 us
    pallas_call x2, Pallas kernels, unpack(): pl.pallas_call(functools.partial(unpack_kernel, write, finish), out_shape...  10.9 us
  transfers between devices with their start and end apart: 31, of which 13 were waited for; matrix products, arithmetic and copies ran while one was open for 5% of the time, Pallas kernels for 31%

profile of v2, /device:TPU:0, one launch (start us, length us, event | category | flops | bytes accessed | tf_op | source)
XLA Modules:
  0.0 247.2 jit_solution(10172496398042864403)
XLA Ops:
  0.7 33.1 %all_to_all.20 = bf16[8,128,512]{2,1,0:T(8,128)(2,1)S(1)} all-to-all(bf16[8,128,512]{2,1,0:T(8,128)(2,1)} %param.14), channel_id=1, replica_groups=mesh['seq'=8,'batch'=4] {'seq'}, dimensions={0} | all-to-all | bytes 2097152 | tf_op jit(solution)/shard_map/all_to_all | solution.py:784
  33.7 3.7 %all-to-all-start.1 = ((bf16[8,128,512]{2,1,0:T(8,128)(2,1)}), bf16[8,128,512]{2,1,0:T(8,128)(2,1)S(1)}, u32[]{:S(2)}, u32[]{:S(2)}) async-start(bf16[8,128,512]{2,1,0:T(8,128)(2,1)} %param.15), calls=%async_computation.1 | async-start | bytes 2097152 | tf_op jit(solution)/shard_map/all_to_all | solution.py:784
  41.0 3.6 %convolution_convert_fusion.q_ref.k_ref.v_ref = bf16[1024,1536]{1,0:T(8,128)(2,1)} fusion(bf16[512,1536]{1,0:T(8,128)(2,1)S(1)} %copy-done.5, bf16[1024,512]{1,0:T(8,128)(2,1)S(1)} %bitcast.41, f32[512]{0:T(512)S(1)} %copy-done.7, f32[512]{0:T(512)S(1)} %copy-done.8, f32[1024]{0:T(1024)S(1)} %rsqrt_bitcast_fusion, f32[1024]{0:T(1024)S(1)} %get-tuple-element.141), kind=kOutput, calls=%fused_computation.1 | convolution fusion | flops 1615331328 | bytes 5779456 | tf_op jit(solution)/shard_map/dot_general | solution.py:41
  44.6 15.7 %shard_map.237.att_ref = bf16[1024,512]{1,0:T(8,128)(2,1)} custom-call(s32[2]{0:T(128)} %pad_add_fusion.meta_ref, f32[3,512]{1,0:T(4,128)} %reshape.156.blend_ref, bf16[1024,1536]{1,0:T(8,128)(2,1)} %convolution_convert_fusion.q_ref.k_ref.v_ref, bf16[1024,1536]{1,0:T(8,128)(2,1)} %convolution_convert_fusion.q_ref.k_ref.v_ref, ...), custom_call_target="tpu_custom_call" | custom-call | flops 1000 | bytes 1000 | tf_op jit(solution)/shard_map/pallas_call | solution.py:463
  60.2 2.8 %all-to-all-done.1 = bf16[8,128,512]{2,1,0:T(8,128)(2,1)S(1)} async-done(((bf16[8,128,512]{2,1,0:T(8,128)(2,1)}), bf16[8,128,512]{2,1,0:T(8,128)(2,1)S(1)}, u32[]{:S(2)}, u32[]{:S(2)}) %all-to-all-start.1) | async-done | bytes 1048608 | tf_op jit(solution)/shard_map/all_to_all | solution.py:784
  64.0 29.6 %shard_map.238 = (bf16[1024,512]{1,0:T(8,128)(2,1)}, f32[1024,512]{1,0:T(8,128)}, f32[1024,512]{1,0:T(8,128)}, bf16[256,4608]{1,0:T(8,128)(2,1)}, bf16[256,4608]...) custom-call(s32[1]{0:T(128)} %bitcast.core_ref, bf16[1024,512]{1,0:T(8,128)(2,1)} %bitcast.42, ...), custom_call_target="tpu_custom_call" | custom-call | flops 1000 | bytes 1000 | tf_op jit(solution)/shard_map/pallas_call | solution.py:665
  93.8 10.4 %shard_map.239 = (bf16[1024,128]{1,0:T(8,128)(2,1)}, bf16[1024,128]{1,0:T(8,128)(2,1)}, bf16[1024,128]{1,0:T(8,128)(2,1)}, f32[3,128]{1,0:T(4,128)}) custom-call(s32[2]{0:T(128)} %pad_add_fusion.meta_ref, f32[3,512]{1,0:T(4,128)} %reshape.156.blend_ref, bf16[1024,1536]{1,0:T(8,128)(2,1)} %convolution_convert_fusion.q_ref.k_ref.v_ref, ...), custom_call_target="tpu_custom_call" | custom-call | flops 1000 | bytes 1000 | tf_op jit(solution)/shard_map/pallas_call | solution.py:488
  109.4 3.8 %all-to-all-start.2 = ((bf16[8,128,512]{2,1,0:T(8,128)(2,1)}), bf16[8,128,512]{2,1,0:T(8,128)(2,1)S(1)}, u32[]{:S(2)}, u32[]{:S(2)}) async-start(bf16[8,128,512]{2,1,0:T(8,128)(2,1)} %bitcast.10), calls=%async_computation.2 | async-start | bytes 2097152 | tf_op jit(solution)/shard_map/all_to_all | solution.py:784
  113.1 10.2 %shard_map.240 = (bf16[1024,128]{1,0:T(8,128)(2,1)}, bf16[1024,128]{1,0:T(8,128)(2,1)}, bf16[1024,128]{1,0:T(8,128)(2,1)}, f32[3,128]{1,0:T(4,128)}) custom-call(s32[2]{0:T(128)} %pad_add_fusion.meta_ref, f32[3,512]{1,0:T(4,128)} %reshape.156.blend_ref, bf16[1024,1536]{1,0:T(8,128)(2,1)} %convolution_convert_fusion.q_ref.k_ref.v_ref, ...), custom_call_target="tpu_custom_call" | custom-call | flops 1000 | bytes 1000 | tf_op jit(solution)/shard_map/pallas_call | solution.py:488
  123.4 10.5 %shard_map.241 = (bf16[1024,128]{1,0:T(8,128)(2,1)}, bf16[1024,128]{1,0:T(8,128)(2,1)}, bf16[1024,128]{1,0:T(8,128)(2,1)}, f32[3,128]{1,0:T(4,128)}) custom-call(s32[2]{0:T(128)} %pad_add_fusion.meta_ref, f32[3,512]{1,0:T(4,128)} %reshape.156.blend_ref, bf16[1024,1536]{1,0:T(8,128)(2,1)} %convolution_convert_fusion.q_ref.k_ref.v_ref, ...), custom_call_target="tpu_custom_call" | custom-call | flops 1000 | bytes 1000 | tf_op jit(solution)/shard_map/pallas_call | solution.py:488
  133.9 10.7 %shard_map.243 = (bf16[1024,128]{1,0:T(8,128)(2,1)}, bf16[1024,128]{1,0:T(8,128)(2,1)}, bf16[1024,128]{1,0:T(8,128)(2,1)}, f32[3,128]{1,0:T(4,128)}) custom-call(s32[2]{0:T(128)} %pad_add_fusion.meta_ref, f32[3,512]{1,0:T(4,128)} %reshape.156.blend_ref, bf16[1024,1536]{1,0:T(8,128)(2,1)} %convolution_convert_fusion.q_ref.k_ref.v_ref, ...), custom_call_target="tpu_custom_call" | custom-call | flops 1000 | bytes 1000 | tf_op jit(solution)/shard_map/pallas_call | solution.py:488
  146.2 2.0 collective-permute-start.4
  148.2 2.4 collective-permute-start.5
  151.7 9.4 %shard_map.244 = (bf16[1024,512]{1,0:T(8,128)(2,1)}, bf16[256,1792]{1,0:T(8,128)(2,1)}, bf16[256,1792]{1,0:T(8,128)(2,1)}) custom-call(s32[1]{0:T(128)} %bitcast.core_ref, bf16[1024,512]{1,0:T(8,128)(2,1)} %bitcast.43, f32[1024,512]{1,0:T(8,128)} %get-tuple-element.82.first_ref, bf16[512,1536]{1,0:T(8,128)(2,1)} %w_ref.1, f32[1,512]{1,0:T(1,128)} %bitcast.56, ...), custom_call_target="tpu_custom_call" | custom-call | flops 1000 | bytes 1000 | tf_op jit(solution)/shard_map/pallas_call | solution.py:762
  161.9 3.2 %collective-permute-start.10 = (bf16[1,16,4608]{2,1,0:T(8,128)(2,1)S(1)}, bf16[1,16,4608]{2,1,0:T(8,128)(2,1)S(1)}, u32[]{:S(2)}, u32[]{:S(2)}) collective-permute-start(bf16[1,16,4608]{2,1,0:T(8,128)(2,1)S(1)} %add_convert_fusion.4.refs_0_), channel_id=1, source_target_pairs={{0,24},{1,25},{2,26},{3,27},{4,28},{5,29},{6,30},{7,31},{8,16},{9,... | collective-permute-start | bytes 442376 | tf_op jit(solution)/shard_map/ppermute | solution.py:863
  166.8 1.5 collective-permute-start.11
  170.8 2.6 %collective-permute-start.9 = (bf16[1,16,4608]{2,1,0:T(8,128)(2,1)S(1)}, bf16[1,16,4608]{2,1,0:T(8,128)(2,1)S(1)}, u32[]{:S(2)}, u32[]{:S(2)}) collective-permute-start(bf16[1,16,4608]{2,1,0:T(8,128)(2,1)S(1)} %add_convert_fusion.4.refs_0_), channel_id=1, source_target_pairs={{0,16},{1,17},{2,18},{3,19},{4,20},{5,21},{6,22},{7,23},{8,24},{9,... | collective-permute-start | bytes 442376 | tf_op jit(solution)/shard_map/ppermute | solution.py:863
  173.4 3.7 %all-to-all-start.3 = ((bf16[8,128,512]{2,1,0:T(8,128)(2,1)}), bf16[8,128,512]{2,1,0:T(8,128)(2,1)S(1)}, u32[]{:S(2)}, u32[]{:S(2)}) async-start(bf16[8,128,512]{2,1,0:T(8,128)(2,1)} %bitcast.20), calls=%async_computation.3 | async-start | bytes 2097152 | tf_op jit(solution)/shard_map/all_to_all | solution.py:784
  178.3 1.6 collective-permute-done.9.refs_2_
  182.2 5.0 %collective-permute-start.14 = (bf16[1,16,1792]{2,1,0:T(8,128)(2,1)S(1)}, bf16[1,16,1792]{2,1,0:T(8,128)(2,1)S(1)}, u32[]{:S(2)}, u32[]{:S(2)}) collective-permute-start(bf16[1,16,1792]{2,1,0:T(8,128)(2,1)S(1)} %get-tuple-element.138), channel_id=1, source_target_pairs={{0,8},{1,9},{2,10},{3,11},{4,12},{5,13},{6,14},{7,15},{8,0},{9,1},... | collective-permute-start | bytes 172040 | tf_op jit(solution)/shard_map/ppermute | solution.py:863
  187.2 3.9 %collective-permute-start.15 = (bf16[1,16,1792]{2,1,0:T(8,128)(2,1)S(1)}, bf16[1,16,1792]{2,1,0:T(8,128)(2,1)S(1)}, u32[]{:S(2)}, u32[]{:S(2)}) collective-permute-start(bf16[1,16,1792]{2,1,0:T(8,128)(2,1)S(1)} %get-tuple-element.137), channel_id=1, source_target_pairs={{0,16},{1,17},{2,18},{3,19},{4,20},{5,21},{6,22},{7,23},{8,24},{9,... | collective-permute-start | bytes 172040 | tf_op jit(solution)/shard_map/ppermute | solution.py:863
  191.1 3.0 %collective-permute-start.20 = (bf16[4,16,4608]{2,1,0:T(8,128)(2,1)S(1)}, bf16[4,16,4608]{2,1,0:T(8,128)(2,1)S(1)}, u32[]{:S(2)}, u32[]{:S(2)}) collective-permute-start(bf16[4,16,4608]{2,1,0:T(8,128)(2,1)S(1)} %shard_map.245.refs_0_), channel_id=1, source_target_pairs={{0,4},{1,5},{2,6},{3,7},{4,0},{5,1},{6,2},{7,3},{8,12},{9,13},{10,... | collective-permute-start | bytes 1769480 | tf_op jit(solution)/shard_map/ppermute | solution.py:863
  196.0 2.8 %collective-permute-start.22 = (bf16[4,16,4608]{2,1,0:T(8,128)(2,1)S(1)}, bf16[4,16,4608]{2,1,0:T(8,128)(2,1)}, u32[]{:S(2)}, u32[]{:S(2)}) collective-permute-start(bf16[4,16,4608]{2,1,0:T(8,128)(2,1)S(1)} %shard_map.245.refs_0_), channel_id=1, source_target_pairs={{0,6},{1,7},{2,4},{3,5},{4,2},{5,3},{6,0},{7,1},{8,14},{9,15},{10,... | collective-permute-start | bytes 1769480 | tf_op jit(solution)/shard_map/ppermute | solution.py:863
  198.7 8.1 %collective-permute-done.15 = bf16[1,16,1792]{2,1,0:T(8,128)(2,1)S(1)} collective-permute-done((bf16[1,16,1792]{2,1,0:T(8,128)(2,1)S(1)}, bf16[1,16,1792]{2,1,0:T(8,128)(2,1)S(1)}, u32[]{:S(2)}, u32[]{:S(2)}) %collective-permute-start.15) | collective-permute-done | bytes 57376 | tf_op jit(solution)/shard_map/ppermute | solution.py:863
  208.3 2.8 %collective-permute-start.18 = (bf16[1,16,1792]{2,1,0:T(8,128)(2,1)S(1)}, bf16[1,16,1792]{2,1,0:T(8,128)(2,1)S(1)}, u32[]{:S(2)}, u32[]{:S(2)}) collective-permute-start(bf16[1,16,1792]{2,1,0:T(8,128)(2,1)S(1)} %pad_maximum_fusion.2.refs_0_), channel_id=1, source_target_pairs={{0,16},{1,17},{2,18},{3,19},{4,20},{5,21},{6,22},{7,23},{8,24},{9,... | collective-permute-start | bytes 172040 | tf_op jit(solution)/shard_map/ppermute | solution.py:863
  211.8 3.5 %collective-permute-start.19 = (bf16[1,16,1792]{2,1,0:T(8,128)(2,1)S(1)}, bf16[1,16,1792]{2,1,0:T(8,128)(2,1)S(1)}, u32[]{:S(2)}, u32[]{:S(2)}) collective-permute-start(bf16[1,16,1792]{2,1,0:T(8,128)(2,1)S(1)} %pad_maximum_fusion.2.refs_0_), channel_id=1, source_target_pairs={{0,24},{1,25},{2,26},{3,27},{4,28},{5,29},{6,30},{7,31},{8,16},{9,... | collective-permute-start | bytes 172040 | tf_op jit(solution)/shard_map/ppermute | solution.py:863
  215.3 2.4 collective-permute-done.19.refs_3_
  223.8 4.5 %collective-permute-done.23.refs_1_ = bf16[4,16,1792]{2,1,0:T(8,128)(2,1)S(1)} collective-permute-done((bf16[4,16,1792]{2,1,0:T(8,128)(2,1)S(1)}, bf16[4,16,1792]{2,1,0:T(8,128)(2,1)S(1)}, u32[]{:S(2)}, u32[]{:S(2)}) %collective-permute-start.23) | collective-permute-done | bytes 229408 | tf_op jit(solution)/shard_map/ppermute | solution.py:863
  228.2 1.6 collective-permute-done.24.refs_2_
  229.8 4.5 %collective-permute-done.25.refs_3_ = bf16[4,16,1792]{2,1,0:T(8,128)(2,1)S(1)} collective-permute-done((bf16[4,16,1792]{2,1,0:T(8,128)(2,1)S(1)}, bf16[4,16,1792]{2,1,0:T(8,128)(2,1)S(1)}, u32[]{:S(2)}, u32[]{:S(2)}) %collective-permute-start.25) | collective-permute-done | bytes 229408 | tf_op jit(solution)/shard_map/ppermute | solution.py:863
  235.1 7.2 %shard_map.250 = (f32[512,2048]{1,0:T(8,128)}, f32[512,512]{1,0:T(8,128)}, f32[2048,512]{1,0:T(8,128)}) custom-call(s32[32]{0:T(128)} %fusion.10.order_ref, bf16[16,16,4608]{2,1,0:T(8,128)(2,1)} %copy-done, bf16[16,16,4608]{2,1,0:T(8,128)(2,1)} %collective-permute-done.26.other_ref), custom_call_target="tpu_custom_call" | custom-call | flops 1000 | bytes 1000 | tf_op jit(solution)/shard_map/pallas_call | solution.py:955
  243.2 3.8 %shard_map.251 = (f32[512,1536]{1,0:T(8,128)}, f32[512]{0:T(512)}, f32[512]{0:T(512)}, f32[512]{0:T(512)}, f32[512]{0:T(512)}, /*index=5*/f32[512]{0:T(512)}, f32[2048]{0:T(1024)}, f32[3,8]{1,0:T(4,128)}) custom-call(s32[32]{0:T(128)} %fusion.10.order_ref, bf16[16,16,1792]{2,1,0:T(8,128)(2,1)} %copy-done.1, bf16[16,16,1792]{2,1,0:T(8,128)(2,1)} %copy-done.6), custom_call_target="tpu_custom_call" | custom-call | flops 1000 | bytes 1000 | tf_op jit(solution)/shard_map/pallas_call | solution.py:955
  (97 shorter events, 32.6 us)
Async XLA Ops:
  0.7 37.6 %copy-start.10 = (s32[8]{0:T(128)S(1)}, s32[8]{0:T(128)}, u32[]{:S(2)}) copy-start(s32[8]{0:T(128)} %param.16) | copy-start | bytes 100
  33.7 29.3 %all-to-all-start.1 = ((bf16[8,128,512]{2,1,0:T(8,128)(2,1)}), bf16[8,128,512]{2,1,0:T(8,128)(2,1)S(1)}, u32[]{:S(2)}, u32[]{:S(2)}) async-start(bf16[8,128,512]{2,1,0:T(8,128)(2,1)} %param.15), calls=%async_computation.1 | async-start | bytes 2097152 | tf_op jit(solution)/shard_map/all_to_all | solution.py:784
  93.6 10.5 %collective-permute-start = (bf16[16,16,4608]{2,1,0:T(8,128)(2,1)}, bf16[16,16,4608]{2,1,0:T(8,128)(2,1)S(1)}, u32[]{:S(2)}, u32[]{:S(2)}) collective-permute-start(bf16[16,16,4608]{2,1,0:T(8,128)(2,1)} %bitcast.57), channel_id=1, source_target_pairs={{0,1},{1,0},{2,3},{3,2},{4,5},{5,4},{6,7},{7,6},{8,9},{9,8},{10,11... | collective-permute-start | bytes 7077896 | tf_op jit(solution)/shard_map/ppermute | solution.py:863
  105.9 38.7 %collective-permute-start.1 = (bf16[4,16,4608]{2,1,0:T(8,128)(2,1)}, bf16[4,16,4608]{2,1,0:T(8,128)(2,1)S(1)}, u32[]{:S(2)}, u32[]{:S(2)}) collective-permute-start(bf16[4,16,4608]{2,1,0:T(8,128)(2,1)} %get-tuple-element.122), channel_id=1, source_target_pairs={{0,4},{1,5},{2,6},{3,7},{4,0},{5,1},{6,2},{7,3},{8,12},{9,13},{10,... | collective-permute-start | bytes 1769480 | tf_op jit(solution)/shard_map/ppermute | solution.py:863
  107.1 37.4 %collective-permute-start.2 = (bf16[4,16,4608]{2,1,0:T(8,128)(2,1)S(1)}, bf16[4,16,4608]{2,1,0:T(8,128)(2,1)}, u32[]{:S(2)}, u32[]{:S(2)}) collective-permute-start(bf16[4,16,4608]{2,1,0:T(8,128)(2,1)S(1)} %get-tuple-element.121), channel_id=1, source_target_pairs={{0,2},{1,3},{2,0},{3,1},{4,6},{5,7},{6,4},{7,5},{8,10},{9,11},{10,... | collective-permute-start | bytes 1769480 | tf_op jit(solution)/shard_map/ppermute | solution.py:863
  108.6 36.0 %collective-permute-start.3 = (bf16[4,16,4608]{2,1,0:T(8,128)(2,1)S(1)}, bf16[4,16,4608]{2,1,0:T(8,128)(2,1)}, u32[]{:S(2)}, u32[]{:S(2)}) collective-permute-start(bf16[4,16,4608]{2,1,0:T(8,128)(2,1)S(1)} %get-tuple-element.120), channel_id=1, source_target_pairs={{0,6},{1,7},{2,4},{3,5},{4,2},{5,3},{6,0},{7,1},{8,14},{9,15},{10,... | collective-permute-start | bytes 1769480 | tf_op jit(solution)/shard_map/ppermute | solution.py:863
  109.4 41.3 %all-to-all-start.2 = ((bf16[8,128,512]{2,1,0:T(8,128)(2,1)}), bf16[8,128,512]{2,1,0:T(8,128)(2,1)S(1)}, u32[]{:S(2)}, u32[]{:S(2)}) async-start(bf16[8,128,512]{2,1,0:T(8,128)(2,1)} %bitcast.10), calls=%async_computation.2 | async-start | bytes 2097152 | tf_op jit(solution)/shard_map/all_to_all | solution.py:784
  146.2 15.0 %collective-permute-start.4 = (bf16[1,16,4608]{2,1,0:T(8,128)(2,1)S(1)}, bf16[1,16,4608]{2,1,0:T(8,128)(2,1)S(1)}, u32[]{:S(2)}, u32[]{:S(2)}) collective-permute-start(bf16[1,16,4608]{2,1,0:T(8,128)(2,1)S(1)} %get-tuple-element.132), channel_id=1, source_target_pairs={{0,8},{1,9},{2,10},{3,11},{4,12},{5,13},{6,14},{7,15},{8,0},{9,1},... | collective-permute-start | bytes 442376 | tf_op jit(solution)/shard_map/ppermute | solution.py:863
  148.2 13.6 %collective-permute-start.5 = (bf16[1,16,4608]{2,1,0:T(8,128)(2,1)S(1)}, bf16[1,16,4608]{2,1,0:T(8,128)(2,1)S(1)}, u32[]{:S(2)}, u32[]{:S(2)}) collective-permute-start(bf16[1,16,4608]{2,1,0:T(8,128)(2,1)S(1)} %get-tuple-element.131), channel_id=1, source_target_pairs={{0,16},{1,17},{2,18},{3,19},{4,20},{5,21},{6,22},{7,23},{8,24},{9,... | collective-permute-start | bytes 442376 | tf_op jit(solution)/shard_map/ppermute | solution.py:863
  150.6 11.2 %collective-permute-start.6 = (bf16[1,16,4608]{2,1,0:T(8,128)(2,1)S(1)}, bf16[1,16,4608]{2,1,0:T(8,128)(2,1)S(1)}, u32[]{:S(2)}, u32[]{:S(2)}) collective-permute-start(bf16[1,16,4608]{2,1,0:T(8,128)(2,1)S(1)} %get-tuple-element.130), channel_id=1, source_target_pairs={{0,24},{1,25},{2,26},{3,27},{4,28},{5,29},{6,30},{7,31},{8,16},{9,... | collective-permute-start | bytes 442376 | tf_op jit(solution)/shard_map/ppermute | solution.py:863
  161.0 4.0 %collective-permute-start.7 = (bf16[16,16,1792]{2,1,0:T(8,128)(2,1)}, bf16[16,16,1792]{2,1,0:T(8,128)(2,1)S(1)}, u32[]{:S(2)}, u32[]{:S(2)}) collective-permute-start(bf16[16,16,1792]{2,1,0:T(8,128)(2,1)} %bitcast.58), channel_id=1, source_target_pairs={{0,1},{1,0},{2,3},{3,2},{4,5},{5,4},{6,7},{7,6},{8,9},{9,8},{10,11... | collective-permute-start | bytes 2752520 | tf_op jit(solution)/shard_map/ppermute | solution.py:863
  161.9 8.9 %collective-permute-start.10 = (bf16[1,16,4608]{2,1,0:T(8,128)(2,1)S(1)}, bf16[1,16,4608]{2,1,0:T(8,128)(2,1)S(1)}, u32[]{:S(2)}, u32[]{:S(2)}) collective-permute-start(bf16[1,16,4608]{2,1,0:T(8,128)(2,1)S(1)} %add_convert_fusion.4.refs_0_), channel_id=1, source_target_pairs={{0,24},{1,25},{2,26},{3,27},{4,28},{5,29},{6,30},{7,31},{8,16},{9,... | collective-permute-start | bytes 442376 | tf_op jit(solution)/shard_map/ppermute | solution.py:863
  166.8 13.2 %collective-permute-start.11 = (bf16[4,16,1792]{2,1,0:T(8,128)(2,1)S(1)}, bf16[4,16,1792]{2,1,0:T(8,128)(2,1)S(1)}, u32[]{:S(2)}, u32[]{:S(2)}) collective-permute-start(bf16[4,16,1792]{2,1,0:T(8,128)(2,1)S(1)} %get-tuple-element.128), channel_id=1, source_target_pairs={{0,4},{1,5},{2,6},{3,7},{4,0},{5,1},{6,2},{7,3},{8,12},{9,13},{10,... | collective-permute-start | bytes 688136 | tf_op jit(solution)/shard_map/ppermute | solution.py:863
  168.3 11.7 %collective-permute-start.12 = (bf16[4,16,1792]{2,1,0:T(8,128)(2,1)S(1)}, bf16[4,16,1792]{2,1,0:T(8,128)(2,1)}, u32[]{:S(2)}, u32[]{:S(2)}) collective-permute-start(bf16[4,16,1792]{2,1,0:T(8,128)(2,1)S(1)} %get-tuple-element.127), channel_id=1, source_target_pairs={{0,2},{1,3},{2,0},{3,1},{4,6},{5,7},{6,4},{7,5},{8,10},{9,11},{10,... | collective-permute-start | bytes 688136 | tf_op jit(solution)/shard_map/ppermute | solution.py:863
  169.8 11.2 %collective-permute-start.13 = (bf16[4,16,1792]{2,1,0:T(8,128)(2,1)S(1)}, bf16[4,16,1792]{2,1,0:T(8,128)(2,1)}, u32[]{:S(2)}, u32[]{:S(2)}) collective-permute-start(bf16[4,16,1792]{2,1,0:T(8,128)(2,1)S(1)} %get-tuple-element.126), channel_id=1, source_target_pairs={{0,6},{1,7},{2,4},{3,5},{4,2},{5,3},{6,0},{7,1},{8,14},{9,15},{10,... | collective-permute-start | bytes 688136 | tf_op jit(solution)/shard_map/ppermute | solution.py:863
  170.3 7.9 %collective-permute-start.8 = (bf16[1,16,4608]{2,1,0:T(8,128)(2,1)S(1)}, bf16[1,16,4608]{2,1,0:T(8,128)(2,1)S(1)}, u32[]{:S(2)}, u32[]{:S(2)}) collective-permute-start(bf16[1,16,4608]{2,1,0:T(8,128)(2,1)S(1)} %add_convert_fusion.4.refs_0_), channel_id=1, source_target_pairs={{0,8},{1,9},{2,10},{3,11},{4,12},{5,13},{6,14},{7,15},{8,0},{9,1},... | collective-permute-start | bytes 442376 | tf_op jit(solution)/shard_map/ppermute | solution.py:863
  170.8 9.1 %collective-permute-start.9 = (bf16[1,16,4608]{2,1,0:T(8,128)(2,1)S(1)}, bf16[1,16,4608]{2,1,0:T(8,128)(2,1)S(1)}, u32[]{:S(2)}, u32[]{:S(2)}) collective-permute-start(bf16[1,16,4608]{2,1,0:T(8,128)(2,1)S(1)} %add_convert_fusion.4.refs_0_), channel_id=1, source_target_pairs={{0,16},{1,17},{2,18},{3,19},{4,20},{5,21},{6,22},{7,23},{8,24},{9,... | collective-permute-start | bytes 442376 | tf_op jit(solution)/shard_map/ppermute | solution.py:863
  173.4 44.4 %all-to-all-start.3 = ((bf16[8,128,512]{2,1,0:T(8,128)(2,1)}), bf16[8,128,512]{2,1,0:T(8,128)(2,1)S(1)}, u32[]{:S(2)}, u32[]{:S(2)}) async-start(bf16[8,128,512]{2,1,0:T(8,128)(2,1)} %bitcast.20), calls=%async_computation.3 | async-start | bytes 2097152 | tf_op jit(solution)/shard_map/all_to_all | solution.py:784
  182.2 13.7 %collective-permute-start.14 = (bf16[1,16,1792]{2,1,0:T(8,128)(2,1)S(1)}, bf16[1,16,1792]{2,1,0:T(8,128)(2,1)S(1)}, u32[]{:S(2)}, u32[]{:S(2)}) collective-permute-start(bf16[1,16,1792]{2,1,0:T(8,128)(2,1)S(1)} %get-tuple-element.138), channel_id=1, source_target_pairs={{0,8},{1,9},{2,10},{3,11},{4,12},{5,13},{6,14},{7,15},{8,0},{9,1},... | collective-permute-start | bytes 172040 | tf_op jit(solution)/shard_map/ppermute | solution.py:863
  187.2 19.6 %collective-permute-start.15 = (bf16[1,16,1792]{2,1,0:T(8,128)(2,1)S(1)}, bf16[1,16,1792]{2,1,0:T(8,128)(2,1)S(1)}, u32[]{:S(2)}, u32[]{:S(2)}) collective-permute-start(bf16[1,16,1792]{2,1,0:T(8,128)(2,1)S(1)} %get-tuple-element.137), channel_id=1, source_target_pairs={{0,16},{1,17},{2,18},{3,19},{4,20},{5,21},{6,22},{7,23},{8,24},{9,... | collective-permute-start | bytes 172040 | tf_op jit(solution)/shard_map/ppermute | solution.py:863
  191.1 15.7 %collective-permute-start.16 = (bf16[1,16,1792]{2,1,0:T(8,128)(2,1)S(1)}, bf16[1,16,1792]{2,1,0:T(8,128)(2,1)S(1)}, u32[]{:S(2)}, u32[]{:S(2)}) collective-permute-start(bf16[1,16,1792]{2,1,0:T(8,128)(2,1)S(1)} %get-tuple-element.136), channel_id=1, source_target_pairs={{0,24},{1,25},{2,26},{3,27},{4,28},{5,29},{6,30},{7,31},{8,16},{9,... | collective-permute-start | bytes 172040 | tf_op jit(solution)/shard_map/ppermute | solution.py:863
  191.1 27.8 %collective-permute-start.20 = (bf16[4,16,4608]{2,1,0:T(8,128)(2,1)S(1)}, bf16[4,16,4608]{2,1,0:T(8,128)(2,1)S(1)}, u32[]{:S(2)}, u32[]{:S(2)}) collective-permute-start(bf16[4,16,4608]{2,1,0:T(8,128)(2,1)S(1)} %shard_map.245.refs_0_), channel_id=1, source_target_pairs={{0,4},{1,5},{2,6},{3,7},{4,0},{5,1},{6,2},{7,3},{8,12},{9,13},{10,... | collective-permute-start | bytes 1769480 | tf_op jit(solution)/shard_map/ppermute | solution.py:863
  194.0 24.8 %collective-permute-start.21 = (bf16[4,16,4608]{2,1,0:T(8,128)(2,1)S(1)}, bf16[4,16,4608]{2,1,0:T(8,128)(2,1)S(1)}, u32[]{:S(2)}, u32[]{:S(2)}) collective-permute-start(bf16[4,16,4608]{2,1,0:T(8,128)(2,1)S(1)} %shard_map.245.refs_0_), channel_id=1, source_target_pairs={{0,2},{1,3},{2,0},{3,1},{4,6},{5,7},{6,4},{7,5},{8,10},{9,11},{10,... | collective-permute-start | bytes 1769480 | tf_op jit(solution)/shard_map/ppermute | solution.py:863
  196.0 22.9 %collective-permute-start.22 = (bf16[4,16,4608]{2,1,0:T(8,128)(2,1)S(1)}, bf16[4,16,4608]{2,1,0:T(8,128)(2,1)}, u32[]{:S(2)}, u32[]{:S(2)}) collective-permute-start(bf16[4,16,4608]{2,1,0:T(8,128)(2,1)S(1)} %shard_map.245.refs_0_), channel_id=1, source_target_pairs={{0,6},{1,7},{2,4},{3,5},{4,2},{5,3},{6,0},{7,1},{8,14},{9,15},{10,... | collective-permute-start | bytes 1769480 | tf_op jit(solution)/shard_map/ppermute | solution.py:863
  206.9 4.9 %collective-permute-start.17 = (bf16[1,16,1792]{2,1,0:T(8,128)(2,1)S(1)}, bf16[1,16,1792]{2,1,0:T(8,128)(2,1)S(1)}, u32[]{:S(2)}, u32[]{:S(2)}) collective-permute-start(bf16[1,16,1792]{2,1,0:T(8,128)(2,1)S(1)} %pad_maximum_fusion.2.refs_0_), channel_id=1, source_target_pairs={{0,8},{1,9},{2,10},{3,11},{4,12},{5,13},{6,14},{7,15},{8,0},{9,1},... | collective-permute-start | bytes 172040 | tf_op jit(solution)/shard_map/ppermute | solution.py:863
  208.3 7.0 %collective-permute-start.18 = (bf16[1,16,1792]{2,1,0:T(8,128)(2,1)S(1)}, bf16[1,16,1792]{2,1,0:T(8,128)(2,1)S(1)}, u32[]{:S(2)}, u32[]{:S(2)}) collective-permute-start(bf16[1,16,1792]{2,1,0:T(8,128)(2,1)S(1)} %pad_maximum_fusion.2.refs_0_), channel_id=1, source_target_pairs={{0,16},{1,17},{2,18},{3,19},{4,20},{5,21},{6,22},{7,23},{8,24},{9,... | collective-permute-start | bytes 172040 | tf_op jit(solution)/shard_map/ppermute | solution.py:863
  211.8 6.0 %collective-permute-start.19 = (bf16[1,16,1792]{2,1,0:T(8,128)(2,1)S(1)}, bf16[1,16,1792]{2,1,0:T(8,128)(2,1)S(1)}, u32[]{:S(2)}, u32[]{:S(2)}) collective-permute-start(bf16[1,16,1792]{2,1,0:T(8,128)(2,1)S(1)} %pad_maximum_fusion.2.refs_0_), channel_id=1, source_target_pairs={{0,24},{1,25},{2,26},{3,27},{4,28},{5,29},{6,30},{7,31},{8,16},{9,... | collective-permute-start | bytes 172040 | tf_op jit(solution)/shard_map/ppermute | solution.py:863
  220.1 15.0 %collective-permute-start.26 = (bf16[16,16,4608]{2,1,0:T(8,128)(2,1)S(1)}, bf16[16,16,4608]{2,1,0:T(8,128)(2,1)}, u32[]{:S(2)}, u32[]{:S(2)}) collective-permute-start(bf16[16,16,4608]{2,1,0:T(8,128)(2,1)S(1)} %shard_map.248.own_ref), channel_id=1, source_target_pairs={{0,1},{1,0},{2,3},{3,2},{4,5},{5,4},{6,7},{7,6},{8,9},{9,8},{10,11... | collective-permute-start | bytes 7077896 | tf_op jit(solution)/shard_map/ppermute | solution.py:863
  220.2 8.0 %collective-permute-start.23 = (bf16[4,16,1792]{2,1,0:T(8,128)(2,1)S(1)}, bf16[4,16,1792]{2,1,0:T(8,128)(2,1)S(1)}, u32[]{:S(2)}, u32[]{:S(2)}) collective-permute-start(bf16[4,16,1792]{2,1,0:T(8,128)(2,1)S(1)} %shard_map.246.refs_0_), channel_id=1, source_target_pairs={{0,4},{1,5},{2,6},{3,7},{4,0},{5,1},{6,2},{7,3},{8,12},{9,13},{10,... | collective-permute-start | bytes 688136 | tf_op jit(solution)/shard_map/ppermute | solution.py:863
  221.4 8.4 %collective-permute-start.24 = (bf16[4,16,1792]{2,1,0:T(8,128)(2,1)S(1)}, bf16[4,16,1792]{2,1,0:T(8,128)(2,1)S(1)}, u32[]{:S(2)}, u32[]{:S(2)}) collective-permute-start(bf16[4,16,1792]{2,1,0:T(8,128)(2,1)S(1)} %shard_map.246.refs_0_), channel_id=1, source_target_pairs={{0,2},{1,3},{2,0},{3,1},{4,6},{5,7},{6,4},{7,5},{8,10},{9,11},{10,... | collective-permute-start | bytes 688136 | tf_op jit(solution)/shard_map/ppermute | solution.py:863
  222.9 11.5 %collective-permute-start.25 = (bf16[4,16,1792]{2,1,0:T(8,128)(2,1)S(1)}, bf16[4,16,1792]{2,1,0:T(8,128)(2,1)S(1)}, u32[]{:S(2)}, u32[]{:S(2)}) collective-permute-start(bf16[4,16,1792]{2,1,0:T(8,128)(2,1)S(1)} %shard_map.246.refs_0_), channel_id=1, source_target_pairs={{0,6},{1,7},{2,4},{3,5},{4,2},{5,3},{6,0},{7,1},{8,14},{9,15},{10,... | collective-permute-start | bytes 688136 | tf_op jit(solution)/shard_map/ppermute | solution.py:863
  234.4 7.9 %collective-permute-start.27 = (bf16[16,16,1792]{2,1,0:T(8,128)(2,1)S(1)}, bf16[16,16,1792]{2,1,0:T(8,128)(2,1)S(1)}, u32[]{:S(2)}, u32[]{:S(2)}) collective-permute-start(bf16[16,16,1792]{2,1,0:T(8,128)(2,1)S(1)} %shard_map.249.own_ref), channel_id=1, source_target_pairs={{0,1},{1,0},{2,3},{3,2},{4,5},{5,4},{6,7},{7,6},{8,9},{9,8},{10,11... | collective-permute-start | bytes 2752520 | tf_op jit(solution)/shard_map/ppermute | solution.py:863
  (10 other events, 95.8 us)

commit v3 on v2

--- a/solution.py
+++ b/solution.py
@@ -72,6 +72,20 @@
 
 def tall(block):
     return jnp.concatenate([block[:, :PAIR], block[:, PAIR:]], 0)
+
+
+def width_of(ref):
+    return ref.shape[1]
+
+
+def blend_rows(blend_ref, first):
+    lane = lax.broadcasted_iota(jnp.int32, (1, PAIR), 1)
+
+    def row(branch, pair):
+        head = 2 * (first + pair)
+        return jnp.where(lane < HEAD, blend_ref[branch, head], blend_ref[branch, head + 1])
+
+    return row
 
 
 def fill_features(meta_ref, q_ref, k_ref, v_ref, halo_k, halo_v, keys, values, fq, fk, split):
@@ -146,9 +160,11 @@
 
 
 def attend_kernel(
-    together, whole_sequence, meta_ref, blend_ref, q_ref, k_ref, v_ref, *refs
+    together, whole_sequence, place_ref, lengths_ref, blend_ref, q_ref, k_ref, v_ref, *refs
 ):
     halo_k, halo_v, state_ref = (None,) * 3 if whole_sequence else refs[:3]
+    meta_ref = lengths_ref[place_ref[0]], place_ref[1]
+    blend_at = blend_rows(blend_ref, pl.program_id(0) * (width_of(q_ref) // PAIR))
     att_ref, keys, values, fq, fk, state = refs[-6:] if whole_sequence else refs[3:4] + refs[-5:]
     total_ref = None if whole_sequence else refs[4]
     rows, width = q_ref.shape
@@ -189,10 +205,10 @@
         sums = {u: times(stack[u], wide[u]) for u in units}
         for s, p in units:
             u, lanes = (s, p), pair_lanes(p)
-            mixed = blend_ref[0:1, lanes] * sums[u][:TILE, :PAIR]
+            mixed = blend_at(0, p) * sums[u][:TILE, :PAIR]
             for c in range(2):
                 mine = sums[u][(c + 1) * TILE : (c + 2) * TILE] + old[u][c]
-                mixed = mixed + blend_ref[c + 1 : c + 2, lanes] * (
+                mixed = mixed + blend_at(c + 1, p) * (
                     mine[:, :PAIR] / mine[:, PAIR:]
                 )
             att_ref[here[s], lanes] = mixed.astype(BF16)
@@ -227,8 +243,10 @@
 
 
 def attend_back_kernel(
-    together, whole_sequence, meta_ref, blend_ref, q_ref, k_ref, v_ref, go_ref, *refs
+    together, number, whole_sequence, place_ref, lengths_ref, blend_ref, q_ref, k_ref, v_ref, go_ref, *refs
 ):
+    meta_ref = lengths_ref[place_ref[0]], place_ref[1]
+    blend_at = blend_rows(blend_ref, number * (width_of(q_ref) // PAIR))
     halo_k, halo_v, state_ref, later_ref = (None,) * 4 if whole_sequence else refs[:4]
     if whole_sequence:
         gq_ref, gk_ref, gv_ref, mix_ref = refs[:4]
@@ -253,15 +271,15 @@
     plain_ones = jnp.ones((TILE, PAIR), BF16)
     high = (lax.broadcasted_iota(jnp.int32, (TILE, PAIR), 1) % HEAD) < HEAD // 2
 
-    def step(number, carry):
-        first = number * together
+    def step(turn, carry):
+        first = turn * together
         at = pl.multiple_of(first * TILE, TILE)
         here = [pl.ds(at + s * TILE, TILE) for s in range(together + 1)]
         window = [pl.ds(at + s * TILE, 2 * TILE) for s in near_by]
         masks = [tile_masks(meta_ref, first + s) for s in near_by]
         q = {(s, p): q_ref[here[s], pair_lanes(p)] for s, p in units}
         go = {(s, p): go_ref[here[s], pair_lanes(p)] for s, p in units}
-        blend = [[blend_ref[c : c + 1, pair_lanes(p)] for c in range(3)] for p in pairs]
+        blend = [[blend_at(c, p) for c in range(3)] for p in pairs]
         fqs = {(s, p): [load_split(fq, (c,), here[s], p) for c in range(2)] for s, p in units}
         feats = {u: [whole(f) for f in fqs[u]] for u in units}
         ks = {(s, p): load_split(keys, (), window[s], p) for s, p in units}
@@ -376,8 +394,8 @@
         share = rows_product(whole(load_split(fq, (c,), here, p)), grads)
         return jnp.where(block, share, 0.0)
 
-    def back_step(number, carry):
-        first = tiles - 1 - number * together
+    def back_step(turn, carry):
+        first = tiles - 1 - turn * together
         at = [pl.multiple_of((first - s) * TILE, TILE) for s in near_by]
         here = [pl.ds(a, TILE) for a in at]
         there = [pl.ds(a + TILE, TILE) for a in at]
@@ -431,7 +449,7 @@
     state = pl.BlockSpec(
         (2, lanes // PAIR, PAIR, 2 * PAIR), lambda i: (0, number(i), 0, 0)
     )
-    ins = [pl.BlockSpec(memory_space=pltpu.SMEM), columns(3, 0)]
+    ins = [pl.BlockSpec(memory_space=pltpu.SMEM)] * 3
     ins += [columns(rows, part) for part in range(3)]
     return columns, ins, [columns(TILE, part) for part in range(2)] + [state]
 
@@ -453,7 +471,11 @@
 UNITS = 16
 
 
-def attend(meta, blend, qkv, halo, state):
+def together(rows, lanes):
+    return min(UNITS * PAIR // lanes, rows // TILE)
+
+
+def attend(place, lengths, blend, qkv, halo, state):
     rows, width = qkv.shape[0], qkv.shape[1] // 3
     lanes = PAIR
     columns, ins, before = attention_specs(rows, width, lanes, lambda i: i)
@@ -461,7 +483,7 @@
     share = (2, width // PAIR, PAIR, 2 * PAIR)
     earlier = () if state is None else (halo, halo, state)
     return pl.pallas_call(
-        functools.partial(attend_kernel, UNITS * PAIR // lanes, state is None),
+        functools.partial(attend_kernel, together(rows, lanes), state is None),
         grid=(width // lanes,),
         out_shape=(
             jax.ShapeDtypeStruct((rows, width), BF16),
@@ -472,10 +494,10 @@
         scratch_shapes=attention_scratch(rows, lanes, False),
         compiler_params=pltpu.CompilerParams(vmem_limit_bytes=VMEM),
         cost_estimate=BRIEF,
-    )(meta, blend, qkv, qkv, qkv, *earlier)
-
-
-def attend_back(meta, blend, qkv, halo, state, later, go, calls, number):
+    )(place, lengths, blend, qkv, qkv, qkv, *earlier)
+
+
+def attend_back(place, lengths, blend, qkv, halo, state, later, go, calls, number):
     rows, width = qkv.shape[0], qkv.shape[1] // 3
     lanes = width // calls
     columns, ins, before = attention_specs(rows, width, lanes, lambda i: number)
@@ -486,7 +508,7 @@
         outs += [outcome((2, lanes // PAIR, PAIR, 2 * PAIR), F32)]
     shapes, blocks = zip(*outs)
     return pl.pallas_call(
-        functools.partial(attend_back_kernel, UNITS * PAIR // lanes, state is None),
+        functools.partial(attend_back_kernel, together(rows, lanes), number, state is None),
         grid=(1,),
         out_shape=shapes,
         in_specs=ins + [columns(rows, 0)] + (before + before[-1:])[: len(others)],
@@ -500,7 +522,7 @@
         ],
         compiler_params=pltpu.CompilerParams(vmem_limit_bytes=VMEM),
         cost_estimate=BRIEF,
-    )(meta, blend, qkv, qkv, qkv, go, *others)
+    )(place, lengths, blend, qkv, qkv, qkv, go, *others)
 
 
 CHUNK = 512
@@ -530,25 +552,62 @@
     return jnp.sum(block, axis=0, keepdims=True)
 
 
-def deal(core_ref, rows, lanes, value, keep_ref, send_ref):
+def enter_kernel(place_ref, w_ref, gain_ref, bias_ref, *refs):
+    parts, x_ref, qkv_ref, whole_x = refs[:-3], refs[-3], refs[-2], refs[-1]
+    span, chunk = parts[0].shape[0], x_ref.shape[0]
+
+    @pl.when(pl.program_id(0) == 0)
+    def _():
+        for k, part in enumerate(parts):
+            at = lax.rem(place_ref[0] + len(parts) - k, len(parts)) * span
+            whole_x[pl.ds(pl.multiple_of(at, span), span), :] = part[...]
+
+    x = whole_x[pl.ds(pl.multiple_of(pl.program_id(0) * chunk, chunk), chunk), :]
+    x_ref[...] = x
+    unit, _ = normalized(x.astype(F32))
+    low = (unit * gain_ref[...] + bias_ref[...]).astype(BF16)
+    qkv_ref[...] = times(low, w_ref[...]).astype(BF16)
+
+
+def enter(place, parts, weight, gain, bias):
+    span, width = parts[0].shape
+    rows, lanes = span * len(parts), weight.shape[1]
+    size = min(CHUNK, rows)
+    return pl.pallas_call(
+        enter_kernel,
+        grid=(rows // size,),
+        out_shape=(
+            jax.ShapeDtypeStruct((rows, width), BF16),
+            jax.ShapeDtypeStruct((rows, lanes), BF16),
+        ),
+        in_specs=[pl.BlockSpec(memory_space=pltpu.SMEM)]
+        + [constant(a.shape) for a in (weight, gain[None], bias[None], *parts)],
+        out_specs=(by_rows(size, width), by_rows(size, lanes)),
+        scratch_shapes=[pltpu.VMEM((rows, width), BF16)],
+        compiler_params=pltpu.CompilerParams(vmem_limit_bytes=VMEM),
+        cost_estimate=BRIEF,
+    )(place, weight, gain[None], bias[None], *parts)
+
+
+def deal(place_ref, rows, lanes, value, keep_ref, send_ref):
     half = value.shape[0] // 2
 
-    @pl.when(core_ref[0] == 0)
+    @pl.when(place_ref[2] == 0)
     def _():
         keep_ref[rows, lanes] = value[:half]
         send_ref[rows, lanes] = value[half:]
 
-    @pl.when(core_ref[0] != 0)
+    @pl.when(place_ref[2] != 0)
     def _():
         keep_ref[rows, lanes] = value[half:]
         send_ref[rows, lanes] = value[:half]
 
 
 def feed_kernel(
-    pieces, core_ref, x_ref, att_ref, grad_ref, out_from, gain_ref, bias_ref, in_from, in_b,
-    down_from, down_b, result_ref, first_ref, go_ref, keep_to, send_to, small_ref, wide_ref,
+    pieces, place_ref, x_ref, att_ref, grad_ref, out_from, gain_ref, bias_ref, in_from, in_b,
+    down_from, down_b, result_to, first_to, go_to, keep_to, send_to, small_ref, wide_ref,
     second, hidden, pre_low, att_low, att_all, grad_all, out_w, in_w, down_w, keep_ref, send_ref,
-    in_sems, out_sems,
+    result_ref, first_ref, go_ref, in_sems, out_sems, row_sems,
 ):
     chunk, width = x_ref.shape
     inner = in_w.shape[1]
@@ -597,15 +656,22 @@
         pre_low[here, lanes] = pre
         wide_ref[:, lanes] += column_sum(pre.astype(F32))
         back = back + times_transposed(pre, in_w[:, lanes])
-    result_ref[...] = result.astype(BF16)
+    result_ref[here, :] = result.astype(BF16)
     small_ref[0:1, :] += column_sum(back * unit)
     small_ref[1:2, :] += column_sum(back)
     small_ref[2:3, :] += column_sum(grad_f)
     grad_first = grad_f + norm_back(back * gain_ref[...], unit, scale)
-    first_ref[...] = grad_first
+    first_ref[here, :] = grad_first
     grad_att = grad_first.astype(BF16)
     att_low[here, :] = grad_att
-    go_ref[...] = times_transposed(grad_att, out_w[...])
+    go_ref[here, :] = times_transposed(grad_att, out_w[...])
+    pairs = ((result_ref, result_to), (first_ref, first_to), (go_ref, go_to))
+    done = [
+        pltpu.make_async_copy(inside.at[here, :], outside.at[here, :], row_sems.at[number, i])
+        for i, (inside, outside) in enumerate(pairs)
+    ]
+    for copy in done:
+        copy.start()
 
     @pl.when(number == pl.num_programs(0) - 1)
     def _():
@@ -626,7 +692,7 @@
                 piece, side = divmod(block * each + below, len(tiles))
                 to = slice(after_out + side * width, after_out + (side + 1) * width)
                 rows = slice(piece % (pieces // 2) * flat, (piece % (pieces // 2) + 1) * flat)
-                mine = core_ref[0] == 2 * piece // pieces
+                mine = place_ref[2] == 2 * piece // pieces
                 some = share[below * flat : (below + 1) * flat]
 
                 @pl.when(mine)
@@ -640,13 +706,18 @@
         leave(slice(after_out, after_out + inner))
         for lanes in tiles:
             share = rows_product(second[...], pre_low[:, lanes]).astype(BF16)
-            deal(core_ref, every, lanes, share, keep_ref, send_ref)
+            deal(place_ref, every, lanes, share, keep_ref, send_ref)
             leave(lanes)
         share = rows_product(att_all[...], att_low[...]).astype(BF16)
-        deal(core_ref, every, slice(inner, after_out), share, keep_ref, send_ref)
+        deal(place_ref, every, slice(inner, after_out), share, keep_ref, send_ref)
         leave(slice(inner, after_out))
         for copy in leaving:
             copy.wait()
+        for step in range(att_all.shape[0] // chunk):
+            rows = slice(step * chunk, (step + 1) * chunk)
+            for i, (inside, outside) in enumerate(pairs):
+                sem = row_sems.at[step, i]
+                pltpu.make_async_copy(inside.at[rows, :], outside.at[rows, :], sem).wait()
 
 
 def by_rows(height, width):
@@ -657,14 +728,15 @@
     return pl.BlockSpec(shape, lambda i: (0, 0))
 
 
-def feed_forward(pieces, core, x, att, grad, out_w, gain, bias, in_w, in_b, down_w, down_b):
+def feed_forward(pieces, place, x, att, grad, out_w, gain, bias, in_w, in_b, down_w, down_b):
     rows, width = x.shape
     inner = in_w.shape[1]
     packed = (width // 2, 2 * inner + width)
-    block, far = by_rows(CHUNK, width), pl.BlockSpec(memory_space=pl.ANY)
+    size = min(CHUNK, rows)
+    block, far = by_rows(size, width), pl.BlockSpec(memory_space=pl.ANY)
     return pl.pallas_call(
         functools.partial(feed_kernel, pieces),
-        grid=(rows // CHUNK,),
+        grid=(rows // size,),
         out_shape=(
             jax.ShapeDtypeStruct((rows, width), BF16),
             jax.ShapeDtypeStruct((rows, width), F32),
@@ -678,7 +750,7 @@
         + [block] * 3
         + [far, constant((1, width)), constant((1, width)), far, constant((1, inner)), far]
         + [constant((1, width))],
-        out_specs=(block, block, block, far, far)
+        out_specs=(far,) * 5
         + (constant((3, width)), constant((1, inner))),
         scratch_shapes=[
             pltpu.VMEM((rows, width), BF16),
@@ -692,16 +764,20 @@
             pltpu.VMEM(down_w.shape, BF16),
             pltpu.VMEM(packed, BF16),
             pltpu.VMEM(packed, BF16),
+            pltpu.VMEM((rows, width), BF16),
+            pltpu.VMEM((rows, width), F32),
+            pltpu.VMEM((rows, width), F32),
             pltpu.SemaphoreType.DMA((1 + 2 * inner // width,)),
             pltpu.SemaphoreType.DMA((4 + 2 * inner // width,)),
+            pltpu.SemaphoreType.DMA((rows // size, 3)),
         ],
         compiler_params=pltpu.CompilerParams(vmem_limit_bytes=VMEM),
         cost_estimate=BRIEF,
-    )(core, x, att, grad, out_w, gain[None], bias[None], in_w, in_b[None], down_w, down_b[None])
+    )(place, x, att, grad, out_w, gain[None], bias[None], in_w, in_b[None], down_w, down_b[None])
 
 
 def project_back_kernel(
-    calls, core_ref, x_ref, first_ref, w_ref, gain_ref, bias_ref, small2_ref, wide_ref, *refs
+    calls, place_ref, x_ref, first_ref, w_ref, gain_ref, bias_ref, small2_ref, wide_ref, *refs
 ):
     grads, mixes = refs[: 3 * calls], refs[3 * calls : 4 * calls]
     result_ref, keep_ref, send_ref, normed, gathered, sums, rows_of = refs[4 * calls :]
@@ -747,21 +823,22 @@
         low = (exact - high.astype(F32)).astype(BF16)
         for part, value in enumerate((high, low)):
             lanes = slice(3 * width + part * PAIR, 3 * width + (part + 1) * PAIR)
-            deal(core_ref, every, lanes, value, keep_ref, send_ref)
+            deal(place_ref, every, lanes, value, keep_ref, send_ref)
         for at in range(0, 3 * width, width):
             lanes = slice(at, at + width)
             share = rows_product(normed[...], gathered[:, lanes]).astype(BF16)
-            deal(core_ref, every, lanes, share, keep_ref, send_ref)
-
-
-def project_back(core, x, grad_first, weight, gain, bias, small2, wide, grads, mixes):
+            deal(place_ref, every, lanes, share, keep_ref, send_ref)
+
+
+def project_back(place, x, grad_first, weight, gain, bias, small2, wide, grads, mixes):
     rows, width = x.shape
     calls = len(mixes)
     packed = (width // 2, 3 * width + 2 * PAIR)
-    block, chunk = by_rows(CHUNK, width), by_rows(CHUNK, width // calls)
+    size = min(CHUNK, rows)
+    block, chunk = by_rows(size, width), by_rows(size, width // calls)
     return pl.pallas_call(
         functools.partial(project_back_kernel, calls),
-        grid=(rows // CHUNK,),
+        grid=(rows // size,),
         out_shape=(jax.ShapeDtypeStruct((rows, width), BF16),)
         + (jax.ShapeDtypeStruct(packed, BF16),) * 2,
         in_specs=[pl.BlockSpec(memory_space=pltpu.SMEM), block, block]
@@ -777,34 +854,73 @@
         ],
         compiler_params=pltpu.CompilerParams(vmem_limit_bytes=VMEM),
         cost_estimate=BRIEF,
-    )(core, x, grad_first, weight, gain[None], bias[None], small2, wide, *grads, *mixes)
+    )(place, x, grad_first, weight, gain[None], bias[None], small2, wide, *grads, *mixes)
 
 
 def to_sequences(block, axis, groups):
     return lax.all_to_all(block, axis, 0, 0, axis_index_groups=groups)
 
 
+def spans_of(block, axis, mine):
+    seqs, devices = block.shape[0], lax.axis_size(axis)
+    spans = []
+    for k in range(seqs):
+        span = lax.dynamic_index_in_dim(block, lax.rem(mine + k, seqs), 0, False)
+        route = [(i, i // seqs * seqs + (i + k) % seqs) for i in range(devices)]
+        spans.append(lax.ppermute(span, axis, route) if k else span)
+    return spans
+
+
 def after(value, *others):
     return lax.optimization_barrier((value,) + others)[0]
 
 
-def join_kernel(*refs):
-    out_ref = refs[-1]
-    size = refs[0].shape[0]
-    for k, part in enumerate(refs[:-1]):
-        out_ref[k * size : (k + 1) * size] = part[...]
-
-
-def join(parts):
-    vmem, part = pl.BlockSpec(memory_space=pltpu.VMEM), parts[0]
+def join_kernel(placed, *refs):
+    parts, outs = refs[: len(placed)], refs[len(placed) :]
+    for part, places in zip(parts, placed):
+        for source, out, to, lanes in places:
+            outs[out][to, :, lanes] = part[source]
+
+
+def join_to(parts, placed, shapes):
+    vmem = pl.BlockSpec(memory_space=pltpu.VMEM)
     return pl.pallas_call(
-        join_kernel,
-        out_shape=jax.ShapeDtypeStruct((len(parts) * part.shape[0],) + part.shape[1:], part.dtype),
+        functools.partial(join_kernel, placed),
+        out_shape=[jax.ShapeDtypeStruct(shape, parts[0].dtype) for shape in shapes],
         in_specs=[vmem] * len(parts),
-        out_specs=vmem,
+        out_specs=[vmem] * len(shapes),
         compiler_params=pltpu.CompilerParams(vmem_limit_bytes=16 * 2**20),
         cost_estimate=BRIEF,
     )(*parts)
+
+
+def split_kernel(count, *refs):
+    first, second = refs[count:]
+    size, _, lanes = refs[0].shape
+    for k, part in enumerate(refs[:count]):
+        first[k * size : (k + 1) * size] = part[:, :, : lanes // 2]
+        second[k * size : (k + 1) * size] = part[:, :, lanes // 2 :]
+
+
+def split_to(parts, shapes):
+    vmem = pl.BlockSpec(memory_space=pltpu.VMEM)
+    return pl.pallas_call(
+        functools.partial(split_kernel, len(parts)),
+        out_shape=[jax.ShapeDtypeStruct(shape, parts[0].dtype) for shape in shapes],
+        in_specs=[vmem] * len(parts),
+        out_specs=[vmem] * 2,
+        compiler_params=pltpu.CompilerParams(vmem_limit_bytes=16 * 2**20),
+        cost_estimate=BRIEF,
+    )(*parts)
+
+
+def join(parts):
+    size, height, lanes = parts[0].shape
+    placed = [
+        [(slice(0, size), 0, slice(k * size, (k + 1) * size), slice(0, lanes))]
+        for k in range(len(parts))
+    ]
+    return join_to(parts, placed, [(len(parts) * size, height, lanes)])[0]
 
 
 def settle_kernel(source_ref, out_ref):
@@ -862,14 +978,15 @@
                 route.append((s * self.batch + b, self.device(place)))
         return lax.ppermute(value, ("seq", "batch"), route)
 
-    def scatter(self, value, level, fine=0, beside=()):
+    def slices(self, value, level):
         size, me = self.sizes[level], self.mine()[level]
         value = value.reshape((size, value.shape[0] // size) + value.shape[1:])
-        parts = [
-            self.swap(lax.dynamic_index_in_dim(value, me ^ k, 0, False), level, k)
-            for k in range(1, size)
-        ]
-        return self.add(lax.dynamic_index_in_dim(value, me, 0, False), parts, fine, beside)
+        return [lax.dynamic_index_in_dim(value, me ^ k, 0, False) for k in range(size)]
+
+    def scatter(self, value, level, fine=0, beside=()):
+        slices = value if isinstance(value, list) else self.slices(value, level)
+        parts = [self.swap(part, level, k) for k, part in enumerate(slices) if k]
+        return self.add(slices[0], parts, fine, beside)
 
     def scatter_cores(self, keep, send, fine=0, beside=()):
         return self.add(self.to_pieces(keep), [self.swap(self.to_pieces(send), "core", 1)], fine, beside)
@@ -892,19 +1009,37 @@
     def to_pieces(self, value):
         return value.reshape(self.pieces // 2, -1, value.shape[1])
 
-    def order(self):
+    def gather_split(self, value, level, beside=()):
+        parts = [after(value, *beside)]
+        parts += [self.swap(value, level, k) for k in range(1, self.sizes[level])]
+        size, height, lanes = value.shape
+        shape = (len(parts) * size, height, lanes // 2)
+        return split_to(parts, [shape, shape])
+
+    def join_ways(self, halves, ways):
+        size, height, half = halves[0].shape
+        size //= 2
+        placed = []
+        for out_lanes, order in ((0, (0, 2)), (0, (1, 3)), (half, (0, 1)), (half, (2, 3))):
+            lanes = slice(out_lanes, out_lanes + half)
+            placed.append(
+                [
+                    (slice(i * size, (i + 1) * size), 0, slice(k * size, (k + 1) * size), lanes)
+                    for i, k in enumerate(order)
+                ]
+            )
+        parts = [halves[0], ways[0], halves[1], ways[1]]
+        return join_to(parts, placed, [(4 * size, height, 2 * half)])[0]
+
+    def code(self):
         me = self.mine()
-        piece = jnp.arange(self.pieces, dtype=jnp.int32)
-        far, near = self.sizes["far"], self.sizes["near"]
-        core = (piece // (far * near)) ^ me["core"]
-        near = ((piece // far) % near) ^ me["near"]
-        return (core * self.sizes["near"] + near) * far + ((piece % far) ^ me["far"])
-
-
-def unpack_kernel(write, finish, order_ref, own_ref, other_ref, *out_refs):
+        return (me["core"] * self.sizes["near"] + me["near"]) * self.sizes["far"] + me["far"]
+
+
+def unpack_kernel(write, finish, place_ref, own_ref, other_ref, *out_refs):
     half = own_ref.shape[0]
     for piece in range(2 * half):
-        at = order_ref[piece]
+        at = place_ref[3] ^ piece
 
         @pl.when(at < half)
         def _(piece=piece, at=at):
@@ -950,7 +1085,7 @@
     blend[...] = small[at : at + 3, : blend.shape[1]]
 
 
-def unpack(write, order, halves, shapes, finish=lambda refs: None, scratch=()):
+def unpack(write, place, halves, shapes, finish=lambda refs: None, scratch=()):
     vmem = pl.BlockSpec(memory_space=pltpu.VMEM)
     return pl.pallas_call(
         functools.partial(unpack_kernel, write, finish),
@@ -958,9 +1093,9 @@
         in_specs=[pl.BlockSpec(memory_space=pltpu.SMEM), vmem, vmem],
         out_specs=[vmem] * len(shapes),
         scratch_shapes=scratch,
-        compiler_params=pltpu.CompilerParams(vmem_limit_bytes=VMEM),
+        compiler_params=pltpu.CompilerParams(vmem_limit_bytes=24 * 2**20),
         cost_estimate=BRIEF,
-    )(order, *halves)
+    )(place, *halves)
 
 
 def local(
@@ -989,49 +1124,49 @@
     if parts > 1:
         groups = [[r * seqs + s for s in range(seqs)] for r in range(parts)]
     mine, part = index % seqs, index // seqs
-    meta = jnp.stack([lax.dynamic_index_in_dim(lengths, mine, 0, False), part * rows])
-    blend = jnp.repeat(blend_weights, width // heads, axis=1)
-
     ring = Ring(lax.axis_size("batch"), devices)
     by_ring = width % (16 * ring.pieces) == 0
     inner = in_weight.shape[1]
-
-    x = to_sequences(inputs, "seq", groups).reshape(rows, width)
-    grad_out = to_sequences(cotangent, "seq", groups).reshape(rows, width)
-
-    normed = layer_norm(x.astype(F32), norm1_gain, norm1_bias).astype(BF16)
-    qkv = times(normed, qkv_weight).astype(BF16)
+    numbers = [mine, part * rows, 0, 0]
+    if by_ring:
+        numbers[2:] = [lax.axis_index("batch") % 2, ring.code()]
+    place = jnp.stack([jnp.asarray(number, jnp.int32) for number in numbers])
+
+    spans = spans_of(inputs, "seq", mine)
+    x, qkv = enter(place, spans, qkv_weight, norm1_gain, norm1_bias)
+    grad_out = to_sequences(after(cotangent, *spans), "seq", groups).reshape(rows, width)
     halo = state = later = None
     if parts > 1:
         state = later = jnp.zeros((2, width // PAIR, PAIR, 2 * PAIR), F32)
         onward = [(i, i + seqs) for i in range(devices - seqs)]
         halo = lax.ppermute(qkv[rows - TILE :, width:], "seq", onward)
-        total = attend(meta, blend, qkv, halo, state)[1]
+        total = attend(place, lengths, blend_weights, qkv, halo, state)[1]
         state = from_parts(total, "seq", parts, seqs, True)
-    attended = attend(meta, blend, qkv, halo, state)[0]
-
-    core = (lax.axis_index("batch") % 2)[None] if by_ring else jnp.zeros(1, jnp.int32)
+    attended = attend(place, lengths, blend_weights, qkv, halo, state)[0]
+
     result, grad_first, grad_o, feed_keep, feed_send, small2, grad_in_b = feed_forward(
         ring.pieces if by_ring else 16,
-        core, x, attended, grad_out, out_weight, norm2_gain, norm2_bias,
+        place, x, attended, grad_out, out_weight, norm2_gain, norm2_bias,
         in_weight, in_bias, down_weight, down_bias,
     )
-    output = to_sequences(result.reshape(seqs, span, width), "seq", groups)
-    def unpack_feed(order, halves):
-        shapes = [(width, inner), (width, width), (inner, width)]
-        return unpack(write_feed, order, halves, shapes)
-
+
+    def move(rows):
+        return to_sequences(rows.reshape(seqs, span, width), "seq", groups)
+
+    feed_shapes = [(width, inner), (width, width), (inner, width)]
     calls = 4
 
-    def back(meta, number, later):
-        return attend_back(meta, blend, qkv, halo, state, later, grad_o, calls, number)
+    def back(place, number, later):
+        return attend_back(
+            place, lengths, blend_weights, qkv, halo, state, later, grad_o, calls, number
+        )
 
     if parts > 1:
-        total = jnp.concatenate([back(meta, number, later)[6] for number in range(calls)], 1)
+        total = jnp.concatenate([back(place, number, later)[6] for number in range(calls)], 1)
         later = from_parts(total, "seq", parts, seqs, False)
-    backs, turn = [], meta
+    backs, turn = [], place
     if by_ring:
-        held = None
+        held, output = None, move(result)
         for number in range(calls):
             if number == 1:
                 held = ring.scatter_cores(feed_keep, feed_send, 0, (backs[0][3],))
@@ -1042,7 +1177,8 @@
         output = settle(after(output, backs[2][3]))
         grad_first = after(grad_first, held, output)
     else:
-        backs = [back(meta, number, later) for number in range(calls)]
+        backs = [back(place, number, later) for number in range(calls)]
+        output = move(result)
     grads = [[call[part] for call in backs] for part in range(3)]
     if parts > 1:
         homeward = [(i + seqs, i) for i in range(devices - seqs)]
@@ -1054,44 +1190,41 @@
                 grads[part][number] = grad.at[rows - TILE :].set(tail.astype(BF16))
     grads = grads[0] + grads[1] + grads[2]
     grad_x, project_keep, project_send = project_back(
-        core, x, grad_first, qkv_weight, norm1_gain, norm1_bias, small2, grad_in_b, grads,
+        place, x, grad_first, qkv_weight, norm1_gain, norm1_bias, small2, grad_in_b, grads,
         [call[3] for call in backs],
     )
 
-    def move(grad_x):
-        return to_sequences(grad_x.reshape(seqs, span, width), "seq", groups)
-
     if by_ring:
-        order = ring.order()
         held = ring.scatter(held, "far", 0, (project_keep,))
         late = ring.scatter_cores(project_keep, project_send, PAIR, (held,))
-        held = ring.gather(held, "far")
+        late = ring.slices(late, "near")
+        halves = ring.gather_split(held, "far", late)
+        ways = [ring.swap(half, "near", k) for half, k in zip(halves, (2, 1))]
+        late = ring.scatter(late, "near", PAIR)
+        halves = [join([half, way]) for half, way in zip(halves, ways)]
+        ways = [ring.swap(half, "near", k) for half, k in zip(halves, (1, 2))]
+        late = ring.scatter(late, "far", PAIR, halves)
+        late = ring.gather(late, "far")
         moved = move(after(grad_x, late))
-        near = [ring.swap(held, "near", k) for k in range(1, ring.sizes["near"])]
-        late = ring.scatter(late, "near", PAIR, (held,))
-        late = ring.scatter(late, "far", PAIR)
-        late = ring.gather(late, "far")
-        last = [ring.swap(late, "near", k) for k in range(1, ring.sizes["near"])]
+        held = ring.join_ways([after(halves[0], late), halves[1]], ways)
+        other = ring.swap(held, "core", 1)
+        feed_grads = unpack(write_feed, place, (held, other), feed_shapes)
+        late = ring.gather(late, "near", feed_grads)
         input_grad = settle(after(moved, late))
-        held = join([after(held, late, input_grad)] + near)
-        other = ring.swap(held, "core", 1)
-        late = join([after(late, held)] + last)
-        rest = ring.swap(late, "core", 1)
-        grad_in_w, grad_out_w, grad_down_w = unpack_feed(order, (held, after(other, late)))
-        project_halves = after(late, grad_out_w), rest
+        halves = after(late, input_grad), ring.swap(late, "core", 1)
     else:
         input_grad = move(grad_x)
-        order = jnp.arange(16, dtype=jnp.int32)
         halves = (feed_keep, feed_send, project_keep, project_send)
         halves = lax.psum([half.astype(F32) for half in halves], ("seq", "batch"))
         halves = [half.reshape(8, width // 16, -1) for half in halves]
-        feed_halves, project_halves = halves[:2], halves[2:]
-        grad_in_w, grad_out_w, grad_down_w = unpack_feed(order, feed_halves)
+        feed_grads = unpack(write_feed, place, halves[:2], feed_shapes)
+        halves = halves[2:]
+    grad_in_w, grad_out_w, grad_down_w = feed_grads
     vectors = [(width,)] * 5 + [(inner,)]
     lines = sum(size for (size,) in vectors) // PAIR + 3
-    lines += -lines % (width // order.shape[0])
+    lines += -lines % (width // (2 * halves[0].shape[0]))
     grad_qkv_w, gain1, bias1, gain2, bias2, grad_down_b, grad_in_b, grad_blend = unpack(
-        write_project, order, project_halves, [(width, 3 * width)] + vectors + [(3, heads)],
+        write_project, place, halves, [(width, 3 * width)] + vectors + [(3, heads)],
         finish_project, [pltpu.VMEM((lines, PAIR), F32)],
     )
     return (

time: 252 us -> 246 us (0.976)
  blocking collectives: 33.1 us -> 0 us
  starting transfers between devices: 56.6 us -> 73.7 us
  waiting for transfers between devices: 29.5 us -> 43.9 us
  matrix products: 3.61 us -> 0 us
  other arithmetic: 7.82 us -> 4.65 us
    all_to_all x1 -> x0, blocking collectives: 33.1 us -> none  [to_sequences(): return lax.all_to_all(block, axis, 0, 0, axis_index_groups=groups)]
    ppermute x0 -> x7, starting transfers between devices: none -> 14.4 us  [spans_of(): spans.append(lax.ppermute(span, axis, route) if k else span)]
    all_to_all x3, starting transfers between devices: 11.2 us -> 23.4 us  [to_sequences(): return lax.all_to_all(block, axis, 0, 0, axis_index_groups=groups)]
    ppermute x28 -> x29, starting transfers between devices: 45.4 us -> 35.9 us  [swap(): return lax.ppermute(value, ('seq', 'batch'), route)]
    ppermute x0 -> x7, waiting for transfers between devices: none -> 6.84 us  [spans_of(): spans.append(lax.ppermute(span, axis, route) if k else span)]
    ppermute x28 -> x29, waiting for transfers between devices: 26.7 us -> 31.8 us  [swap(): return lax.ppermute(value, ('seq', 'batch'), route)]
    pallas_call x10 -> x13, Pallas kernels: 88.4 us -> 92.2 us  [the longest x4 41.8 us: attend_back(): pl.pallas_call(functools.partial(attend_back_kernel, together(rows, lanes...]
    dot_general x1 -> x0, matrix products: 3.61 us -> none  [times(): lax.dot_general(left, right, (((1,), (0,)), ((), ())), preferred_element_...]
  transfers between devices with their start and end apart: 31 -> 39, of which waited for: 13 -> 12; matrix products, arithmetic and copies ran while one was open for 5% -> 2% of each run, Pallas kernels for 31% -> 34%
where the time goes in v3:
time: 246 us; the launch traced here: 242 us
  Pallas kernels  113 us (46%)
  starting transfers between devices  73.7 us (30%)
  waiting for transfers between devices  43.9 us (18%)
  local copies, waits for them, and re-layouts  4.99 us (2%)
  other arithmetic  4.65 us (2%)
    pallas_call x4, Pallas kernels, attend_back(): pl.pallas_call(functools.partial(attend_back_kernel, together(rows, lanes...  41.8 us
    ppermute x29, starting transfers between devices, swap(): return lax.ppermute(value, ('seq', 'batch'), route)  35.9 us
    ppermute x29, waiting for transfers between devices, swap(): return lax.ppermute(value, ('seq', 'batch'), route)  31.8 us
    pallas_call x1, Pallas kernels, feed_forward(): pl.pallas_call(functools.partial(feed_kernel, pieces), grid=(rows // size...  28.7 us
    all_to_all x3, starting transfers between devices, to_sequences(): return lax.all_to_all(block, axis, 0, 0, axis_index_groups=groups)  23.4 us
    pallas_call x1, Pallas kernels, attend(): pl.pallas_call(functools.partial(attend_kernel, together(rows, lanes), st...  15.7 us
    ppermute x7, starting transfers between devices, spans_of(): spans.append(lax.ppermute(span, axis, route) if k else span)  14.4 us
    pallas_call x1, Pallas kernels, project_back(): pl.pallas_call(functools.partial(project_back_kernel, calls), grid=(rows...  9.52 us
  transfers between devices with their start and end apart: 39, of which 12 were waited for; matrix products, arithmetic and copies ran while one was open for 2% of the time, Pallas kernels for 34%

profile of v3, /device:TPU:0, one launch (start us, length us, event | category | flops | bytes accessed | tf_op | source)
XLA Modules:
  0.0 241.7 jit_solution(13385073214649198444)
XLA Ops:
  0.8 2.0 dynamic-slice_bitcast_fusion.8
  2.8 3.0 %collective-permute-start = (bf16[128,512]{1,0:T(8,128)(2,1)S(1)}, bf16[128,512]{1,0:T(8,128)(2,1)S(1)}, u32[]{:S(2)}, u32[]{:S(2)}) collective-permute-start(bf16[128,512]{1,0:T(8,128)(2,1)S(1)} %get-tuple-element.142), channel_id=1, source_target_pairs={{0,4},{4,8},{8,12},{12,16},{16,20},{20,24},{24,28},{28,0},{1,5},{5... | collective-permute-start | bytes 393224 | tf_op jit(solution)/shard_map/ppermute | solution.py:870
  7.3 2.5 %collective-permute-start.2 = (bf16[128,512]{1,0:T(8,128)(2,1)S(1)}, bf16[128,512]{1,0:T(8,128)(2,1)S(1)}, u32[]{:S(2)}, u32[]{:S(2)}) collective-permute-start(bf16[128,512]{1,0:T(8,128)(2,1)S(1)} %get-tuple-element.140), channel_id=1, source_target_pairs={{0,12},{4,16},{8,20},{12,24},{16,28},{20,0},{24,4},{28,8},{1,13},{... | collective-permute-start | bytes 393224 | tf_op jit(solution)/shard_map/ppermute | solution.py:870
  11.1 2.6 %collective-permute-start.4 = (bf16[128,512]{1,0:T(8,128)(2,1)S(1)}, bf16[128,512]{1,0:T(8,128)(2,1)S(1)}, u32[]{:S(2)}, u32[]{:S(2)}) collective-permute-start(bf16[128,512]{1,0:T(8,128)(2,1)S(1)} %get-tuple-element.138), channel_id=1, source_target_pairs={{0,20},{4,24},{8,28},{12,0},{16,4},{20,8},{24,12},{28,16},{1,21},{... | collective-permute-start | bytes 393224 | tf_op jit(solution)/shard_map/ppermute | solution.py:870
  15.1 2.0 collective-permute-start.6
  17.2 6.5 %collective-permute-done.2.refs_3_ = bf16[128,512]{1,0:T(8,128)(2,1)S(1)} collective-permute-done((bf16[128,512]{1,0:T(8,128)(2,1)S(1)}, bf16[128,512]{1,0:T(8,128)(2,1)S(1)}, u32[]{:S(2)}, u32[]{:S(2)}) %collective-permute-start.2) | collective-permute-done | bytes 131104 | tf_op jit(solution)/shard_map/ppermute | solution.py:870
  24.0 12.0 %all-to-all-start = ((bf16[8,128,512]{2,1,0:T(8,128)(2,1)}), bf16[8,128,512]{2,1,0:T(8,128)(2,1)S(1)}, u32[]{:S(2)}, u32[]{:S(2)}) async-start(bf16[8,128,512]{2,1,0:T(8,128)(2,1)} %param.15), calls=%async_computation | async-start | bytes 2097152 | tf_op jit(solution)/shard_map/all_to_all | solution.py:861
  36.7 5.6 %shard_map.237 = (bf16[1024,512]{1,0:T(8,128)(2,1)}, bf16[1024,1536]{1,0:T(8,128)(2,1)}) custom-call(s32[4]{0:T(128)} %pad_add_fusion.place_ref, bf16[512,1536]{1,0:T(8,128)(2,1)} %w_ref.3, f32[1,512]{1,0:T(1,128)} %bitcast.62, f32[1,512]{1,0:T(1,128)} %bitcast.64, bf16[128,512]{1,0:T(8,128)(2,1)} %get-tuple-element.143.refs_0_, bf16[128,512]{1,0:T(8,128)(2,1)} %copy-done.5, ...), custom_call_target="tpu_custom_call" | custom-call | flops 1000 | bytes 1000 | tf_op jit(solution)/shard_map/pallas_call | solution.py:576
  42.3 15.7 %shard_map.238.att_ref = bf16[1024,512]{1,0:T(8,128)(2,1)} custom-call(s32[4]{0:T(128)} %pad_add_fusion.place_ref, s32[8]{0:T(128)} %lengths_ref.9, f32[3,8]{1,0:T(4,128)} %blend_ref.9, bf16[1024,1536]{1,0:T(8,128)(2,1)} %get-tuple-element.73.q_ref.k_ref.v_ref, bf16[1024,1536]{1,0:T(8,128)(2,1)} %get-tuple-element.73.q_ref.k_ref.v_ref, ...), custom_call_target="tpu_custom_call" | custom-call | flops 1000 | bytes 1000 | tf_op jit(solution)/shard_map/pallas_call | solution.py:485
  58.0 3.1 %all-to-all-done = bf16[8,128,512]{2,1,0:T(8,128)(2,1)S(1)} async-done(((bf16[8,128,512]{2,1,0:T(8,128)(2,1)}), bf16[8,128,512]{2,1,0:T(8,128)(2,1)S(1)}, u32[]{:S(2)}, u32[]{:S(2)}) %all-to-all-start) | async-done | bytes 1048608 | tf_op jit(solution)/shard_map/all_to_all | solution.py:861
  62.1 28.7 %shard_map.239 = (bf16[1024,512]{1,0:T(8,128)(2,1)}, f32[1024,512]{1,0:T(8,128)}, f32[1024,512]{1,0:T(8,128)}, bf16[256,4608]{1,0:T(8,128)(2,1)}, bf16[256,4608]...) custom-call(s32[4]{0:T(128)} %pad_add_fusion.place_ref, bf16[1024,512]{1,0:T(8,128)(2,1)} %get-tuple-element.72.x_ref, ...), custom_call_target="tpu_custom_call" | custom-call | flops 1000 | bytes 1000 | tf_op jit(solution)/shard_map/pallas_call | solution.py:737
  91.0 10.4 %shard_map.240 = (bf16[1024,128]{1,0:T(8,128)(2,1)}, bf16[1024,128]{1,0:T(8,128)(2,1)}, bf16[1024,128]{1,0:T(8,128)(2,1)}, f32[3,128]{1,0:T(4,128)}) custom-call(s32[4]{0:T(128)} %pad_add_fusion.place_ref, s32[8]{0:T(128)} %lengths_ref.9, f32[3,8]{1,0:T(4,128)} %blend_ref.9, bf16[1024,1536]{1,0:T(8,128)(2,1)} %get-tuple-element.73.q_ref.k_ref.v_ref, ...), custom_call_target="tpu_custom_call" | custom-call | flops 1000 | bytes 1000 | tf_op jit(solution)/shard_map/pallas_call | solution.py:510
  103.1 2.1 collective-permute-start.10
  106.6 3.8 %all-to-all-start.1 = ((bf16[8,128,512]{2,1,0:T(8,128)(2,1)}), bf16[8,128,512]{2,1,0:T(8,128)(2,1)S(1)}, u32[]{:S(2)}, u32[]{:S(2)}) async-start(bf16[8,128,512]{2,1,0:T(8,128)(2,1)} %bitcast.19), calls=%async_computation.1 | async-start | bytes 2097152 | tf_op jit(solution)/shard_map/all_to_all | solution.py:861
  110.4 10.2 %shard_map.241 = (bf16[1024,128]{1,0:T(8,128)(2,1)}, bf16[1024,128]{1,0:T(8,128)(2,1)}, bf16[1024,128]{1,0:T(8,128)(2,1)}, f32[3,128]{1,0:T(4,128)}) custom-call(s32[4]{0:T(128)} %pad_add_fusion.place_ref, s32[8]{0:T(128)} %lengths_ref.9, f32[3,8]{1,0:T(4,128)} %blend_ref.9, bf16[1024,1536]{1,0:T(8,128)(2,1)} %get-tuple-element.73.q_ref.k_ref.v_ref, ...), custom_call_target="tpu_custom_call" | custom-call | flops 1000 | bytes 1000 | tf_op jit(solution)/shard_map/pallas_call | solution.py:510
  120.6 10.5 %shard_map.242 = (bf16[1024,128]{1,0:T(8,128)(2,1)}, bf16[1024,128]{1,0:T(8,128)(2,1)}, bf16[1024,128]{1,0:T(8,128)(2,1)}, f32[3,128]{1,0:T(4,128)}) custom-call(s32[4]{0:T(128)} %pad_add_fusion.place_ref, s32[8]{0:T(128)} %lengths_ref.9, f32[3,8]{1,0:T(4,128)} %blend_ref.9, bf16[1024,1536]{1,0:T(8,128)(2,1)} %get-tuple-element.73.q_ref.k_ref.v_ref, ...), custom_call_target="tpu_custom_call" | custom-call | flops 1000 | bytes 1000 | tf_op jit(solution)/shard_map/pallas_call | solution.py:510
  131.1 10.7 %shard_map.244 = (bf16[1024,128]{1,0:T(8,128)(2,1)}, bf16[1024,128]{1,0:T(8,128)(2,1)}, bf16[1024,128]{1,0:T(8,128)(2,1)}, f32[3,128]{1,0:T(4,128)}) custom-call(s32[4]{0:T(128)} %pad_add_fusion.place_ref, s32[8]{0:T(128)} %lengths_ref.9, f32[3,8]{1,0:T(4,128)} %blend_ref.9, bf16[1024,1536]{1,0:T(8,128)(2,1)} %get-tuple-element.73.q_ref.k_ref.v_ref, ...), custom_call_target="tpu_custom_call" | custom-call | flops 1000 | bytes 1000 | tf_op jit(solution)/shard_map/pallas_call | solution.py:510
  143.4 2.0 collective-permute-start.11
  145.4 2.4 collective-permute-start.12
  148.9 9.5 %shard_map.245 = (bf16[1024,512]{1,0:T(8,128)(2,1)}, bf16[256,1792]{1,0:T(8,128)(2,1)}, bf16[256,1792]{1,0:T(8,128)(2,1)}) custom-call(s32[4]{0:T(128)} %pad_add_fusion.place_ref, bf16[1024,512]{1,0:T(8,128)(2,1)} %get-tuple-element.72.x_ref, f32[1024,512]{1,0:T(8,128)} %get-tuple-element.91.first_ref, bf16[512,1536]{1,0:T(8,128)(2,1)} %w_ref.3, ...), custom_call_target="tpu_custom_call" | custom-call | flops 1000 | bytes 1000 | tf_op jit(solution)/shard_map/pallas_call | solution.py:839
  159.1 2.2 collective-permute-start.18
  170.2 9.8 %collective-permute-done.19.refs_2_ = bf16[1,16,4608]{2,1,0:T(8,128)(2,1)S(1)} collective-permute-done((bf16[1,16,4608]{2,1,0:T(8,128)(2,1)S(1)}, bf16[1,16,4608]{2,1,0:T(8,128)(2,1)S(1)}, u32[]{:S(2)}, u32[]{:S(2)}) %collective-permute-start.19) | collective-permute-done | bytes 147488 | tf_op jit(solution)/shard_map/ppermute | solution.py:979
  183.3 3.0 %collective-permute-start.23 = (bf16[1,16,1792]{2,1,0:T(8,128)(2,1)S(1)}, bf16[1,16,1792]{2,1,0:T(8,128)(2,1)S(1)}, u32[]{:S(2)}, u32[]{:S(2)}) collective-permute-start(bf16[1,16,1792]{2,1,0:T(8,128)(2,1)S(1)} %get-tuple-element.158), channel_id=1, source_target_pairs={{0,8},{1,9},{2,10},{3,11},{4,12},{5,13},{6,14},{7,15},{8,0},{9,1},... | collective-permute-start | bytes 172040 | tf_op jit(solution)/shard_map/ppermute | solution.py:979
  190.7 2.0 collective-permute-done.24
  197.9 2.3 collective-permute-done.27.refs_2_
  200.3 2.1 collective-permute-done.28.refs_3_
  203.5 7.6 %all-to-all-start.2 = ((bf16[8,128,512]{2,1,0:T(8,128)(2,1)}), bf16[8,128,512]{2,1,0:T(8,128)(2,1)S(1)}, u32[]{:S(2)}, u32[]{:S(2)}) async-start(bf16[8,128,512]{2,1,0:T(8,128)(2,1)} %bitcast.57), calls=%async_computation.2 | async-start | bytes 2097152 | tf_op jit(solution)/shard_map/all_to_all | solution.py:861
  211.2 2.0 collective-permute-start.32
  214.7 6.5 %shard_map.251 = (f32[512,2048]{1,0:T(8,128)}, f32[512,512]{1,0:T(8,128)}, f32[2048,512]{1,0:T(8,128)}) custom-call(s32[4]{0:T(128)S(1)} %copy-done.2, bf16[16,16,4608]{2,1,0:T(8,128)(2,1)S(1)} %shard_map.250.own_ref, bf16[16,16,4608]{2,1,0:T(8,128)(2,1)} %collective-permute-done.31.other_ref), custom_call_target="tpu_custom_call" | custom-call | flops 1000 | bytes 1000 | tf_op jit(solution)/shard_map/pallas_call | solution.py:1090
  221.2 14.0 %collective-permute-done.32.refs_1_ = bf16[4,16,1792]{2,1,0:T(8,128)(2,1)S(1)} collective-permute-done((bf16[4,16,1792]{2,1,0:T(8,128)(2,1)}, bf16[4,16,1792]{2,1,0:T(8,128)(2,1)S(1)}, u32[]{:S(2)}, u32[]{:S(2)}) %collective-permute-start.32) | collective-permute-done | bytes 229408 | tf_op jit(solution)/shard_map/ppermute | solution.py:979
  235.4 2.2 all-to-all-done.2.source_ref
  238.6 2.9 %shard_map.254 = (f32[512,1536]{1,0:T(8,128)}, f32[512]{0:T(512)}, f32[512]{0:T(512)}, f32[512]{0:T(512)}, f32[512]{0:T(512)}, /*index=5*/f32[512]{0:T(512)}, f32[2048]{0:T(1024)}, f32[3,8]{1,0:T(4,128)}) custom-call(s32[4]{0:T(128)S(1)} %copy-done.2, bf16[16,16,1792]{2,1,0:T(8,128)(2,1)S(1)} %shard_map.252.own_ref, ...), custom_call_target="tpu_custom_call" | custom-call | flops 1000 | bytes 1000 | tf_op jit(solution)/shard_map/pallas_call | solution.py:1090
  (109 shorter events, 38.2 us)
Async XLA Ops:
  2.8 11.0 %collective-permute-start = (bf16[128,512]{1,0:T(8,128)(2,1)S(1)}, bf16[128,512]{1,0:T(8,128)(2,1)S(1)}, u32[]{:S(2)}, u32[]{:S(2)}) collective-permute-start(bf16[128,512]{1,0:T(8,128)(2,1)S(1)} %get-tuple-element.142), channel_id=1, source_target_pairs={{0,4},{4,8},{8,12},{12,16},{16,20},{20,24},{24,28},{28,0},{1,5},{5... | collective-permute-start | bytes 393224 | tf_op jit(solution)/shard_map/ppermute | solution.py:870
  5.7 9.4 %collective-permute-start.1 = (bf16[128,512]{1,0:T(8,128)(2,1)S(1)}, bf16[128,512]{1,0:T(8,128)(2,1)S(1)}, u32[]{:S(2)}, u32[]{:S(2)}) collective-permute-start(bf16[128,512]{1,0:T(8,128)(2,1)S(1)} %get-tuple-element.141), channel_id=1, source_target_pairs={{0,8},{4,12},{8,16},{12,20},{16,24},{20,28},{24,0},{28,4},{1,9},{5... | collective-permute-start | bytes 393224 | tf_op jit(solution)/shard_map/ppermute | solution.py:870
  7.3 16.3 %collective-permute-start.2 = (bf16[128,512]{1,0:T(8,128)(2,1)S(1)}, bf16[128,512]{1,0:T(8,128)(2,1)S(1)}, u32[]{:S(2)}, u32[]{:S(2)}) collective-permute-start(bf16[128,512]{1,0:T(8,128)(2,1)S(1)} %get-tuple-element.140), channel_id=1, source_target_pairs={{0,12},{4,16},{8,20},{12,24},{16,28},{20,0},{24,4},{28,8},{1,13},{... | collective-permute-start | bytes 393224 | tf_op jit(solution)/shard_map/ppermute | solution.py:870
  9.8 14.1 %collective-permute-start.3 = (bf16[128,512]{1,0:T(8,128)(2,1)S(1)}, bf16[128,512]{1,0:T(8,128)(2,1)S(1)}, u32[]{:S(2)}, u32[]{:S(2)}) collective-permute-start(bf16[128,512]{1,0:T(8,128)(2,1)S(1)} %get-tuple-element.139), channel_id=1, source_target_pairs={{0,16},{4,20},{8,24},{12,28},{16,0},{20,4},{24,8},{28,12},{1,17},{... | collective-permute-start | bytes 393224 | tf_op jit(solution)/shard_map/ppermute | solution.py:870
  11.1 12.9 %collective-permute-start.4 = (bf16[128,512]{1,0:T(8,128)(2,1)S(1)}, bf16[128,512]{1,0:T(8,128)(2,1)S(1)}, u32[]{:S(2)}, u32[]{:S(2)}) collective-permute-start(bf16[128,512]{1,0:T(8,128)(2,1)S(1)} %get-tuple-element.138), channel_id=1, source_target_pairs={{0,20},{4,24},{8,28},{12,0},{16,4},{20,8},{24,12},{28,16},{1,21},{... | collective-permute-start | bytes 393224 | tf_op jit(solution)/shard_map/ppermute | solution.py:870
  13.7 10.3 %collective-permute-start.5 = (bf16[128,512]{1,0:T(8,128)(2,1)S(1)}, bf16[128,512]{1,0:T(8,128)(2,1)S(1)}, u32[]{:S(2)}, u32[]{:S(2)}) collective-permute-start(bf16[128,512]{1,0:T(8,128)(2,1)S(1)} %get-tuple-element.144), channel_id=1, source_target_pairs={{0,24},{4,28},{8,0},{12,4},{16,8},{20,12},{24,16},{28,20},{1,25},{... | collective-permute-start | bytes 393224 | tf_op jit(solution)/shard_map/ppermute | solution.py:870
  15.1 8.9 %collective-permute-start.6 = (bf16[128,512]{1,0:T(8,128)(2,1)S(1)}, bf16[128,512]{1,0:T(8,128)(2,1)S(1)}, u32[]{:S(2)}, u32[]{:S(2)}) collective-permute-start(bf16[128,512]{1,0:T(8,128)(2,1)S(1)} %get-tuple-element.137), channel_id=1, source_target_pairs={{0,28},{4,0},{8,4},{12,8},{16,12},{20,16},{24,20},{28,24},{1,29},{... | collective-permute-start | bytes 393224 | tf_op jit(solution)/shard_map/ppermute | solution.py:870
  24.0 37.1 %all-to-all-start = ((bf16[8,128,512]{2,1,0:T(8,128)(2,1)}), bf16[8,128,512]{2,1,0:T(8,128)(2,1)S(1)}, u32[]{:S(2)}, u32[]{:S(2)}) async-start(bf16[8,128,512]{2,1,0:T(8,128)(2,1)} %param.15), calls=%async_computation | async-start | bytes 2097152 | tf_op jit(solution)/shard_map/all_to_all | solution.py:861
  90.9 10.5 %collective-permute-start.7 = (bf16[16,16,4608]{2,1,0:T(8,128)(2,1)}, bf16[16,16,4608]{2,1,0:T(8,128)(2,1)S(1)}, u32[]{:S(2)}, u32[]{:S(2)}) collective-permute-start(bf16[16,16,4608]{2,1,0:T(8,128)(2,1)} %bitcast.69), channel_id=1, source_target_pairs={{0,1},{1,0},{2,3},{3,2},{4,5},{5,4},{6,7},{7,6},{8,9},{9,8},{10,11... | collective-permute-start | bytes 7077896 | tf_op jit(solution)/shard_map/ppermute | solution.py:979
  103.1 38.6 %collective-permute-start.10 = (bf16[4,16,4608]{2,1,0:T(8,128)(2,1)}, bf16[4,16,4608]{2,1,0:T(8,128)(2,1)S(1)}, u32[]{:S(2)}, u32[]{:S(2)}) collective-permute-start(bf16[4,16,4608]{2,1,0:T(8,128)(2,1)} %get-tuple-element.132), channel_id=1, source_target_pairs={{0,6},{1,7},{2,4},{3,5},{4,2},{5,3},{6,0},{7,1},{8,14},{9,15},{10,... | collective-permute-start | bytes 1769480 | tf_op jit(solution)/shard_map/ppermute | solution.py:979
  105.3 36.5 %collective-permute-start.8 = (bf16[4,16,4608]{2,1,0:T(8,128)(2,1)S(1)}, bf16[4,16,4608]{2,1,0:T(8,128)(2,1)}, u32[]{:S(2)}, u32[]{:S(2)}) collective-permute-start(bf16[4,16,4608]{2,1,0:T(8,128)(2,1)S(1)} %get-tuple-element.134), channel_id=1, source_target_pairs={{0,4},{1,5},{2,6},{3,7},{4,0},{5,1},{6,2},{7,3},{8,12},{9,13},{10,... | collective-permute-start | bytes 1769480 | tf_op jit(solution)/shard_map/ppermute | solution.py:979
  106.1 35.7 %collective-permute-start.9 = (bf16[4,16,4608]{2,1,0:T(8,128)(2,1)S(1)}, bf16[4,16,4608]{2,1,0:T(8,128)(2,1)}, u32[]{:S(2)}, u32[]{:S(2)}) collective-permute-start(bf16[4,16,4608]{2,1,0:T(8,128)(2,1)S(1)} %get-tuple-element.133), channel_id=1, source_target_pairs={{0,2},{1,3},{2,0},{3,1},{4,6},{5,7},{6,4},{7,5},{8,10},{9,11},{10,... | collective-permute-start | bytes 1769480 | tf_op jit(solution)/shard_map/ppermute | solution.py:979
  106.6 41.2 %all-to-all-start.1 = ((bf16[8,128,512]{2,1,0:T(8,128)(2,1)}), bf16[8,128,512]{2,1,0:T(8,128)(2,1)S(1)}, u32[]{:S(2)}, u32[]{:S(2)}) async-start(bf16[8,128,512]{2,1,0:T(8,128)(2,1)} %bitcast.19), calls=%async_computation.1 | async-start | bytes 2097152 | tf_op jit(solution)/shard_map/all_to_all | solution.py:861
  143.4 15.1 %collective-permute-start.11 = (bf16[1,16,4608]{2,1,0:T(8,128)(2,1)S(1)}, bf16[1,16,4608]{2,1,0:T(8,128)(2,1)S(1)}, u32[]{:S(2)}, u32[]{:S(2)}) collective-permute-start(bf16[1,16,4608]{2,1,0:T(8,128)(2,1)S(1)} %get-tuple-element.152), channel_id=1, source_target_pairs={{0,8},{1,9},{2,10},{3,11},{4,12},{5,13},{6,14},{7,15},{8,0},{9,1},... | collective-permute-start | bytes 442376 | tf_op jit(solution)/shard_map/ppermute | solution.py:979
  145.4 13.6 %collective-permute-start.12 = (bf16[1,16,4608]{2,1,0:T(8,128)(2,1)S(1)}, bf16[1,16,4608]{2,1,0:T(8,128)(2,1)S(1)}, u32[]{:S(2)}, u32[]{:S(2)}) collective-permute-start(bf16[1,16,4608]{2,1,0:T(8,128)(2,1)S(1)} %get-tuple-element.151), channel_id=1, source_target_pairs={{0,16},{1,17},{2,18},{3,19},{4,20},{5,21},{6,22},{7,23},{8,24},{9,... | collective-permute-start | bytes 442376 | tf_op jit(solution)/shard_map/ppermute | solution.py:979
  147.8 11.3 %collective-permute-start.13 = (bf16[1,16,4608]{2,1,0:T(8,128)(2,1)S(1)}, bf16[1,16,4608]{2,1,0:T(8,128)(2,1)S(1)}, u32[]{:S(2)}, u32[]{:S(2)}) collective-permute-start(bf16[1,16,4608]{2,1,0:T(8,128)(2,1)S(1)} %get-tuple-element.150), channel_id=1, source_target_pairs={{0,24},{1,25},{2,26},{3,27},{4,28},{5,29},{6,30},{7,31},{8,16},{9,... | collective-permute-start | bytes 442376 | tf_op jit(solution)/shard_map/ppermute | solution.py:979
  159.1 9.3 %collective-permute-start.18 = (bf16[1,16,4608]{2,1,0:T(8,128)(2,1)S(1)}, bf16[1,16,4608]{2,1,0:T(8,128)(2,1)S(1)}, u32[]{:S(2)}, u32[]{:S(2)}) collective-permute-start(bf16[1,16,4608]{2,1,0:T(8,128)(2,1)S(1)} %add_convert_fusion.2.refs_0_), channel_id=1, source_target_pairs={{0,8},{1,9},{2,10},{3,11},{4,12},{5,13},{6,14},{7,15},{8,0},{9,1},... | collective-permute-start | bytes 442376 | tf_op jit(solution)/shard_map/ppermute | solution.py:979
  163.1 20.0 %collective-permute-start.15 = (bf16[4,16,1792]{2,1,0:T(8,128)(2,1)S(1)}, bf16[4,16,1792]{2,1,0:T(8,128)(2,1)S(1)}, u32[]{:S(2)}, u32[]{:S(2)}) collective-permute-start(bf16[4,16,1792]{2,1,0:T(8,128)(2,1)S(1)} %get-tuple-element.148), channel_id=1, source_target_pairs={{0,4},{1,5},{2,6},{3,7},{4,0},{5,1},{6,2},{7,3},{8,12},{9,13},{10,... | collective-permute-start | bytes 688136 | tf_op jit(solution)/shard_map/ppermute | solution.py:979
  164.9 18.2 %collective-permute-start.16 = (bf16[4,16,1792]{2,1,0:T(8,128)(2,1)S(1)}, bf16[4,16,1792]{2,1,0:T(8,128)(2,1)S(1)}, u32[]{:S(2)}, u32[]{:S(2)}) collective-permute-start(bf16[4,16,1792]{2,1,0:T(8,128)(2,1)S(1)} %get-tuple-element.147), channel_id=1, source_target_pairs={{0,2},{1,3},{2,0},{3,1},{4,6},{5,7},{6,4},{7,5},{8,10},{9,11},{10,... | collective-permute-start | bytes 688136 | tf_op jit(solution)/shard_map/ppermute | solution.py:979
  166.4 16.7 %collective-permute-start.17 = (bf16[4,16,1792]{2,1,0:T(8,128)(2,1)S(1)}, bf16[4,16,1792]{2,1,0:T(8,128)(2,1)S(1)}, u32[]{:S(2)}, u32[]{:S(2)}) collective-permute-start(bf16[4,16,1792]{2,1,0:T(8,128)(2,1)S(1)} %get-tuple-element.146), channel_id=1, source_target_pairs={{0,6},{1,7},{2,4},{3,5},{4,2},{5,3},{6,0},{7,1},{8,14},{9,15},{10,... | collective-permute-start | bytes 688136 | tf_op jit(solution)/shard_map/ppermute | solution.py:979
  166.6 13.4 %collective-permute-start.19 = (bf16[1,16,4608]{2,1,0:T(8,128)(2,1)S(1)}, bf16[1,16,4608]{2,1,0:T(8,128)(2,1)S(1)}, u32[]{:S(2)}, u32[]{:S(2)}) collective-permute-start(bf16[1,16,4608]{2,1,0:T(8,128)(2,1)S(1)} %add_convert_fusion.2.refs_0_), channel_id=1, source_target_pairs={{0,16},{1,17},{2,18},{3,19},{4,20},{5,21},{6,22},{7,23},{8,24},{9,... | collective-permute-start | bytes 442376 | tf_op jit(solution)/shard_map/ppermute | solution.py:979
  168.4 11.6 %collective-permute-start.20 = (bf16[1,16,4608]{2,1,0:T(8,128)(2,1)S(1)}, bf16[1,16,4608]{2,1,0:T(8,128)(2,1)S(1)}, u32[]{:S(2)}, u32[]{:S(2)}) collective-permute-start(bf16[1,16,4608]{2,1,0:T(8,128)(2,1)S(1)} %add_convert_fusion.2.refs_0_), channel_id=1, source_target_pairs={{0,24},{1,25},{2,26},{3,27},{4,28},{5,29},{6,30},{7,31},{8,16},{9,... | collective-permute-start | bytes 442376 | tf_op jit(solution)/shard_map/ppermute | solution.py:979
  180.1 8.7 %collective-permute-start.22 = (bf16[4,16,2304]{2,1,0:T(8,128)(2,1)S(1)}, bf16[4,16,2304]{2,1,0:T(8,128)(2,1)S(1)}, u32[]{:S(2)}, u32[]{:S(2)}) collective-permute-start(bf16[4,16,2304]{2,1,0:T(8,128)(2,1)S(1)} %get-tuple-element.113.refs_0_), channel_id=1, source_target_pairs={{0,4},{1,5},{2,6},{3,7},{4,0},{5,1},{6,2},{7,3},{8,12},{9,13},{10,... | collective-permute-start | bytes 884744 | tf_op jit(solution)/shard_map/ppermute | solution.py:979
  181.6 7.8 %collective-permute-start.21 = (bf16[4,16,2304]{2,1,0:T(8,128)(2,1)S(1)}, bf16[4,16,2304]{2,1,0:T(8,128)(2,1)S(1)}, u32[]{:S(2)}, u32[]{:S(2)}) collective-permute-start(bf16[4,16,2304]{2,1,0:T(8,128)(2,1)S(1)} %get-tuple-element.112.refs_0_), channel_id=1, source_target_pairs={{0,2},{1,3},{2,0},{3,1},{4,6},{5,7},{6,4},{7,5},{8,10},{9,11},{10,... | collective-permute-start | bytes 884744 | tf_op jit(solution)/shard_map/ppermute | solution.py:979
  183.3 7.3 %collective-permute-start.23 = (bf16[1,16,1792]{2,1,0:T(8,128)(2,1)S(1)}, bf16[1,16,1792]{2,1,0:T(8,128)(2,1)S(1)}, u32[]{:S(2)}, u32[]{:S(2)}) collective-permute-start(bf16[1,16,1792]{2,1,0:T(8,128)(2,1)S(1)} %get-tuple-element.158), channel_id=1, source_target_pairs={{0,8},{1,9},{2,10},{3,11},{4,12},{5,13},{6,14},{7,15},{8,0},{9,1},... | collective-permute-start | bytes 172040 | tf_op jit(solution)/shard_map/ppermute | solution.py:979
  188.8 14.3 %collective-permute-start.30 = (bf16[8,16,2304]{2,1,0:T(8,128)(2,1)S(1)}, bf16[8,16,2304]{2,1,0:T(8,128)(2,1)S(1)}, u32[]{:S(2)}, u32[]{:S(2)}) collective-permute-start(bf16[8,16,2304]{2,1,0:T(8,128)(2,1)S(1)} %shard_map.248.refs_2_), channel_id=1, source_target_pairs={{0,2},{1,3},{2,0},{3,1},{4,6},{5,7},{6,4},{7,5},{8,10},{9,11},{10,... | collective-permute-start | bytes 1769480 | tf_op jit(solution)/shard_map/ppermute | solution.py:979
  189.4 13.9 %collective-permute-start.29 = (bf16[8,16,2304]{2,1,0:T(8,128)(2,1)S(1)}, bf16[8,16,2304]{2,1,0:T(8,128)(2,1)S(1)}, u32[]{:S(2)}, u32[]{:S(2)}) collective-permute-start(bf16[8,16,2304]{2,1,0:T(8,128)(2,1)S(1)} %shard_map.247.refs_0_), channel_id=1, source_target_pairs={{0,4},{1,5},{2,6},{3,7},{4,0},{5,1},{6,2},{7,3},{8,12},{9,13},{10,... | collective-permute-start | bytes 1769480 | tf_op jit(solution)/shard_map/ppermute | solution.py:979
  203.5 11.3 %collective-permute-start.31 = (bf16[16,16,4608]{2,1,0:T(8,128)(2,1)S(1)}, bf16[16,16,4608]{2,1,0:T(8,128)(2,1)}, u32[]{:S(2)}, u32[]{:S(2)}) collective-permute-start(bf16[16,16,4608]{2,1,0:T(8,128)(2,1)S(1)} %shard_map.250.own_ref), channel_id=1, source_target_pairs={{0,1},{1,0},{2,3},{3,2},{4,5},{5,4},{6,7},{7,6},{8,9},{9,8},{10,11... | collective-permute-start | bytes 7077896 | tf_op jit(solution)/shard_map/ppermute | solution.py:979
  203.5 34.1 %all-to-all-start.2 = ((bf16[8,128,512]{2,1,0:T(8,128)(2,1)}), bf16[8,128,512]{2,1,0:T(8,128)(2,1)S(1)}, u32[]{:S(2)}, u32[]{:S(2)}) async-start(bf16[8,128,512]{2,1,0:T(8,128)(2,1)} %bitcast.57), calls=%async_computation.2 | async-start | bytes 2097152 | tf_op jit(solution)/shard_map/all_to_all | solution.py:861
  211.2 24.1 %collective-permute-start.32 = (bf16[4,16,1792]{2,1,0:T(8,128)(2,1)}, bf16[4,16,1792]{2,1,0:T(8,128)(2,1)S(1)}, u32[]{:S(2)}, u32[]{:S(2)}) collective-permute-start(bf16[4,16,1792]{2,1,0:T(8,128)(2,1)} %copy-done), channel_id=1, source_target_pairs={{0,4},{1,5},{2,6},{3,7},{4,0},{5,1},{6,2},{7,3},{8,12},{9,13},{10,... | collective-permute-start | bytes 688136 | tf_op jit(solution)/shard_map/ppermute | solution.py:979
  213.2 22.0 %collective-permute-start.33 = (bf16[4,16,1792]{2,1,0:T(8,128)(2,1)}, bf16[4,16,1792]{2,1,0:T(8,128)(2,1)S(1)}, u32[]{:S(2)}, u32[]{:S(2)}) collective-permute-start(bf16[4,16,1792]{2,1,0:T(8,128)(2,1)} %copy-done), channel_id=1, source_target_pairs={{0,2},{1,3},{2,0},{3,1},{4,6},{5,7},{6,4},{7,5},{8,10},{9,11},{10,... | collective-permute-start | bytes 688136 | tf_op jit(solution)/shard_map/ppermute | solution.py:979
  213.7 21.5 %collective-permute-start.34 = (bf16[4,16,1792]{2,1,0:T(8,128)(2,1)}, bf16[4,16,1792]{2,1,0:T(8,128)(2,1)S(1)}, u32[]{:S(2)}, u32[]{:S(2)}) collective-permute-start(bf16[4,16,1792]{2,1,0:T(8,128)(2,1)} %copy-done), channel_id=1, source_target_pairs={{0,6},{1,7},{2,4},{3,5},{4,2},{5,3},{6,0},{7,1},{8,14},{9,15},{10,... | collective-permute-start | bytes 688136 | tf_op jit(solution)/shard_map/ppermute | solution.py:979
  (19 other events, 190.4 us)

commit v4 on v3

--- a/solution.py
+++ b/solution.py
@@ -246,7 +246,7 @@
     together, number, whole_sequence, place_ref, lengths_ref, blend_ref, q_ref, k_ref, v_ref, go_ref, *refs
 ):
     meta_ref = lengths_ref[place_ref[0]], place_ref[1]
-    blend_at = blend_rows(blend_ref, number * (width_of(q_ref) // PAIR))
+    blend_at = blend_rows(blend_ref, (number + pl.program_id(0)) * (width_of(q_ref) // PAIR))
     halo_k, halo_v, state_ref, later_ref = (None,) * 4 if whole_sequence else refs[:4]
     if whole_sequence:
         gq_ref, gk_ref, gv_ref, mix_ref = refs[:4]
@@ -497,19 +497,30 @@
     )(place, lengths, blend, qkv, qkv, qkv, *earlier)
 
 
-def attend_back(place, lengths, blend, qkv, halo, state, later, go, calls, number):
+def attend_back(place, lengths, blend, qkv, halo, state, later, go, first, count):
     rows, width = qkv.shape[0], qkv.shape[1] // 3
-    lanes = width // calls
-    columns, ins, before = attention_specs(rows, width, lanes, lambda i: number)
+    lanes = PAIR
+    columns, ins, before = attention_specs(rows, width, lanes, lambda i: first + i)
     others = () if state is None else (halo, halo, state, later)
-    outs = [outcome((rows, lanes), BF16)] * 3 + [outcome((3, lanes), F32)]
+
+    def side_by_side(height, dtype):
+        shape = jax.ShapeDtypeStruct((height, count * lanes), dtype)
+        return shape, pl.BlockSpec((height, lanes), lambda i: (0, i))
+
+    outs = [side_by_side(rows, BF16)] * 3 + [side_by_side(3, F32)]
     if state is not None:
-        outs += [outcome((TILE, lanes), BF16)] * 2
-        outs += [outcome((2, lanes // PAIR, PAIR, 2 * PAIR), F32)]
+        share = (2, 1, PAIR, 2 * PAIR)
+        outs += [side_by_side(TILE, BF16)] * 2
+        outs += [
+            (
+                jax.ShapeDtypeStruct((2, count) + share[2:], F32),
+                pl.BlockSpec(share, lambda i: (0, i, 0, 0)),
+            )
+        ]
     shapes, blocks = zip(*outs)
     return pl.pallas_call(
-        functools.partial(attend_back_kernel, together(rows, lanes), number, state is None),
-        grid=(1,),
+        functools.partial(attend_back_kernel, together(rows, lanes), first, state is None),
+        grid=(count,),
         out_shape=shapes,
         in_specs=ins + [columns(rows, 0)] + (before + before[-1:])[: len(others)],
         out_specs=blocks,
@@ -542,10 +553,9 @@
 
 def gelu_pair(field):
     square = field * field
-    bent = jnp.tanh(GELU_A * field * (1.0 + GELU_B * square))
-    half = 0.5 + 0.5 * bent
-    slope = half + 0.5 * field * (1.0 - bent * bent) * (GELU_A + 3.0 * GELU_A * GELU_B * square)
-    return field * half, slope
+    half = 0.5 + 0.5 * jnp.tanh(field * (GELU_A + GELU_A * GELU_B * square))
+    act = field * half
+    return act, half + act * (1.0 - half) * (2.0 * GELU_A + 6.0 * GELU_A * GELU_B * square)
 
 
 def column_sum(block):
@@ -559,7 +569,7 @@
     @pl.when(pl.program_id(0) == 0)
     def _():
         for k, part in enumerate(parts):
-            at = lax.rem(place_ref[0] + len(parts) - k, len(parts)) * span
+            at = (place_ref[0] ^ k) * span
             whole_x[pl.ds(pl.multiple_of(at, span), span), :] = part[...]
 
     x = whole_x[pl.ds(pl.multiple_of(pl.program_id(0) * chunk, chunk), chunk), :]
@@ -685,23 +695,26 @@
                 copy.start()
                 leaving.append(copy)
 
-        flat, each, after_out = width // pieces, pieces, inner + width
+        flat, after_out = width // pieces, inner + width
+
+        def spread(block, share, ref):
+            for below in range(pieces):
+                piece, side = divmod(block * pieces + below, len(tiles))
+                rows = slice(piece % (pieces // 2) * flat, (piece % (pieces // 2) + 1) * flat)
+                lanes = slice(after_out + side * width, after_out + (side + 1) * width)
+                ref[rows, lanes] = share[below * flat : (below + 1) * flat]
+
         for block, lanes in enumerate(tiles):
             share = rows_product(hidden[:, lanes], grad_all[...]).astype(BF16)
-            for below in range(each):
-                piece, side = divmod(block * each + below, len(tiles))
-                to = slice(after_out + side * width, after_out + (side + 1) * width)
-                rows = slice(piece % (pieces // 2) * flat, (piece % (pieces // 2) + 1) * flat)
-                mine = place_ref[2] == 2 * piece // pieces
-                some = share[below * flat : (below + 1) * flat]
-
-                @pl.when(mine)
-                def _(rows=rows, to=to, some=some):
-                    keep_ref[rows, to] = some
-
-                @pl.when(jnp.logical_not(mine))
-                def _(rows=rows, to=to, some=some):
-                    send_ref[rows, to] = some
+            mine = place_ref[2] == 2 * block // len(tiles)
+
+            @pl.when(mine)
+            def _(block=block, share=share):
+                spread(block, share, keep_ref)
+
+            @pl.when(jnp.logical_not(mine))
+            def _(block=block, share=share):
+                spread(block, share, send_ref)
 
         leave(slice(after_out, after_out + inner))
         for lanes in tiles:
@@ -835,7 +848,7 @@
     calls = len(mixes)
     packed = (width // 2, 3 * width + 2 * PAIR)
     size = min(CHUNK, rows)
-    block, chunk = by_rows(size, width), by_rows(size, width // calls)
+    block = by_rows(size, width)
     return pl.pallas_call(
         functools.partial(project_back_kernel, calls),
         grid=(rows // size,),
@@ -843,7 +856,7 @@
         + (jax.ShapeDtypeStruct(packed, BF16),) * 2,
         in_specs=[pl.BlockSpec(memory_space=pltpu.SMEM), block, block]
         + [constant(a.shape) for a in (weight, gain[None], bias[None], small2, wide)]
-        + [chunk] * (3 * calls)
+        + [by_rows(size, grad.shape[1]) for grad in grads]
         + [constant(mix.shape) for mix in mixes],
         out_specs=(block, constant(packed), constant(packed)),
         scratch_shapes=[
@@ -865,8 +878,8 @@
     seqs, devices = block.shape[0], lax.axis_size(axis)
     spans = []
     for k in range(seqs):
-        span = lax.dynamic_index_in_dim(block, lax.rem(mine + k, seqs), 0, False)
-        route = [(i, i // seqs * seqs + (i + k) % seqs) for i in range(devices)]
+        span = lax.dynamic_index_in_dim(block, mine ^ k, 0, False)
+        route = [(i, i ^ k) for i in range(devices)]
         spans.append(lax.ppermute(span, axis, route) if k else span)
     return spans
 
@@ -1125,7 +1138,7 @@
         groups = [[r * seqs + s for s in range(seqs)] for r in range(parts)]
     mine, part = index % seqs, index // seqs
     ring = Ring(lax.axis_size("batch"), devices)
-    by_ring = width % (16 * ring.pieces) == 0
+    by_ring = width % (16 * ring.pieces) == 0 and ring.sizes["near"] == 4
     inner = in_weight.shape[1]
     numbers = [mine, part * rows, 0, 0]
     if by_ring:
@@ -1154,36 +1167,32 @@
         return to_sequences(rows.reshape(seqs, span, width), "seq", groups)
 
     feed_shapes = [(width, inner), (width, width), (inner, width)]
-    calls = 4
-
-    def back(place, number, later):
+    calls = ((0, 1), (1, width // PAIR - 1))
+
+    def back(place, pairs, later):
         return attend_back(
-            place, lengths, blend_weights, qkv, halo, state, later, grad_o, calls, number
+            place, lengths, blend_weights, qkv, halo, state, later, grad_o, *pairs
         )
 
     if parts > 1:
-        total = jnp.concatenate([back(place, number, later)[6] for number in range(calls)], 1)
+        total = jnp.concatenate([back(place, pairs, later)[6] for pairs in calls], 1)
         later = from_parts(total, "seq", parts, seqs, False)
-    backs, turn = [], place
     if by_ring:
-        held, output = None, move(result)
-        for number in range(calls):
-            if number == 1:
-                held = ring.scatter_cores(feed_keep, feed_send, 0, (backs[0][3],))
-                turn = after(turn, held)
-            backs.append(back(turn, number, later))
-            turn = after(turn, backs[-1][3])
-        held = ring.scatter(held, "near", 0, (backs[3][3],))
-        output = settle(after(output, backs[2][3]))
+        output = move(result)
+        backs = [back(place, calls[0], later)]
+        held = ring.scatter_cores(feed_keep, feed_send, 0, (backs[0][3],))
+        backs.append(back(after(place, held), calls[1], later))
+        held = ring.scatter(held, "near", 0, (backs[1][3],))
+        output = settle(after(output, backs[1][3]))
         grad_first = after(grad_first, held, output)
     else:
-        backs = [back(place, number, later) for number in range(calls)]
+        backs = [back(place, pairs, later) for pairs in calls]
         output = move(result)
     grads = [[call[part] for call in backs] for part in range(3)]
     if parts > 1:
         homeward = [(i + seqs, i) for i in range(devices - seqs)]
         for part in (1, 2):
-            for number in range(calls):
+            for number in range(len(calls)):
                 received = lax.ppermute(backs[number][part + 3], "seq", homeward)
                 grad = grads[part][number]
                 tail = grad[rows - TILE :].astype(F32) + received.astype(F32)
@@ -1197,10 +1206,9 @@
     if by_ring:
         held = ring.scatter(held, "far", 0, (project_keep,))
         late = ring.scatter_cores(project_keep, project_send, PAIR, (held,))
-        late = ring.slices(late, "near")
-        halves = ring.gather_split(held, "far", late)
+        late = ring.scatter(late, "near", PAIR)
+        halves = ring.gather_split(held, "far", (late,))
         ways = [ring.swap(half, "near", k) for half, k in zip(halves, (2, 1))]
-        late = ring.scatter(late, "near", PAIR)
         halves = [join([half, way]) for half, way in zip(halves, ways)]
         ways = [ring.swap(half, "near", k) for half, k in zip(halves, (1, 2))]
         late = ring.scatter(late, "far", PAIR, halves)

time: 246 us -> 243 us (0.988)
  waiting for transfers between devices: 43.9 us -> 57 us
  starting transfers between devices: 73.7 us -> 62.7 us
  Pallas kernels: 113 us -> 108 us
    ppermute x7, waiting for transfers between devices: 6.84 us -> 13.9 us  [spans_of(): spans.append(lax.ppermute(span, axis, route) if k else span)]
    ppermute x29, waiting for transfers between devices: 31.8 us -> 38 us  [swap(): return lax.ppermute(value, ('seq', 'batch'), route)]
    all_to_all x3, starting transfers between devices: 23.4 us -> 18.2 us  [to_sequences(): return lax.all_to_all(block, axis, 0, 0, axis_index_groups=groups)]
    ppermute x29, starting transfers between devices: 35.9 us -> 31.4 us  [swap(): return lax.ppermute(value, ('seq', 'batch'), route)]
    pallas_call x4 -> x2, Pallas kernels: 41.8 us -> 37.4 us  [attend_back(): pl.pallas_call(functools.partial(attend_back_kernel, together(rows, lanes...]
  transfers between devices with their start and end apart: 39 -> 39, of which waited for: 12 -> 18; matrix products, arithmetic and copies ran while one was open for 2% -> 1% of each run, Pallas kernels for 34% -> 33%
where the time goes in v4:
time: 243 us; the launch traced here: 239 us
  Pallas kernels  108 us (44%)
  starting transfers between devices  62.7 us (26%)
  waiting for transfers between devices  57 us (23%)
  local copies, waits for them, and re-layouts  4.98 us (2%)
  other arithmetic  4.65 us (2%)
    ppermute x29, waiting for transfers between devices, swap(): return lax.ppermute(value, ('seq', 'batch'), route)  38 us
    pallas_call x2, Pallas kernels, attend_back(): pl.pallas_call(functools.partial(attend_back_kernel, together(rows, lanes...  37.4 us
    ppermute x29, starting transfers between devices, swap(): return lax.ppermute(value, ('seq', 'batch'), route)  31.4 us
    pallas_call x1, Pallas kernels, feed_forward(): pl.pallas_call(functools.partial(feed_kernel, pieces), grid=(rows // size...  27.2 us
    all_to_all x3, starting transfers between devices, to_sequences(): return lax.all_to_all(block, axis, 0, 0, axis_index_groups=groups)  18.2 us
    pallas_call x1, Pallas kernels, attend(): pl.pallas_call(functools.partial(attend_kernel, together(rows, lanes), st...  15.7 us
    ppermute x7, waiting for transfers between devices, spans_of(): spans.append(lax.ppermute(span, axis, route) if k else span)  13.9 us
    ppermute x7, starting transfers between devices, spans_of(): spans.append(lax.ppermute(span, axis, route) if k else span)  13.1 us
  transfers between devices with their start and end apart: 39, of which 18 were waited for; matrix products, arithmetic and copies ran while one was open for 1% of the time, Pallas kernels for 33%

profile of v4, /device:TPU:0, one launch (start us, length us, event | category | flops | bytes accessed | tf_op | source)
XLA Modules:
  0.0 238.8 jit_solution(2964317901845351886)
XLA Ops:
  0.7 2.0 dynamic-slice_bitcast_fusion.8
  2.7 3.0 %collective-permute-start = (bf16[128,512]{1,0:T(8,128)(2,1)S(1)}, bf16[128,512]{1,0:T(8,128)(2,1)S(1)}, u32[]{:S(2)}, u32[]{:S(2)}) collective-permute-start(bf16[128,512]{1,0:T(8,128)(2,1)S(1)} %get-tuple-element.120), channel_id=1, source_target_pairs={{0,4},{4,0},{8,12},{12,8},{16,20},{20,16},{24,28},{28,24},{1,5},{5... | collective-permute-start | bytes 393224 | tf_op jit(solution)/shard_map/ppermute | solution.py:883
  7.3 3.0 %collective-permute-start.3 = (bf16[128,512]{1,0:T(8,128)(2,1)S(1)}, bf16[128,512]{1,0:T(8,128)(2,1)S(1)}, u32[]{:S(2)}, u32[]{:S(2)}) collective-permute-start(bf16[128,512]{1,0:T(8,128)(2,1)S(1)} %get-tuple-element.117), channel_id=1, source_target_pairs={{0,16},{4,20},{8,24},{12,28},{16,0},{20,4},{24,8},{28,12},{1,17},{... | collective-permute-start | bytes 393224 | tf_op jit(solution)/shard_map/ppermute | solution.py:883
  11.5 3.6 %collective-permute-start.5 = (bf16[128,512]{1,0:T(8,128)(2,1)S(1)}, bf16[128,512]{1,0:T(8,128)(2,1)S(1)}, u32[]{:S(2)}, u32[]{:S(2)}) collective-permute-start(bf16[128,512]{1,0:T(8,128)(2,1)S(1)} %get-tuple-element.122), channel_id=1, source_target_pairs={{0,24},{4,28},{8,16},{12,20},{16,8},{20,12},{24,0},{28,4},{1,25},{... | collective-permute-start | bytes 393224 | tf_op jit(solution)/shard_map/ppermute | solution.py:883
  17.1 12.6 %collective-permute-done.4.refs_5_ = bf16[128,512]{1,0:T(8,128)(2,1)S(1)} collective-permute-done((bf16[128,512]{1,0:T(8,128)(2,1)S(1)}, bf16[128,512]{1,0:T(8,128)(2,1)S(1)}, u32[]{:S(2)}, u32[]{:S(2)}) %collective-permute-start.4) | collective-permute-done | bytes 131104 | tf_op jit(solution)/shard_map/ppermute | solution.py:883
  29.7 7.8 %all-to-all-start = ((bf16[8,128,512]{2,1,0:T(8,128)(2,1)}), bf16[8,128,512]{2,1,0:T(8,128)(2,1)S(1)}, u32[]{:S(2)}, u32[]{:S(2)}) async-start(bf16[8,128,512]{2,1,0:T(8,128)(2,1)} %param.15), calls=%async_computation | async-start | bytes 2097152 | tf_op jit(solution)/shard_map/all_to_all | solution.py:874
  38.2 5.6 %shard_map.237 = (bf16[1024,512]{1,0:T(8,128)(2,1)}, bf16[1024,1536]{1,0:T(8,128)(2,1)}) custom-call(s32[4]{0:T(128)} %pad_add_fusion.place_ref, bf16[512,1536]{1,0:T(8,128)(2,1)} %w_ref.3, f32[1,512]{1,0:T(1,128)} %bitcast.62, f32[1,512]{1,0:T(1,128)} %bitcast.64, bf16[128,512]{1,0:T(8,128)(2,1)} %get-tuple-element.121.refs_0_, bf16[128,512]{1,0:T(8,128)(2,1)} %copy-done.5, ...), custom_call_target="tpu_custom_call" | custom-call | flops 1000 | bytes 1000 | tf_op jit(solution)/shard_map/pallas_call | solution.py:586
  43.8 15.7 %shard_map.238.att_ref = bf16[1024,512]{1,0:T(8,128)(2,1)} custom-call(s32[4]{0:T(128)} %pad_add_fusion.place_ref, s32[8]{0:T(128)} %lengths_ref.5, f32[3,8]{1,0:T(4,128)} %blend_ref.5, bf16[1024,1536]{1,0:T(8,128)(2,1)} %get-tuple-element.62.q_ref.k_ref.v_ref, bf16[1024,1536]{1,0:T(8,128)(2,1)} %get-tuple-element.62.q_ref.k_ref.v_ref, ...), custom_call_target="tpu_custom_call" | custom-call | flops 1000 | bytes 1000 | tf_op jit(solution)/shard_map/pallas_call | solution.py:485
  59.5 2.9 %all-to-all-done = bf16[8,128,512]{2,1,0:T(8,128)(2,1)S(1)} async-done(((bf16[8,128,512]{2,1,0:T(8,128)(2,1)}), bf16[8,128,512]{2,1,0:T(8,128)(2,1)S(1)}, u32[]{:S(2)}, u32[]{:S(2)}) %all-to-all-start) | async-done | bytes 1048608 | tf_op jit(solution)/shard_map/all_to_all | solution.py:874
  63.4 27.2 %shard_map.239 = (bf16[1024,512]{1,0:T(8,128)(2,1)}, f32[1024,512]{1,0:T(8,128)}, f32[1024,512]{1,0:T(8,128)}, bf16[256,4608]{1,0:T(8,128)(2,1)}, bf16[256,4608]...) custom-call(s32[4]{0:T(128)} %pad_add_fusion.place_ref, bf16[1024,512]{1,0:T(8,128)(2,1)} %get-tuple-element.61.x_ref, ...), custom_call_target="tpu_custom_call" | custom-call | flops 1000 | bytes 1000 | tf_op jit(solution)/shard_map/pallas_call | solution.py:750
  90.7 10.5 %shard_map.240 = (bf16[1024,128]{1,0:T(8,128)(2,1)}, bf16[1024,128]{1,0:T(8,128)(2,1)}, bf16[1024,128]{1,0:T(8,128)(2,1)}, f32[3,128]{1,0:T(4,128)}) custom-call(s32[4]{0:T(128)} %pad_add_fusion.place_ref, s32[8]{0:T(128)} %lengths_ref.5, f32[3,8]{1,0:T(4,128)} %blend_ref.5, bf16[1024,1536]{1,0:T(8,128)(2,1)} %get-tuple-element.62.q_ref.k_ref.v_ref, ...), custom_call_target="tpu_custom_call" | custom-call | flops 1000 | bytes 1000 | tf_op jit(solution)/shard_map/pallas_call | solution.py:521
  103.1 2.1 collective-permute-start.10
  106.6 3.8 %all-to-all-start.1 = ((bf16[8,128,512]{2,1,0:T(8,128)(2,1)}), bf16[8,128,512]{2,1,0:T(8,128)(2,1)S(1)}, u32[]{:S(2)}, u32[]{:S(2)}) async-start(bf16[8,128,512]{2,1,0:T(8,128)(2,1)} %bitcast.19), calls=%async_computation.1 | async-start | bytes 2097152 | tf_op jit(solution)/shard_map/all_to_all | solution.py:874
  110.3 26.9 %shard_map.241 = (bf16[1024,384]{1,0:T(8,128)(2,1)}, bf16[1024,384]{1,0:T(8,128)(2,1)}, bf16[1024,384]{1,0:T(8,128)(2,1)}, f32[3,384]{1,0:T(4,128)}) custom-call(s32[4]{0:T(128)} %pad_add_fusion.place_ref, s32[8]{0:T(128)} %lengths_ref.5, f32[3,8]{1,0:T(4,128)} %blend_ref.5, bf16[1024,1536]{1,0:T(8,128)(2,1)} %get-tuple-element.62.q_ref.k_ref.v_ref, ...), custom_call_target="tpu_custom_call" | custom-call | flops 1000 | bytes 1000 | tf_op jit(solution)/shard_map/pallas_call | solution.py:521
  138.2 2.9 %collective-permute-done.8 = bf16[4,16,4608]{2,1,0:T(8,128)(2,1)} collective-permute-done((bf16[4,16,4608]{2,1,0:T(8,128)(2,1)S(1)}, bf16[4,16,4608]{2,1,0:T(8,128)(2,1)}, u32[]{:S(2)}, u32[]{:S(2)}) %collective-permute-start.8) | collective-permute-done | bytes 589856 | tf_op jit(solution)/shard_map/ppermute | solution.py:992
  143.8 3.4 %collective-permute-start.11 = (bf16[1,16,4608]{2,1,0:T(8,128)(2,1)S(1)}, bf16[1,16,4608]{2,1,0:T(8,128)(2,1)S(1)}, u32[]{:S(2)}, u32[]{:S(2)}) collective-permute-start(bf16[1,16,4608]{2,1,0:T(8,128)(2,1)S(1)} %get-tuple-element.130), channel_id=1, source_target_pairs={{0,8},{1,9},{2,10},{3,11},{4,12},{5,13},{6,14},{7,15},{8,0},{9,1},... | collective-permute-start | bytes 442376 | tf_op jit(solution)/shard_map/ppermute | solution.py:992
  148.2 10.3 %shard_map.243 = (bf16[1024,512]{1,0:T(8,128)(2,1)}, bf16[256,1792]{1,0:T(8,128)(2,1)}, bf16[256,1792]{1,0:T(8,128)(2,1)}) custom-call(s32[4]{0:T(128)} %pad_add_fusion.place_ref, bf16[1024,512]{1,0:T(8,128)(2,1)} %get-tuple-element.61.x_ref, f32[1024,512]{1,0:T(8,128)} %get-tuple-element.75.first_ref, bf16[512,1536]{1,0:T(8,128)(2,1)} %w_ref.3, ...), custom_call_target="tpu_custom_call" | custom-call | flops 1000 | bytes 1000 | tf_op jit(solution)/shard_map/pallas_call | solution.py:852
  158.7 2.6 %collective-permute-done.14 = bf16[16,16,1792]{2,1,0:T(8,128)(2,1)S(1)} collective-permute-done((bf16[16,16,1792]{2,1,0:T(8,128)(2,1)}, bf16[16,16,1792]{2,1,0:T(8,128)(2,1)S(1)}, u32[]{:S(2)}, u32[]{:S(2)}) %collective-permute-start.14) | collective-permute-done | bytes 917536 | tf_op jit(solution)/shard_map/ppermute | solution.py:992
  163.0 2.2 collective-permute-start.17
  168.1 4.3 %collective-permute-done.17 = bf16[4,16,1792]{2,1,0:T(8,128)(2,1)S(1)} collective-permute-done((bf16[4,16,1792]{2,1,0:T(8,128)(2,1)S(1)}, bf16[4,16,1792]{2,1,0:T(8,128)(2,1)S(1)}, u32[]{:S(2)}, u32[]{:S(2)}) %collective-permute-start.17) | collective-permute-done | bytes 229408 | tf_op jit(solution)/shard_map/ppermute | solution.py:992
  173.4 2.9 %collective-permute-done.16 = bf16[4,16,1792]{2,1,0:T(8,128)(2,1)S(1)} collective-permute-done((bf16[4,16,1792]{2,1,0:T(8,128)(2,1)S(1)}, bf16[4,16,1792]{2,1,0:T(8,128)(2,1)S(1)}, u32[]{:S(2)}, u32[]{:S(2)}) %collective-permute-start.16) | collective-permute-done | bytes 229408 | tf_op jit(solution)/shard_map/ppermute | solution.py:992
  176.7 3.6 %collective-permute-done.19.refs_2_ = bf16[1,16,4608]{2,1,0:T(8,128)(2,1)S(1)} collective-permute-done((bf16[1,16,4608]{2,1,0:T(8,128)(2,1)S(1)}, bf16[1,16,4608]{2,1,0:T(8,128)(2,1)S(1)}, u32[]{:S(2)}, u32[]{:S(2)}) %collective-permute-start.19) | collective-permute-done | bytes 147488 | tf_op jit(solution)/shard_map/ppermute | solution.py:992
  183.9 3.1 %collective-permute-start.24 = (bf16[1,16,1792]{2,1,0:T(8,128)(2,1)S(1)}, bf16[1,16,1792]{2,1,0:T(8,128)(2,1)S(1)}, u32[]{:S(2)}, u32[]{:S(2)}) collective-permute-start(bf16[1,16,1792]{2,1,0:T(8,128)(2,1)S(1)} %get-tuple-element.135), channel_id=1, source_target_pairs={{0,16},{1,17},{2,18},{3,19},{4,20},{5,21},{6,22},{7,23},{8,24},{9,... | collective-permute-start | bytes 172040 | tf_op jit(solution)/shard_map/ppermute | solution.py:992
  191.3 2.4 collective-permute-start.26
  194.3 1.8 collective-permute-start.28
  196.1 2.9 %collective-permute-done.27.refs_2_ = bf16[1,16,1792]{2,1,0:T(8,128)(2,1)S(1)} collective-permute-done((bf16[1,16,1792]{2,1,0:T(8,128)(2,1)S(1)}, bf16[1,16,1792]{2,1,0:T(8,128)(2,1)S(1)}, u32[]{:S(2)}, u32[]{:S(2)}) %collective-permute-start.27) | collective-permute-done | bytes 57376 | tf_op jit(solution)/shard_map/ppermute | solution.py:992
  201.5 6.6 %all-to-all-start.2 = ((bf16[8,128,512]{2,1,0:T(8,128)(2,1)}), bf16[8,128,512]{2,1,0:T(8,128)(2,1)S(1)}, u32[]{:S(2)}, u32[]{:S(2)}) async-start(bf16[8,128,512]{2,1,0:T(8,128)(2,1)} %bitcast.57), calls=%async_computation.2 | async-start | bytes 2097152 | tf_op jit(solution)/shard_map/all_to_all | solution.py:874
  208.2 2.0 collective-permute-start.32
  211.7 6.5 %shard_map.249 = (f32[512,2048]{1,0:T(8,128)}, f32[512,512]{1,0:T(8,128)}, f32[2048,512]{1,0:T(8,128)}) custom-call(s32[4]{0:T(128)S(1)} %copy-done.2, bf16[16,16,4608]{2,1,0:T(8,128)(2,1)S(1)} %shard_map.248.own_ref, bf16[16,16,4608]{2,1,0:T(8,128)(2,1)} %collective-permute-done.31.other_ref), custom_call_target="tpu_custom_call" | custom-call | flops 1000 | bytes 1000 | tf_op jit(solution)/shard_map/pallas_call | solution.py:1103
  218.2 14.0 %collective-permute-done.32.refs_1_ = bf16[4,16,1792]{2,1,0:T(8,128)(2,1)S(1)} collective-permute-done((bf16[4,16,1792]{2,1,0:T(8,128)(2,1)}, bf16[4,16,1792]{2,1,0:T(8,128)(2,1)S(1)}, u32[]{:S(2)}, u32[]{:S(2)}) %collective-permute-start.32) | collective-permute-done | bytes 229408 | tf_op jit(solution)/shard_map/ppermute | solution.py:992
  232.4 2.2 all-to-all-done.2.source_ref
  235.6 2.9 %shard_map.252 = (f32[512,1536]{1,0:T(8,128)}, f32[512]{0:T(512)}, f32[512]{0:T(512)}, f32[512]{0:T(512)}, f32[512]{0:T(512)}, /*index=5*/f32[512]{0:T(512)}, f32[2048]{0:T(1024)}, f32[3,8]{1,0:T(4,128)}) custom-call(s32[4]{0:T(128)S(1)} %copy-done.2, bf16[16,16,1792]{2,1,0:T(8,128)(2,1)S(1)} %shard_map.250.own_ref, ...), custom_call_target="tpu_custom_call" | custom-call | flops 1000 | bytes 1000 | tf_op jit(solution)/shard_map/pallas_call | solution.py:1103
  (107 shorter events, 34.0 us)
Async XLA Ops:
  2.7 8.8 %collective-permute-start = (bf16[128,512]{1,0:T(8,128)(2,1)S(1)}, bf16[128,512]{1,0:T(8,128)(2,1)S(1)}, u32[]{:S(2)}, u32[]{:S(2)}) collective-permute-start(bf16[128,512]{1,0:T(8,128)(2,1)S(1)} %get-tuple-element.120), channel_id=1, source_target_pairs={{0,4},{4,0},{8,12},{12,8},{16,20},{20,16},{24,28},{28,24},{1,5},{5... | collective-permute-start | bytes 393224 | tf_op jit(solution)/shard_map/ppermute | solution.py:883
  5.7 10.7 %collective-permute-start.1 = (bf16[128,512]{1,0:T(8,128)(2,1)S(1)}, bf16[128,512]{1,0:T(8,128)(2,1)S(1)}, u32[]{:S(2)}, u32[]{:S(2)}) collective-permute-start(bf16[128,512]{1,0:T(8,128)(2,1)S(1)} %get-tuple-element.119), channel_id=1, source_target_pairs={{0,8},{4,12},{8,0},{12,4},{16,24},{20,28},{24,16},{28,20},{1,9},{5... | collective-permute-start | bytes 393224 | tf_op jit(solution)/shard_map/ppermute | solution.py:883
  7.3 9.8 %collective-permute-start.2 = (bf16[128,512]{1,0:T(8,128)(2,1)S(1)}, bf16[128,512]{1,0:T(8,128)(2,1)S(1)}, u32[]{:S(2)}, u32[]{:S(2)}) collective-permute-start(bf16[128,512]{1,0:T(8,128)(2,1)S(1)} %get-tuple-element.118), channel_id=1, source_target_pairs={{0,12},{4,8},{8,4},{12,0},{16,28},{20,24},{24,20},{28,16},{1,13},{... | collective-permute-start | bytes 393224 | tf_op jit(solution)/shard_map/ppermute | solution.py:883
  7.3 9.8 %collective-permute-start.3 = (bf16[128,512]{1,0:T(8,128)(2,1)S(1)}, bf16[128,512]{1,0:T(8,128)(2,1)S(1)}, u32[]{:S(2)}, u32[]{:S(2)}) collective-permute-start(bf16[128,512]{1,0:T(8,128)(2,1)S(1)} %get-tuple-element.117), channel_id=1, source_target_pairs={{0,16},{4,20},{8,24},{12,28},{16,0},{20,4},{24,8},{28,12},{1,17},{... | collective-permute-start | bytes 393224 | tf_op jit(solution)/shard_map/ppermute | solution.py:883
  10.2 19.5 %collective-permute-start.4 = (bf16[128,512]{1,0:T(8,128)(2,1)S(1)}, bf16[128,512]{1,0:T(8,128)(2,1)S(1)}, u32[]{:S(2)}, u32[]{:S(2)}) collective-permute-start(bf16[128,512]{1,0:T(8,128)(2,1)S(1)} %get-tuple-element.116), channel_id=1, source_target_pairs={{0,20},{4,16},{8,28},{12,24},{16,4},{20,0},{24,12},{28,8},{1,21},{... | collective-permute-start | bytes 393224 | tf_op jit(solution)/shard_map/ppermute | solution.py:883
  11.5 18.2 %collective-permute-start.5 = (bf16[128,512]{1,0:T(8,128)(2,1)S(1)}, bf16[128,512]{1,0:T(8,128)(2,1)S(1)}, u32[]{:S(2)}, u32[]{:S(2)}) collective-permute-start(bf16[128,512]{1,0:T(8,128)(2,1)S(1)} %get-tuple-element.122), channel_id=1, source_target_pairs={{0,24},{4,28},{8,16},{12,20},{16,8},{20,12},{24,0},{28,4},{1,25},{... | collective-permute-start | bytes 393224 | tf_op jit(solution)/shard_map/ppermute | solution.py:883
  16.4 13.3 %collective-permute-start.6 = (bf16[128,512]{1,0:T(8,128)(2,1)S(1)}, bf16[128,512]{1,0:T(8,128)(2,1)S(1)}, u32[]{:S(2)}, u32[]{:S(2)}) collective-permute-start(bf16[128,512]{1,0:T(8,128)(2,1)S(1)} %get-tuple-element.115), channel_id=1, source_target_pairs={{0,28},{4,24},{8,20},{12,16},{16,12},{20,8},{24,4},{28,0},{1,29},{... | collective-permute-start | bytes 393224 | tf_op jit(solution)/shard_map/ppermute | solution.py:883
  29.7 32.7 %all-to-all-start = ((bf16[8,128,512]{2,1,0:T(8,128)(2,1)}), bf16[8,128,512]{2,1,0:T(8,128)(2,1)S(1)}, u32[]{:S(2)}, u32[]{:S(2)}) async-start(bf16[8,128,512]{2,1,0:T(8,128)(2,1)} %param.15), calls=%async_computation | async-start | bytes 2097152 | tf_op jit(solution)/shard_map/all_to_all | solution.py:874
  90.6 10.7 %collective-permute-start.7 = (bf16[16,16,4608]{2,1,0:T(8,128)(2,1)}, bf16[16,16,4608]{2,1,0:T(8,128)(2,1)S(1)}, u32[]{:S(2)}, u32[]{:S(2)}) collective-permute-start(bf16[16,16,4608]{2,1,0:T(8,128)(2,1)} %bitcast.69), channel_id=1, source_target_pairs={{0,1},{1,0},{2,3},{3,2},{4,5},{5,4},{6,7},{7,6},{8,9},{9,8},{10,11... | collective-permute-start | bytes 7077896 | tf_op jit(solution)/shard_map/ppermute | solution.py:992
  103.1 34.1 %collective-permute-start.10 = (bf16[4,16,4608]{2,1,0:T(8,128)(2,1)}, bf16[4,16,4608]{2,1,0:T(8,128)(2,1)S(1)}, u32[]{:S(2)}, u32[]{:S(2)}) collective-permute-start(bf16[4,16,4608]{2,1,0:T(8,128)(2,1)} %get-tuple-element.110), channel_id=1, source_target_pairs={{0,6},{1,7},{2,4},{3,5},{4,2},{5,3},{6,0},{7,1},{8,14},{9,15},{10,... | collective-permute-start | bytes 1769480 | tf_op jit(solution)/shard_map/ppermute | solution.py:992
  105.2 33.0 %collective-permute-start.9 = (bf16[4,16,4608]{2,1,0:T(8,128)(2,1)S(1)}, bf16[4,16,4608]{2,1,0:T(8,128)(2,1)}, u32[]{:S(2)}, u32[]{:S(2)}) collective-permute-start(bf16[4,16,4608]{2,1,0:T(8,128)(2,1)S(1)} %get-tuple-element.111), channel_id=1, source_target_pairs={{0,2},{1,3},{2,0},{3,1},{4,6},{5,7},{6,4},{7,5},{8,10},{9,11},{10,... | collective-permute-start | bytes 1769480 | tf_op jit(solution)/shard_map/ppermute | solution.py:992
  105.7 35.4 %collective-permute-start.8 = (bf16[4,16,4608]{2,1,0:T(8,128)(2,1)S(1)}, bf16[4,16,4608]{2,1,0:T(8,128)(2,1)}, u32[]{:S(2)}, u32[]{:S(2)}) collective-permute-start(bf16[4,16,4608]{2,1,0:T(8,128)(2,1)S(1)} %get-tuple-element.112), channel_id=1, source_target_pairs={{0,4},{1,5},{2,6},{3,7},{4,0},{5,1},{6,2},{7,3},{8,12},{9,13},{10,... | collective-permute-start | bytes 1769480 | tf_op jit(solution)/shard_map/ppermute | solution.py:992
  106.6 40.6 %all-to-all-start.1 = ((bf16[8,128,512]{2,1,0:T(8,128)(2,1)}), bf16[8,128,512]{2,1,0:T(8,128)(2,1)S(1)}, u32[]{:S(2)}, u32[]{:S(2)}) async-start(bf16[8,128,512]{2,1,0:T(8,128)(2,1)} %bitcast.19), calls=%async_computation.1 | async-start | bytes 2097152 | tf_op jit(solution)/shard_map/all_to_all | solution.py:874
  142.7 15.9 %collective-permute-start.13 = (bf16[1,16,4608]{2,1,0:T(8,128)(2,1)S(1)}, bf16[1,16,4608]{2,1,0:T(8,128)(2,1)S(1)}, u32[]{:S(2)}, u32[]{:S(2)}) collective-permute-start(bf16[1,16,4608]{2,1,0:T(8,128)(2,1)S(1)} %get-tuple-element.128), channel_id=1, source_target_pairs={{0,24},{1,25},{2,26},{3,27},{4,28},{5,29},{6,30},{7,31},{8,16},{9,... | collective-permute-start | bytes 442376 | tf_op jit(solution)/shard_map/ppermute | solution.py:992
  143.8 14.9 %collective-permute-start.12 = (bf16[1,16,4608]{2,1,0:T(8,128)(2,1)S(1)}, bf16[1,16,4608]{2,1,0:T(8,128)(2,1)S(1)}, u32[]{:S(2)}, u32[]{:S(2)}) collective-permute-start(bf16[1,16,4608]{2,1,0:T(8,128)(2,1)S(1)} %get-tuple-element.129), channel_id=1, source_target_pairs={{0,16},{1,17},{2,18},{3,19},{4,20},{5,21},{6,22},{7,23},{8,24},{9,... | collective-permute-start | bytes 442376 | tf_op jit(solution)/shard_map/ppermute | solution.py:992
  143.8 14.9 %collective-permute-start.11 = (bf16[1,16,4608]{2,1,0:T(8,128)(2,1)S(1)}, bf16[1,16,4608]{2,1,0:T(8,128)(2,1)S(1)}, u32[]{:S(2)}, u32[]{:S(2)}) collective-permute-start(bf16[1,16,4608]{2,1,0:T(8,128)(2,1)S(1)} %get-tuple-element.130), channel_id=1, source_target_pairs={{0,8},{1,9},{2,10},{3,11},{4,12},{5,13},{6,14},{7,15},{8,0},{9,1},... | collective-permute-start | bytes 442376 | tf_op jit(solution)/shard_map/ppermute | solution.py:992
  163.0 9.5 %collective-permute-start.17 = (bf16[4,16,1792]{2,1,0:T(8,128)(2,1)S(1)}, bf16[4,16,1792]{2,1,0:T(8,128)(2,1)S(1)}, u32[]{:S(2)}, u32[]{:S(2)}) collective-permute-start(bf16[4,16,1792]{2,1,0:T(8,128)(2,1)S(1)} %get-tuple-element.124), channel_id=1, source_target_pairs={{0,6},{1,7},{2,4},{3,5},{4,2},{5,3},{6,0},{7,1},{8,14},{9,15},{10,... | collective-permute-start | bytes 688136 | tf_op jit(solution)/shard_map/ppermute | solution.py:992
  165.2 11.1 %collective-permute-start.16 = (bf16[4,16,1792]{2,1,0:T(8,128)(2,1)S(1)}, bf16[4,16,1792]{2,1,0:T(8,128)(2,1)S(1)}, u32[]{:S(2)}, u32[]{:S(2)}) collective-permute-start(bf16[4,16,1792]{2,1,0:T(8,128)(2,1)S(1)} %get-tuple-element.125), channel_id=1, source_target_pairs={{0,2},{1,3},{2,0},{3,1},{4,6},{5,7},{6,4},{7,5},{8,10},{9,11},{10,... | collective-permute-start | bytes 688136 | tf_op jit(solution)/shard_map/ppermute | solution.py:992
  165.7 10.8 %collective-permute-start.15 = (bf16[4,16,1792]{2,1,0:T(8,128)(2,1)S(1)}, bf16[4,16,1792]{2,1,0:T(8,128)(2,1)S(1)}, u32[]{:S(2)}, u32[]{:S(2)}) collective-permute-start(bf16[4,16,1792]{2,1,0:T(8,128)(2,1)S(1)} %get-tuple-element.126), channel_id=1, source_target_pairs={{0,4},{1,5},{2,6},{3,7},{4,0},{5,1},{6,2},{7,3},{8,12},{9,13},{10,... | collective-permute-start | bytes 688136 | tf_op jit(solution)/shard_map/ppermute | solution.py:992
  166.6 10.2 %collective-permute-start.18 = (bf16[1,16,4608]{2,1,0:T(8,128)(2,1)S(1)}, bf16[1,16,4608]{2,1,0:T(8,128)(2,1)S(1)}, u32[]{:S(2)}, u32[]{:S(2)}) collective-permute-start(bf16[1,16,4608]{2,1,0:T(8,128)(2,1)S(1)} %add_convert_fusion.2.refs_0_), channel_id=1, source_target_pairs={{0,8},{1,9},{2,10},{3,11},{4,12},{5,13},{6,14},{7,15},{8,0},{9,1},... | collective-permute-start | bytes 442376 | tf_op jit(solution)/shard_map/ppermute | solution.py:992
  166.6 13.7 %collective-permute-start.19 = (bf16[1,16,4608]{2,1,0:T(8,128)(2,1)S(1)}, bf16[1,16,4608]{2,1,0:T(8,128)(2,1)S(1)}, u32[]{:S(2)}, u32[]{:S(2)}) collective-permute-start(bf16[1,16,4608]{2,1,0:T(8,128)(2,1)S(1)} %add_convert_fusion.2.refs_0_), channel_id=1, source_target_pairs={{0,16},{1,17},{2,18},{3,19},{4,20},{5,21},{6,22},{7,23},{8,24},{9,... | collective-permute-start | bytes 442376 | tf_op jit(solution)/shard_map/ppermute | solution.py:992
  172.5 7.8 %collective-permute-start.20 = (bf16[1,16,4608]{2,1,0:T(8,128)(2,1)S(1)}, bf16[1,16,4608]{2,1,0:T(8,128)(2,1)S(1)}, u32[]{:S(2)}, u32[]{:S(2)}) collective-permute-start(bf16[1,16,4608]{2,1,0:T(8,128)(2,1)S(1)} %add_convert_fusion.2.refs_0_), channel_id=1, source_target_pairs={{0,24},{1,25},{2,26},{3,27},{4,28},{5,29},{6,30},{7,31},{8,16},{9,... | collective-permute-start | bytes 442376 | tf_op jit(solution)/shard_map/ppermute | solution.py:992
  181.9 7.8 %collective-permute-start.22 = (bf16[4,16,2304]{2,1,0:T(8,128)(2,1)S(1)}, bf16[4,16,2304]{2,1,0:T(8,128)(2,1)S(1)}, u32[]{:S(2)}, u32[]{:S(2)}) collective-permute-start(bf16[4,16,2304]{2,1,0:T(8,128)(2,1)S(1)} %get-tuple-element.91.refs_0_), channel_id=1, source_target_pairs={{0,4},{1,5},{2,6},{3,7},{4,0},{5,1},{6,2},{7,3},{8,12},{9,13},{10,... | collective-permute-start | bytes 884744 | tf_op jit(solution)/shard_map/ppermute | solution.py:992
  182.8 7.5 %collective-permute-start.25 = (bf16[1,16,1792]{2,1,0:T(8,128)(2,1)S(1)}, bf16[1,16,1792]{2,1,0:T(8,128)(2,1)S(1)}, u32[]{:S(2)}, u32[]{:S(2)}) collective-permute-start(bf16[1,16,1792]{2,1,0:T(8,128)(2,1)S(1)} %get-tuple-element.134), channel_id=1, source_target_pairs={{0,24},{1,25},{2,26},{3,27},{4,28},{5,29},{6,30},{7,31},{8,16},{9,... | collective-permute-start | bytes 172040 | tf_op jit(solution)/shard_map/ppermute | solution.py:992
  183.9 7.0 %collective-permute-start.24 = (bf16[1,16,1792]{2,1,0:T(8,128)(2,1)S(1)}, bf16[1,16,1792]{2,1,0:T(8,128)(2,1)S(1)}, u32[]{:S(2)}, u32[]{:S(2)}) collective-permute-start(bf16[1,16,1792]{2,1,0:T(8,128)(2,1)S(1)} %get-tuple-element.135), channel_id=1, source_target_pairs={{0,16},{1,17},{2,18},{3,19},{4,20},{5,21},{6,22},{7,23},{8,24},{9,... | collective-permute-start | bytes 172040 | tf_op jit(solution)/shard_map/ppermute | solution.py:992
  187.3 14.0 %collective-permute-start.29 = (bf16[8,16,2304]{2,1,0:T(8,128)(2,1)S(1)}, bf16[8,16,2304]{2,1,0:T(8,128)(2,1)S(1)}, u32[]{:S(2)}, u32[]{:S(2)}) collective-permute-start(bf16[8,16,2304]{2,1,0:T(8,128)(2,1)S(1)} %shard_map.245.refs_0_), channel_id=1, source_target_pairs={{0,4},{1,5},{2,6},{3,7},{4,0},{5,1},{6,2},{7,3},{8,12},{9,13},{10,... | collective-permute-start | bytes 1769480 | tf_op jit(solution)/shard_map/ppermute | solution.py:992
  189.7 11.6 %collective-permute-start.30 = (bf16[8,16,2304]{2,1,0:T(8,128)(2,1)S(1)}, bf16[8,16,2304]{2,1,0:T(8,128)(2,1)S(1)}, u32[]{:S(2)}, u32[]{:S(2)}) collective-permute-start(bf16[8,16,2304]{2,1,0:T(8,128)(2,1)S(1)} %shard_map.246.refs_2_), channel_id=1, source_target_pairs={{0,2},{1,3},{2,0},{3,1},{4,6},{5,7},{6,4},{7,5},{8,10},{9,11},{10,... | collective-permute-start | bytes 1769480 | tf_op jit(solution)/shard_map/ppermute | solution.py:992
  201.4 10.3 %collective-permute-start.31 = (bf16[16,16,4608]{2,1,0:T(8,128)(2,1)S(1)}, bf16[16,16,4608]{2,1,0:T(8,128)(2,1)}, u32[]{:S(2)}, u32[]{:S(2)}) collective-permute-start(bf16[16,16,4608]{2,1,0:T(8,128)(2,1)S(1)} %shard_map.248.own_ref), channel_id=1, source_target_pairs={{0,1},{1,0},{2,3},{3,2},{4,5},{5,4},{6,7},{7,6},{8,9},{9,8},{10,11... | collective-permute-start | bytes 7077896 | tf_op jit(solution)/shard_map/ppermute | solution.py:992
  201.5 33.1 %all-to-all-start.2 = ((bf16[8,128,512]{2,1,0:T(8,128)(2,1)}), bf16[8,128,512]{2,1,0:T(8,128)(2,1)S(1)}, u32[]{:S(2)}, u32[]{:S(2)}) async-start(bf16[8,128,512]{2,1,0:T(8,128)(2,1)} %bitcast.57), calls=%async_computation.2 | async-start | bytes 2097152 | tf_op jit(solution)/shard_map/all_to_all | solution.py:874
  208.2 24.1 %collective-permute-start.32 = (bf16[4,16,1792]{2,1,0:T(8,128)(2,1)}, bf16[4,16,1792]{2,1,0:T(8,128)(2,1)S(1)}, u32[]{:S(2)}, u32[]{:S(2)}) collective-permute-start(bf16[4,16,1792]{2,1,0:T(8,128)(2,1)} %copy-done), channel_id=1, source_target_pairs={{0,4},{1,5},{2,6},{3,7},{4,0},{5,1},{6,2},{7,3},{8,12},{9,13},{10,... | collective-permute-start | bytes 688136 | tf_op jit(solution)/shard_map/ppermute | solution.py:992
  210.2 22.0 %collective-permute-start.33 = (bf16[4,16,1792]{2,1,0:T(8,128)(2,1)}, bf16[4,16,1792]{2,1,0:T(8,128)(2,1)S(1)}, u32[]{:S(2)}, u32[]{:S(2)}) collective-permute-start(bf16[4,16,1792]{2,1,0:T(8,128)(2,1)} %copy-done), channel_id=1, source_target_pairs={{0,2},{1,3},{2,0},{3,1},{4,6},{5,7},{6,4},{7,5},{8,10},{9,11},{10,... | collective-permute-start | bytes 688136 | tf_op jit(solution)/shard_map/ppermute | solution.py:992
  211.4 20.8 %collective-permute-start.34 = (bf16[4,16,1792]{2,1,0:T(8,128)(2,1)}, bf16[4,16,1792]{2,1,0:T(8,128)(2,1)S(1)}, u32[]{:S(2)}, u32[]{:S(2)}) collective-permute-start(bf16[4,16,1792]{2,1,0:T(8,128)(2,1)} %copy-done), channel_id=1, source_target_pairs={{0,6},{1,7},{2,4},{3,5},{4,2},{5,3},{6,0},{7,1},{8,14},{9,15},{10,... | collective-permute-start | bytes 688136 | tf_op jit(solution)/shard_map/ppermute | solution.py:992
  (19 other events, 196.0 us)

commit v5 on v4

--- a/solution.py
+++ b/solution.py
@@ -278,7 +278,7 @@
         window = [pl.ds(at + s * TILE, 2 * TILE) for s in near_by]
         masks = [tile_masks(meta_ref, first + s) for s in near_by]
         q = {(s, p): q_ref[here[s], pair_lanes(p)] for s, p in units}
-        go = {(s, p): go_ref[here[s], pair_lanes(p)] for s, p in units}
+        go = {(s, p): go_ref[here[s], pair_lanes(p)].astype(F32) for s, p in units}
         blend = [[blend_at(c, p) for c in range(3)] for p in pairs]
         fqs = {(s, p): [load_split(fq, (c,), here[s], p) for c in range(2)] for s, p in units}
         feats = {u: [whole(f) for f in fqs[u]] for u in units}
@@ -617,7 +617,7 @@
     pieces, place_ref, x_ref, att_ref, grad_ref, out_from, gain_ref, bias_ref, in_from, in_b,
     down_from, down_b, result_to, first_to, go_to, keep_to, send_to, small_ref, wide_ref,
     second, hidden, pre_low, att_low, att_all, grad_all, out_w, in_w, down_w, keep_ref, send_ref,
-    result_ref, first_ref, go_ref, in_sems, out_sems, row_sems,
+    result_ref, go_ref, in_sems, out_sems, row_sems,
 ):
     chunk, width = x_ref.shape
     inner = in_w.shape[1]
@@ -671,11 +671,10 @@
     small_ref[1:2, :] += column_sum(back)
     small_ref[2:3, :] += column_sum(grad_f)
     grad_first = grad_f + norm_back(back * gain_ref[...], unit, scale)
-    first_ref[here, :] = grad_first
     grad_att = grad_first.astype(BF16)
     att_low[here, :] = grad_att
-    go_ref[here, :] = times_transposed(grad_att, out_w[...])
-    pairs = ((result_ref, result_to), (first_ref, first_to), (go_ref, go_to))
+    go_ref[here, :] = times_transposed(grad_att, out_w[...]).astype(BF16)
+    pairs = ((result_ref, result_to), (att_low, first_to), (go_ref, go_to))
     done = [
         pltpu.make_async_copy(inside.at[here, :], outside.at[here, :], row_sems.at[number, i])
         for i, (inside, outside) in enumerate(pairs)
@@ -745,15 +744,15 @@
     rows, width = x.shape
     inner = in_w.shape[1]
     packed = (width // 2, 2 * inner + width)
-    size = min(CHUNK, rows)
+    size = min(2 * CHUNK, rows)
     block, far = by_rows(size, width), pl.BlockSpec(memory_space=pl.ANY)
     return pl.pallas_call(
         functools.partial(feed_kernel, pieces),
         grid=(rows // size,),
         out_shape=(
             jax.ShapeDtypeStruct((rows, width), BF16),
-            jax.ShapeDtypeStruct((rows, width), F32),
-            jax.ShapeDtypeStruct((rows, width), F32),
+            jax.ShapeDtypeStruct((rows, width), BF16),
+            jax.ShapeDtypeStruct((rows, width), BF16),
             jax.ShapeDtypeStruct(packed, BF16),
             jax.ShapeDtypeStruct(packed, BF16),
             jax.ShapeDtypeStruct((3, width), F32),
@@ -778,8 +777,7 @@
             pltpu.VMEM(packed, BF16),
             pltpu.VMEM(packed, BF16),
             pltpu.VMEM((rows, width), BF16),
-            pltpu.VMEM((rows, width), F32),
-            pltpu.VMEM((rows, width), F32),
+            pltpu.VMEM((rows, width), BF16),
             pltpu.SemaphoreType.DMA((1 + 2 * inner // width,)),
             pltpu.SemaphoreType.DMA((4 + 2 * inner // width,)),
             pltpu.SemaphoreType.DMA((rows // size, 3)),
@@ -809,7 +807,7 @@
     back = times_transposed(grad, w_ref[...])
     sums[0:1, :] += column_sum(back * unit)
     sums[1:2, :] += column_sum(back)
-    grad_x = first_ref[...] + norm_back(back * gain_ref[...], unit, scale)
+    grad_x = first_ref[...].astype(F32) + norm_back(back * gain_ref[...], unit, scale)
     result_ref[...] = grad_x.astype(BF16)
 
     @pl.when(number == pl.num_programs(0) - 1)

time: 243 us -> 240 us (0.988)
  transfers between devices with their start and end apart: 39 -> 39, of which waited for: 18 -> 16; matrix products, arithmetic and copies ran while one was open for 1% -> 1% of each run, Pallas kernels for 33% -> 33%
where the time goes in v5:
time: 240 us; the launch traced here: 236 us
  Pallas kernels  107 us (45%)
  starting transfers between devices  61.8 us (26%)
  waiting for transfers between devices  56.5 us (24%)
  local copies, waits for them, and re-layouts  4.98 us (2%)
  other arithmetic  4.65 us (2%)
    ppermute x29, waiting for transfers between devices, swap(): return lax.ppermute(value, ('seq', 'batch'), route)  37.6 us
    pallas_call x2, Pallas kernels, attend_back(): pl.pallas_call(functools.partial(attend_back_kernel, together(rows, lanes...  37.2 us
    ppermute x29, starting transfers between devices, swap(): return lax.ppermute(value, ('seq', 'batch'), route)  32 us
    pallas_call x1, Pallas kernels, feed_forward(): pl.pallas_call(functools.partial(feed_kernel, pieces), grid=(rows // size...  26.4 us
    all_to_all x3, starting transfers between devices, to_sequences(): return lax.all_to_all(block, axis, 0, 0, axis_index_groups=groups)  16.7 us
    pallas_call x1, Pallas kernels, attend(): pl.pallas_call(functools.partial(attend_kernel, together(rows, lanes), st...  15.9 us
    ppermute x7, waiting for transfers between devices, spans_of(): spans.append(lax.ppermute(span, axis, route) if k else span)  13.9 us
    ppermute x7, starting transfers between devices, spans_of(): spans.append(lax.ppermute(span, axis, route) if k else span)  13.1 us
  transfers between devices with their start and end apart: 39, of which 16 were waited for; matrix products, arithmetic and copies ran while one was open for 1% of the time, Pallas kernels for 33%

profile of v5, /device:TPU:0, one launch (start us, length us, event | category | flops | bytes accessed | tf_op | source)
XLA Modules:
  0.0 236.1 jit_solution(9831859377950680409)
XLA Ops:
  0.7 2.0 dynamic-slice_bitcast_fusion.8
  2.7 3.0 %collective-permute-start = (bf16[128,512]{1,0:T(8,128)(2,1)S(1)}, bf16[128,512]{1,0:T(8,128)(2,1)S(1)}, u32[]{:S(2)}, u32[]{:S(2)}) collective-permute-start(bf16[128,512]{1,0:T(8,128)(2,1)S(1)} %get-tuple-element.120), channel_id=1, source_target_pairs={{0,4},{4,0},{8,12},{12,8},{16,20},{20,16},{24,28},{28,24},{1,5},{5... | collective-permute-start | bytes 393224 | tf_op jit(solution)/shard_map/ppermute | solution.py:881
  7.3 3.0 %collective-permute-start.3 = (bf16[128,512]{1,0:T(8,128)(2,1)S(1)}, bf16[128,512]{1,0:T(8,128)(2,1)S(1)}, u32[]{:S(2)}, u32[]{:S(2)}) collective-permute-start(bf16[128,512]{1,0:T(8,128)(2,1)S(1)} %get-tuple-element.117), channel_id=1, source_target_pairs={{0,16},{4,20},{8,24},{12,28},{16,0},{20,4},{24,8},{28,12},{1,17},{... | collective-permute-start | bytes 393224 | tf_op jit(solution)/shard_map/ppermute | solution.py:881
  11.5 3.6 %collective-permute-start.5 = (bf16[128,512]{1,0:T(8,128)(2,1)S(1)}, bf16[128,512]{1,0:T(8,128)(2,1)S(1)}, u32[]{:S(2)}, u32[]{:S(2)}) collective-permute-start(bf16[128,512]{1,0:T(8,128)(2,1)S(1)} %get-tuple-element.122), channel_id=1, source_target_pairs={{0,24},{4,28},{8,16},{12,20},{16,8},{20,12},{24,0},{28,4},{1,25},{... | collective-permute-start | bytes 393224 | tf_op jit(solution)/shard_map/ppermute | solution.py:881
  17.1 12.6 %collective-permute-done.4.refs_5_ = bf16[128,512]{1,0:T(8,128)(2,1)S(1)} collective-permute-done((bf16[128,512]{1,0:T(8,128)(2,1)S(1)}, bf16[128,512]{1,0:T(8,128)(2,1)S(1)}, u32[]{:S(2)}, u32[]{:S(2)}) %collective-permute-start.4) | collective-permute-done | bytes 131104 | tf_op jit(solution)/shard_map/ppermute | solution.py:881
  29.7 7.8 %all-to-all-start = ((bf16[8,128,512]{2,1,0:T(8,128)(2,1)}), bf16[8,128,512]{2,1,0:T(8,128)(2,1)S(1)}, u32[]{:S(2)}, u32[]{:S(2)}) async-start(bf16[8,128,512]{2,1,0:T(8,128)(2,1)} %param.15), calls=%async_computation | async-start | bytes 2097152 | tf_op jit(solution)/shard_map/all_to_all | solution.py:872
  38.2 5.6 %shard_map.237 = (bf16[1024,512]{1,0:T(8,128)(2,1)}, bf16[1024,1536]{1,0:T(8,128)(2,1)}) custom-call(s32[4]{0:T(128)} %pad_add_fusion.place_ref, bf16[512,1536]{1,0:T(8,128)(2,1)} %w_ref.3, f32[1,512]{1,0:T(1,128)} %bitcast.62, f32[1,512]{1,0:T(1,128)} %bitcast.64, bf16[128,512]{1,0:T(8,128)(2,1)} %get-tuple-element.121.refs_0_, bf16[128,512]{1,0:T(8,128)(2,1)} %copy-done.5, ...), custom_call_target="tpu_custom_call" | custom-call | flops 1000 | bytes 1000 | tf_op jit(solution)/shard_map/pallas_call | solution.py:586
  43.8 15.9 %shard_map.238.att_ref = bf16[1024,512]{1,0:T(8,128)(2,1)} custom-call(s32[4]{0:T(128)} %pad_add_fusion.place_ref, s32[8]{0:T(128)} %lengths_ref.5, f32[3,8]{1,0:T(4,128)} %blend_ref.5, bf16[1024,1536]{1,0:T(8,128)(2,1)} %get-tuple-element.62.q_ref.k_ref.v_ref, bf16[1024,1536]{1,0:T(8,128)(2,1)} %get-tuple-element.62.q_ref.k_ref.v_ref, ...), custom_call_target="tpu_custom_call" | custom-call | flops 1000 | bytes 1000 | tf_op jit(solution)/shard_map/pallas_call | solution.py:485
  59.7 2.8 %all-to-all-done = bf16[8,128,512]{2,1,0:T(8,128)(2,1)S(1)} async-done(((bf16[8,128,512]{2,1,0:T(8,128)(2,1)}), bf16[8,128,512]{2,1,0:T(8,128)(2,1)S(1)}, u32[]{:S(2)}, u32[]{:S(2)}) %all-to-all-start) | async-done | bytes 1048608 | tf_op jit(solution)/shard_map/all_to_all | solution.py:872
  63.4 26.4 %shard_map.239 = (bf16[1024,512]{1,0:T(8,128)(2,1)}, bf16[1024,512]{1,0:T(8,128)(2,1)}, bf16[1024,512]{1,0:T(8,128)(2,1)}, bf16[256,4608]{1,0:T(8,128)(2,1)}, bf...) custom-call(s32[4]{0:T(128)} %pad_add_fusion.place_ref, bf16[1024,512]{1,0:T(8,128)(2,1)} %get-tuple-element.61.x_ref, ...), custom_call_target="tpu_custom_call" | custom-call | flops 1000 | bytes 1000 | tf_op jit(solution)/shard_map/pallas_call | solution.py:749
  90.0 10.3 %shard_map.240 = (bf16[1024,128]{1,0:T(8,128)(2,1)}, bf16[1024,128]{1,0:T(8,128)(2,1)}, bf16[1024,128]{1,0:T(8,128)(2,1)}, f32[3,128]{1,0:T(4,128)}) custom-call(s32[4]{0:T(128)} %pad_add_fusion.place_ref, s32[8]{0:T(128)} %lengths_ref.5, f32[3,8]{1,0:T(4,128)} %blend_ref.5, bf16[1024,1536]{1,0:T(8,128)(2,1)} %get-tuple-element.62.q_ref.k_ref.v_ref, ...), custom_call_target="tpu_custom_call" | custom-call | flops 1000 | bytes 1000 | tf_op jit(solution)/shard_map/pallas_call | solution.py:521
  102.1 2.1 collective-permute-start.10
  105.6 3.7 %all-to-all-start.1 = ((bf16[8,128,512]{2,1,0:T(8,128)(2,1)}), bf16[8,128,512]{2,1,0:T(8,128)(2,1)S(1)}, u32[]{:S(2)}, u32[]{:S(2)}) async-start(bf16[8,128,512]{2,1,0:T(8,128)(2,1)} %bitcast.19), calls=%async_computation.1 | async-start | bytes 2097152 | tf_op jit(solution)/shard_map/all_to_all | solution.py:872
  109.3 26.9 %shard_map.241 = (bf16[1024,384]{1,0:T(8,128)(2,1)}, bf16[1024,384]{1,0:T(8,128)(2,1)}, bf16[1024,384]{1,0:T(8,128)(2,1)}, f32[3,384]{1,0:T(4,128)}) custom-call(s32[4]{0:T(128)} %pad_add_fusion.place_ref, s32[8]{0:T(128)} %lengths_ref.5, f32[3,8]{1,0:T(4,128)} %blend_ref.5, bf16[1024,1536]{1,0:T(8,128)(2,1)} %get-tuple-element.62.q_ref.k_ref.v_ref, ...), custom_call_target="tpu_custom_call" | custom-call | flops 1000 | bytes 1000 | tf_op jit(solution)/shard_map/pallas_call | solution.py:521
  136.2 3.9 %collective-permute-done.8 = bf16[4,16,4608]{2,1,0:T(8,128)(2,1)} collective-permute-done((bf16[4,16,4608]{2,1,0:T(8,128)(2,1)S(1)}, bf16[4,16,4608]{2,1,0:T(8,128)(2,1)}, u32[]{:S(2)}, u32[]{:S(2)}) %collective-permute-start.8) | collective-permute-done | bytes 589856 | tf_op jit(solution)/shard_map/ppermute | solution.py:990
  143.4 2.8 %collective-permute-start.13 = (bf16[1,16,4608]{2,1,0:T(8,128)(2,1)S(1)}, bf16[1,16,4608]{2,1,0:T(8,128)(2,1)S(1)}, u32[]{:S(2)}, u32[]{:S(2)}) collective-permute-start(bf16[1,16,4608]{2,1,0:T(8,128)(2,1)S(1)} %get-tuple-element.128), channel_id=1, source_target_pairs={{0,24},{1,25},{2,26},{3,27},{4,28},{5,29},{6,30},{7,31},{8,16},{9,... | collective-permute-start | bytes 442376 | tf_op jit(solution)/shard_map/ppermute | solution.py:990
  147.2 10.0 %shard_map.243 = (bf16[1024,512]{1,0:T(8,128)(2,1)}, bf16[256,1792]{1,0:T(8,128)(2,1)}, bf16[256,1792]{1,0:T(8,128)(2,1)}) custom-call(s32[4]{0:T(128)} %pad_add_fusion.place_ref, bf16[1024,512]{1,0:T(8,128)(2,1)} %get-tuple-element.61.x_ref, bf16[1024,512]{1,0:T(8,128)(2,1)} %get-tuple-element.75.first_ref, bf16[512,1536]{1,0:T(8,128)(2,1)} %w_ref.3, ...), custom_call_target="tpu_custom_call" | custom-call | flops 1000 | bytes 1000 | tf_op jit(solution)/shard_map/pallas_call | solution.py:850
  157.4 2.6 %collective-permute-done.14 = bf16[16,16,1792]{2,1,0:T(8,128)(2,1)S(1)} collective-permute-done((bf16[16,16,1792]{2,1,0:T(8,128)(2,1)}, bf16[16,16,1792]{2,1,0:T(8,128)(2,1)S(1)}, u32[]{:S(2)}, u32[]{:S(2)}) %collective-permute-start.14) | collective-permute-done | bytes 917536 | tf_op jit(solution)/shard_map/ppermute | solution.py:990
  165.2 1.6 collective-permute-start.19
  166.9 2.5 %collective-permute-done.15 = bf16[4,16,1792]{2,1,0:T(8,128)(2,1)S(1)} collective-permute-done((bf16[4,16,1792]{2,1,0:T(8,128)(2,1)S(1)}, bf16[4,16,1792]{2,1,0:T(8,128)(2,1)S(1)}, u32[]{:S(2)}, u32[]{:S(2)}) %collective-permute-start.15) | collective-permute-done | bytes 229408 | tf_op jit(solution)/shard_map/ppermute | solution.py:990
  171.4 4.1 %collective-permute-done.17 = bf16[4,16,1792]{2,1,0:T(8,128)(2,1)S(1)} collective-permute-done((bf16[4,16,1792]{2,1,0:T(8,128)(2,1)S(1)}, bf16[4,16,1792]{2,1,0:T(8,128)(2,1)S(1)}, u32[]{:S(2)}, u32[]{:S(2)}) %collective-permute-start.17) | collective-permute-done | bytes 229408 | tf_op jit(solution)/shard_map/ppermute | solution.py:990
  175.7 3.3 %collective-permute-done.19.refs_2_ = bf16[1,16,4608]{2,1,0:T(8,128)(2,1)S(1)} collective-permute-done((bf16[1,16,4608]{2,1,0:T(8,128)(2,1)S(1)}, bf16[1,16,4608]{2,1,0:T(8,128)(2,1)S(1)}, u32[]{:S(2)}, u32[]{:S(2)}) %collective-permute-start.19) | collective-permute-done | bytes 147488 | tf_op jit(solution)/shard_map/ppermute | solution.py:990
  181.8 2.3 collective-permute-start.23
  184.2 2.4 %collective-permute-start.25 = (bf16[1,16,1792]{2,1,0:T(8,128)(2,1)S(1)}, bf16[1,16,1792]{2,1,0:T(8,128)(2,1)S(1)}, u32[]{:S(2)}, u32[]{:S(2)}) collective-permute-start(bf16[1,16,1792]{2,1,0:T(8,128)(2,1)S(1)} %get-tuple-element.134), channel_id=1, source_target_pairs={{0,24},{1,25},{2,26},{3,27},{4,28},{5,29},{6,30},{7,31},{8,16},{9,... | collective-permute-start | bytes 172040 | tf_op jit(solution)/shard_map/ppermute | solution.py:990
  195.1 2.5 %collective-permute-done.27.refs_2_ = bf16[1,16,1792]{2,1,0:T(8,128)(2,1)S(1)} collective-permute-done((bf16[1,16,1792]{2,1,0:T(8,128)(2,1)S(1)}, bf16[1,16,1792]{2,1,0:T(8,128)(2,1)S(1)}, u32[]{:S(2)}, u32[]{:S(2)}) %collective-permute-start.27) | collective-permute-done | bytes 57376 | tf_op jit(solution)/shard_map/ppermute | solution.py:990
  197.6 1.8 collective-permute-done.28.refs_3_
  200.4 5.1 %all-to-all-start.2 = ((bf16[8,128,512]{2,1,0:T(8,128)(2,1)}), bf16[8,128,512]{2,1,0:T(8,128)(2,1)S(1)}, u32[]{:S(2)}, u32[]{:S(2)}) async-start(bf16[8,128,512]{2,1,0:T(8,128)(2,1)} %bitcast.57), calls=%async_computation.2 | async-start | bytes 2097152 | tf_op jit(solution)/shard_map/all_to_all | solution.py:872
  205.5 2.0 collective-permute-start.32
  209.1 6.5 %shard_map.249 = (f32[512,2048]{1,0:T(8,128)}, f32[512,512]{1,0:T(8,128)}, f32[2048,512]{1,0:T(8,128)}) custom-call(s32[4]{0:T(128)S(1)} %copy-done.2, bf16[16,16,4608]{2,1,0:T(8,128)(2,1)S(1)} %shard_map.248.own_ref, bf16[16,16,4608]{2,1,0:T(8,128)(2,1)} %collective-permute-done.31.other_ref), custom_call_target="tpu_custom_call" | custom-call | flops 1000 | bytes 1000 | tf_op jit(solution)/shard_map/pallas_call | solution.py:1101
  215.5 14.0 %collective-permute-done.32.refs_1_ = bf16[4,16,1792]{2,1,0:T(8,128)(2,1)S(1)} collective-permute-done((bf16[4,16,1792]{2,1,0:T(8,128)(2,1)}, bf16[4,16,1792]{2,1,0:T(8,128)(2,1)S(1)}, u32[]{:S(2)}, u32[]{:S(2)}) %collective-permute-start.32) | collective-permute-done | bytes 229408 | tf_op jit(solution)/shard_map/ppermute | solution.py:990
  229.7 2.2 all-to-all-done.2.source_ref
  233.0 2.9 %shard_map.252 = (f32[512,1536]{1,0:T(8,128)}, f32[512]{0:T(512)}, f32[512]{0:T(512)}, f32[512]{0:T(512)}, f32[512]{0:T(512)}, /*index=5*/f32[512]{0:T(512)}, f32[2048]{0:T(1024)}, f32[3,8]{1,0:T(4,128)}) custom-call(s32[4]{0:T(128)S(1)} %copy-done.2, bf16[16,16,1792]{2,1,0:T(8,128)(2,1)S(1)} %shard_map.250.own_ref, ...), custom_call_target="tpu_custom_call" | custom-call | flops 1000 | bytes 1000 | tf_op jit(solution)/shard_map/pallas_call | solution.py:1101
  (107 shorter events, 36.5 us)
Async XLA Ops:
  2.7 8.8 %collective-permute-start = (bf16[128,512]{1,0:T(8,128)(2,1)S(1)}, bf16[128,512]{1,0:T(8,128)(2,1)S(1)}, u32[]{:S(2)}, u32[]{:S(2)}) collective-permute-start(bf16[128,512]{1,0:T(8,128)(2,1)S(1)} %get-tuple-element.120), channel_id=1, source_target_pairs={{0,4},{4,0},{8,12},{12,8},{16,20},{20,16},{24,28},{28,24},{1,5},{5... | collective-permute-start | bytes 393224 | tf_op jit(solution)/shard_map/ppermute | solution.py:881
  5.7 10.7 %collective-permute-start.1 = (bf16[128,512]{1,0:T(8,128)(2,1)S(1)}, bf16[128,512]{1,0:T(8,128)(2,1)S(1)}, u32[]{:S(2)}, u32[]{:S(2)}) collective-permute-start(bf16[128,512]{1,0:T(8,128)(2,1)S(1)} %get-tuple-element.119), channel_id=1, source_target_pairs={{0,8},{4,12},{8,0},{12,4},{16,24},{20,28},{24,16},{28,20},{1,9},{5... | collective-permute-start | bytes 393224 | tf_op jit(solution)/shard_map/ppermute | solution.py:881
  7.3 9.8 %collective-permute-start.2 = (bf16[128,512]{1,0:T(8,128)(2,1)S(1)}, bf16[128,512]{1,0:T(8,128)(2,1)S(1)}, u32[]{:S(2)}, u32[]{:S(2)}) collective-permute-start(bf16[128,512]{1,0:T(8,128)(2,1)S(1)} %get-tuple-element.118), channel_id=1, source_target_pairs={{0,12},{4,8},{8,4},{12,0},{16,28},{20,24},{24,20},{28,16},{1,13},{... | collective-permute-start | bytes 393224 | tf_op jit(solution)/shard_map/ppermute | solution.py:881
  7.3 9.8 %collective-permute-start.3 = (bf16[128,512]{1,0:T(8,128)(2,1)S(1)}, bf16[128,512]{1,0:T(8,128)(2,1)S(1)}, u32[]{:S(2)}, u32[]{:S(2)}) collective-permute-start(bf16[128,512]{1,0:T(8,128)(2,1)S(1)} %get-tuple-element.117), channel_id=1, source_target_pairs={{0,16},{4,20},{8,24},{12,28},{16,0},{20,4},{24,8},{28,12},{1,17},{... | collective-permute-start | bytes 393224 | tf_op jit(solution)/shard_map/ppermute | solution.py:881
  10.2 19.5 %collective-permute-start.4 = (bf16[128,512]{1,0:T(8,128)(2,1)S(1)}, bf16[128,512]{1,0:T(8,128)(2,1)S(1)}, u32[]{:S(2)}, u32[]{:S(2)}) collective-permute-start(bf16[128,512]{1,0:T(8,128)(2,1)S(1)} %get-tuple-element.116), channel_id=1, source_target_pairs={{0,20},{4,16},{8,28},{12,24},{16,4},{20,0},{24,12},{28,8},{1,21},{... | collective-permute-start | bytes 393224 | tf_op jit(solution)/shard_map/ppermute | solution.py:881
  11.5 18.2 %collective-permute-start.5 = (bf16[128,512]{1,0:T(8,128)(2,1)S(1)}, bf16[128,512]{1,0:T(8,128)(2,1)S(1)}, u32[]{:S(2)}, u32[]{:S(2)}) collective-permute-start(bf16[128,512]{1,0:T(8,128)(2,1)S(1)} %get-tuple-element.122), channel_id=1, source_target_pairs={{0,24},{4,28},{8,16},{12,20},{16,8},{20,12},{24,0},{28,4},{1,25},{... | collective-permute-start | bytes 393224 | tf_op jit(solution)/shard_map/ppermute | solution.py:881
  16.4 13.3 %collective-permute-start.6 = (bf16[128,512]{1,0:T(8,128)(2,1)S(1)}, bf16[128,512]{1,0:T(8,128)(2,1)S(1)}, u32[]{:S(2)}, u32[]{:S(2)}) collective-permute-start(bf16[128,512]{1,0:T(8,128)(2,1)S(1)} %get-tuple-element.115), channel_id=1, source_target_pairs={{0,28},{4,24},{8,20},{12,16},{16,12},{20,8},{24,4},{28,0},{1,29},{... | collective-permute-start | bytes 393224 | tf_op jit(solution)/shard_map/ppermute | solution.py:881
  29.7 32.7 %all-to-all-start = ((bf16[8,128,512]{2,1,0:T(8,128)(2,1)}), bf16[8,128,512]{2,1,0:T(8,128)(2,1)S(1)}, u32[]{:S(2)}, u32[]{:S(2)}) async-start(bf16[8,128,512]{2,1,0:T(8,128)(2,1)} %param.15), calls=%async_computation | async-start | bytes 2097152 | tf_op jit(solution)/shard_map/all_to_all | solution.py:872
  89.9 10.4 %collective-permute-start.7 = (bf16[16,16,4608]{2,1,0:T(8,128)(2,1)}, bf16[16,16,4608]{2,1,0:T(8,128)(2,1)S(1)}, u32[]{:S(2)}, u32[]{:S(2)}) collective-permute-start(bf16[16,16,4608]{2,1,0:T(8,128)(2,1)} %bitcast.69), channel_id=1, source_target_pairs={{0,1},{1,0},{2,3},{3,2},{4,5},{5,4},{6,7},{7,6},{8,9},{9,8},{10,11... | collective-permute-start | bytes 7077896 | tf_op jit(solution)/shard_map/ppermute | solution.py:990
  102.1 34.1 %collective-permute-start.10 = (bf16[4,16,4608]{2,1,0:T(8,128)(2,1)}, bf16[4,16,4608]{2,1,0:T(8,128)(2,1)S(1)}, u32[]{:S(2)}, u32[]{:S(2)}) collective-permute-start(bf16[4,16,4608]{2,1,0:T(8,128)(2,1)} %get-tuple-element.110), channel_id=1, source_target_pairs={{0,6},{1,7},{2,4},{3,5},{4,2},{5,3},{6,0},{7,1},{8,14},{9,15},{10,... | collective-permute-start | bytes 1769480 | tf_op jit(solution)/shard_map/ppermute | solution.py:990
  104.2 35.9 %collective-permute-start.8 = (bf16[4,16,4608]{2,1,0:T(8,128)(2,1)S(1)}, bf16[4,16,4608]{2,1,0:T(8,128)(2,1)}, u32[]{:S(2)}, u32[]{:S(2)}) collective-permute-start(bf16[4,16,4608]{2,1,0:T(8,128)(2,1)S(1)} %get-tuple-element.112), channel_id=1, source_target_pairs={{0,4},{1,5},{2,6},{3,7},{4,0},{5,1},{6,2},{7,3},{8,12},{9,13},{10,... | collective-permute-start | bytes 1769480 | tf_op jit(solution)/shard_map/ppermute | solution.py:990
  105.0 35.1 %collective-permute-start.9 = (bf16[4,16,4608]{2,1,0:T(8,128)(2,1)S(1)}, bf16[4,16,4608]{2,1,0:T(8,128)(2,1)}, u32[]{:S(2)}, u32[]{:S(2)}) collective-permute-start(bf16[4,16,4608]{2,1,0:T(8,128)(2,1)S(1)} %get-tuple-element.111), channel_id=1, source_target_pairs={{0,2},{1,3},{2,0},{3,1},{4,6},{5,7},{6,4},{7,5},{8,10},{9,11},{10,... | collective-permute-start | bytes 1769480 | tf_op jit(solution)/shard_map/ppermute | solution.py:990
  105.6 40.6 %all-to-all-start.1 = ((bf16[8,128,512]{2,1,0:T(8,128)(2,1)}), bf16[8,128,512]{2,1,0:T(8,128)(2,1)S(1)}, u32[]{:S(2)}, u32[]{:S(2)}) async-start(bf16[8,128,512]{2,1,0:T(8,128)(2,1)} %bitcast.19), calls=%async_computation.1 | async-start | bytes 2097152 | tf_op jit(solution)/shard_map/all_to_all | solution.py:872
  141.7 15.6 %collective-permute-start.11 = (bf16[1,16,4608]{2,1,0:T(8,128)(2,1)S(1)}, bf16[1,16,4608]{2,1,0:T(8,128)(2,1)S(1)}, u32[]{:S(2)}, u32[]{:S(2)}) collective-permute-start(bf16[1,16,4608]{2,1,0:T(8,128)(2,1)S(1)} %get-tuple-element.130), channel_id=1, source_target_pairs={{0,8},{1,9},{2,10},{3,11},{4,12},{5,13},{6,14},{7,15},{8,0},{9,1},... | collective-permute-start | bytes 442376 | tf_op jit(solution)/shard_map/ppermute | solution.py:990
  141.8 15.5 %collective-permute-start.12 = (bf16[1,16,4608]{2,1,0:T(8,128)(2,1)S(1)}, bf16[1,16,4608]{2,1,0:T(8,128)(2,1)S(1)}, u32[]{:S(2)}, u32[]{:S(2)}) collective-permute-start(bf16[1,16,4608]{2,1,0:T(8,128)(2,1)S(1)} %get-tuple-element.129), channel_id=1, source_target_pairs={{0,16},{1,17},{2,18},{3,19},{4,20},{5,21},{6,22},{7,23},{8,24},{9,... | collective-permute-start | bytes 442376 | tf_op jit(solution)/shard_map/ppermute | solution.py:990
  143.4 14.0 %collective-permute-start.13 = (bf16[1,16,4608]{2,1,0:T(8,128)(2,1)S(1)}, bf16[1,16,4608]{2,1,0:T(8,128)(2,1)S(1)}, u32[]{:S(2)}, u32[]{:S(2)}) collective-permute-start(bf16[1,16,4608]{2,1,0:T(8,128)(2,1)S(1)} %get-tuple-element.128), channel_id=1, source_target_pairs={{0,24},{1,25},{2,26},{3,27},{4,28},{5,29},{6,30},{7,31},{8,16},{9,... | collective-permute-start | bytes 442376 | tf_op jit(solution)/shard_map/ppermute | solution.py:990
  161.7 7.7 %collective-permute-start.15 = (bf16[4,16,1792]{2,1,0:T(8,128)(2,1)S(1)}, bf16[4,16,1792]{2,1,0:T(8,128)(2,1)S(1)}, u32[]{:S(2)}, u32[]{:S(2)}) collective-permute-start(bf16[4,16,1792]{2,1,0:T(8,128)(2,1)S(1)} %get-tuple-element.126), channel_id=1, source_target_pairs={{0,4},{1,5},{2,6},{3,7},{4,0},{5,1},{6,2},{7,3},{8,12},{9,13},{10,... | collective-permute-start | bytes 688136 | tf_op jit(solution)/shard_map/ppermute | solution.py:990
  162.9 8.5 %collective-permute-start.16 = (bf16[4,16,1792]{2,1,0:T(8,128)(2,1)S(1)}, bf16[4,16,1792]{2,1,0:T(8,128)(2,1)S(1)}, u32[]{:S(2)}, u32[]{:S(2)}) collective-permute-start(bf16[4,16,1792]{2,1,0:T(8,128)(2,1)S(1)} %get-tuple-element.125), channel_id=1, source_target_pairs={{0,2},{1,3},{2,0},{3,1},{4,6},{5,7},{6,4},{7,5},{8,10},{9,11},{10,... | collective-permute-start | bytes 688136 | tf_op jit(solution)/shard_map/ppermute | solution.py:990
  164.4 11.1 %collective-permute-start.17 = (bf16[4,16,1792]{2,1,0:T(8,128)(2,1)S(1)}, bf16[4,16,1792]{2,1,0:T(8,128)(2,1)S(1)}, u32[]{:S(2)}, u32[]{:S(2)}) collective-permute-start(bf16[4,16,1792]{2,1,0:T(8,128)(2,1)S(1)} %get-tuple-element.124), channel_id=1, source_target_pairs={{0,6},{1,7},{2,4},{3,5},{4,2},{5,3},{6,0},{7,1},{8,14},{9,15},{10,... | collective-permute-start | bytes 688136 | tf_op jit(solution)/shard_map/ppermute | solution.py:990
  165.2 10.4 %collective-permute-start.18 = (bf16[1,16,4608]{2,1,0:T(8,128)(2,1)S(1)}, bf16[1,16,4608]{2,1,0:T(8,128)(2,1)S(1)}, u32[]{:S(2)}, u32[]{:S(2)}) collective-permute-start(bf16[1,16,4608]{2,1,0:T(8,128)(2,1)S(1)} %add_convert_fusion.2.refs_0_), channel_id=1, source_target_pairs={{0,8},{1,9},{2,10},{3,11},{4,12},{5,13},{6,14},{7,15},{8,0},{9,1},... | collective-permute-start | bytes 442376 | tf_op jit(solution)/shard_map/ppermute | solution.py:990
  165.2 13.8 %collective-permute-start.19 = (bf16[1,16,4608]{2,1,0:T(8,128)(2,1)S(1)}, bf16[1,16,4608]{2,1,0:T(8,128)(2,1)S(1)}, u32[]{:S(2)}, u32[]{:S(2)}) collective-permute-start(bf16[1,16,4608]{2,1,0:T(8,128)(2,1)S(1)} %add_convert_fusion.2.refs_0_), channel_id=1, source_target_pairs={{0,16},{1,17},{2,18},{3,19},{4,20},{5,21},{6,22},{7,23},{8,24},{9,... | collective-permute-start | bytes 442376 | tf_op jit(solution)/shard_map/ppermute | solution.py:990
  169.4 9.6 %collective-permute-start.20 = (bf16[1,16,4608]{2,1,0:T(8,128)(2,1)S(1)}, bf16[1,16,4608]{2,1,0:T(8,128)(2,1)S(1)}, u32[]{:S(2)}, u32[]{:S(2)}) collective-permute-start(bf16[1,16,4608]{2,1,0:T(8,128)(2,1)S(1)} %add_convert_fusion.2.refs_0_), channel_id=1, source_target_pairs={{0,24},{1,25},{2,26},{3,27},{4,28},{5,29},{6,30},{7,31},{8,16},{9,... | collective-permute-start | bytes 442376 | tf_op jit(solution)/shard_map/ppermute | solution.py:990
  179.1 7.5 %collective-permute-start.22 = (bf16[4,16,2304]{2,1,0:T(8,128)(2,1)S(1)}, bf16[4,16,2304]{2,1,0:T(8,128)(2,1)S(1)}, u32[]{:S(2)}, u32[]{:S(2)}) collective-permute-start(bf16[4,16,2304]{2,1,0:T(8,128)(2,1)S(1)} %get-tuple-element.91.refs_0_), channel_id=1, source_target_pairs={{0,4},{1,5},{2,6},{3,7},{4,0},{5,1},{6,2},{7,3},{8,12},{9,13},{10,... | collective-permute-start | bytes 884744 | tf_op jit(solution)/shard_map/ppermute | solution.py:990
  180.3 7.2 %collective-permute-start.21 = (bf16[4,16,2304]{2,1,0:T(8,128)(2,1)S(1)}, bf16[4,16,2304]{2,1,0:T(8,128)(2,1)S(1)}, u32[]{:S(2)}, u32[]{:S(2)}) collective-permute-start(bf16[4,16,2304]{2,1,0:T(8,128)(2,1)S(1)} %get-tuple-element.90.refs_0_), channel_id=1, source_target_pairs={{0,2},{1,3},{2,0},{3,1},{4,6},{5,7},{6,4},{7,5},{8,10},{9,11},{10,... | collective-permute-start | bytes 884744 | tf_op jit(solution)/shard_map/ppermute | solution.py:990
  181.8 6.9 %collective-permute-start.23 = (bf16[1,16,1792]{2,1,0:T(8,128)(2,1)S(1)}, bf16[1,16,1792]{2,1,0:T(8,128)(2,1)S(1)}, u32[]{:S(2)}, u32[]{:S(2)}) collective-permute-start(bf16[1,16,1792]{2,1,0:T(8,128)(2,1)S(1)} %get-tuple-element.136), channel_id=1, source_target_pairs={{0,8},{1,9},{2,10},{3,11},{4,12},{5,13},{6,14},{7,15},{8,0},{9,1},... | collective-permute-start | bytes 172040 | tf_op jit(solution)/shard_map/ppermute | solution.py:990
  186.6 13.5 %collective-permute-start.30 = (bf16[8,16,2304]{2,1,0:T(8,128)(2,1)S(1)}, bf16[8,16,2304]{2,1,0:T(8,128)(2,1)S(1)}, u32[]{:S(2)}, u32[]{:S(2)}) collective-permute-start(bf16[8,16,2304]{2,1,0:T(8,128)(2,1)S(1)} %shard_map.246.refs_2_), channel_id=1, source_target_pairs={{0,2},{1,3},{2,0},{3,1},{4,6},{5,7},{6,4},{7,5},{8,10},{9,11},{10,... | collective-permute-start | bytes 1769480 | tf_op jit(solution)/shard_map/ppermute | solution.py:990
  187.5 12.6 %collective-permute-start.29 = (bf16[8,16,2304]{2,1,0:T(8,128)(2,1)S(1)}, bf16[8,16,2304]{2,1,0:T(8,128)(2,1)S(1)}, u32[]{:S(2)}, u32[]{:S(2)}) collective-permute-start(bf16[8,16,2304]{2,1,0:T(8,128)(2,1)S(1)} %shard_map.245.refs_0_), channel_id=1, source_target_pairs={{0,4},{1,5},{2,6},{3,7},{4,0},{5,1},{6,2},{7,3},{8,12},{9,13},{10,... | collective-permute-start | bytes 1769480 | tf_op jit(solution)/shard_map/ppermute | solution.py:990
  200.3 8.7 %collective-permute-start.31 = (bf16[16,16,4608]{2,1,0:T(8,128)(2,1)S(1)}, bf16[16,16,4608]{2,1,0:T(8,128)(2,1)}, u32[]{:S(2)}, u32[]{:S(2)}) collective-permute-start(bf16[16,16,4608]{2,1,0:T(8,128)(2,1)S(1)} %shard_map.248.own_ref), channel_id=1, source_target_pairs={{0,1},{1,0},{2,3},{3,2},{4,5},{5,4},{6,7},{7,6},{8,9},{9,8},{10,11... | collective-permute-start | bytes 7077896 | tf_op jit(solution)/shard_map/ppermute | solution.py:990
  200.4 31.5 %all-to-all-start.2 = ((bf16[8,128,512]{2,1,0:T(8,128)(2,1)}), bf16[8,128,512]{2,1,0:T(8,128)(2,1)S(1)}, u32[]{:S(2)}, u32[]{:S(2)}) async-start(bf16[8,128,512]{2,1,0:T(8,128)(2,1)} %bitcast.57), calls=%async_computation.2 | async-start | bytes 2097152 | tf_op jit(solution)/shard_map/all_to_all | solution.py:872
  205.5 24.1 %collective-permute-start.32 = (bf16[4,16,1792]{2,1,0:T(8,128)(2,1)}, bf16[4,16,1792]{2,1,0:T(8,128)(2,1)S(1)}, u32[]{:S(2)}, u32[]{:S(2)}) collective-permute-start(bf16[4,16,1792]{2,1,0:T(8,128)(2,1)} %copy-done), channel_id=1, source_target_pairs={{0,4},{1,5},{2,6},{3,7},{4,0},{5,1},{6,2},{7,3},{8,12},{9,13},{10,... | collective-permute-start | bytes 688136 | tf_op jit(solution)/shard_map/ppermute | solution.py:990
  207.5 22.0 %collective-permute-start.33 = (bf16[4,16,1792]{2,1,0:T(8,128)(2,1)}, bf16[4,16,1792]{2,1,0:T(8,128)(2,1)S(1)}, u32[]{:S(2)}, u32[]{:S(2)}) collective-permute-start(bf16[4,16,1792]{2,1,0:T(8,128)(2,1)} %copy-done), channel_id=1, source_target_pairs={{0,2},{1,3},{2,0},{3,1},{4,6},{5,7},{6,4},{7,5},{8,10},{9,11},{10,... | collective-permute-start | bytes 688136 | tf_op jit(solution)/shard_map/ppermute | solution.py:990
  208.2 21.4 %collective-permute-start.34 = (bf16[4,16,1792]{2,1,0:T(8,128)(2,1)}, bf16[4,16,1792]{2,1,0:T(8,128)(2,1)S(1)}, u32[]{:S(2)}, u32[]{:S(2)}) collective-permute-start(bf16[4,16,1792]{2,1,0:T(8,128)(2,1)} %copy-done), channel_id=1, source_target_pairs={{0,6},{1,7},{2,4},{3,5},{4,2},{5,3},{6,0},{7,1},{8,14},{9,15},{10,... | collective-permute-start | bytes 688136 | tf_op jit(solution)/shard_map/ppermute | solution.py:990
  (19 other events, 194.3 us)
